TPU v7x, 256 devices: a whole 4x4x8 slice. The times are simulated.
256 devices in a mesh: row: 32 (over y, z), col: 8 (over x, core).
Axes of the slice: x: 4, y: 4, z: 8, core: 2. Of those that a mesh axis runs over, the one named last changes fastest.
Arguments:
- membership: float32 [32768, 512], P(('row', 'col')), may hold values from 0.02 to 0.12
- tile_count: int32 [256], P(('row', 'col')), may hold values from 16 to 128, as said below
- tile_rows: int32 [256, 128], P(('row', 'col')), may hold values from 0 to 7
- tile_cols: int32 [256, 128], P(('row', 'col')), may hold values from 0 to 31
- edge_masks: int32 [256, 128, 128, 128], P(('row', 'col')), may hold values 0 or 1
- neg_rows: int32 [256, 32], P(('row', 'col')), may hold values from 0 to 7
- neg_cols: int32 [256, 32], P(('row', 'col')), may hold values from 0 to 31
- neg_weight: float32 [256, 32], P(('row', 'col')), may hold values from 0.003 to 0.03
Outputs:
- membership_grad: float32 [32768, 512], P(('row', 'col'))
Inputs may be any that keep to these rules, and one draw needn't show every extreme that they name: `tile_count`: some device in every draw has all 128 slots live; the others far fewer.
All inputs are finite; a program needn't handle non-finite values. No bound on the sum of `edge_masks` on one device may be relied on, other than what follows from the above.
Results may differ from a plain program's by a relative error of at most 0.0015.
Values may be sent and summed in bfloat16 or wider, within the bound.
No kernel may reach another device: no remote copies, remote signals or barrier semaphores. Data moves between devices by JAX's collectives and lax.ppermute only.
A program may use at most 128 MiB of HBM per device.

v0:
```python
import functools

import jax
import jax.numpy as jnp
from jax import lax
from jax.experimental import pallas as pl
from jax.experimental.pallas import tpu as pltpu
from jax.sharding import PartitionSpec as P

NY, NZ, NX, NC = 4, 8, 4, 2
T = 128
C = 512
BF = jnp.bfloat16
F32 = jnp.float32
VMEM = pl.BlockSpec(memory_space=pltpu.VMEM)
SMEM = pl.BlockSpec(memory_space=pltpu.SMEM)
PARAMS = pltpu.CompilerParams(vmem_limit_bytes=28 * 1024 * 1024)
SLOTS = 16
BUFFERS = 4
PIECES = ((0, 256), (256, 512))


def from_y(x, k):
    perm = [(((y + k) % NY) * NZ + z, y * NZ + z) for y in range(NY) for z in range(NZ)]
    return lax.ppermute(x, "row", perm)


def from_z(x, k):
    perm = [(y * NZ + (z + k) % NZ, y * NZ + z) for y in range(NY) for z in range(NZ)]
    return lax.ppermute(x, "row", perm)


def from_x(x, k):
    perm = [(((s + k) % NX) * NC + c, s * NC + c) for s in range(NX) for c in range(NC)]
    return lax.ppermute(x, "col", perm)


def from_core(x):
    perm = [(s * NC + 1 - c, s * NC + c) for s in range(NX) for c in range(NC)]
    return lax.ppermute(x, "col", perm)


def prep_kernel(ints, nw, masks, m_ref, w_ref, buf, sem):
    n_slots, n_neg = masks.shape[1], nw.shape[1]
    at_neg, at_pos = 2 * n_slots, 2 * (n_slots + n_neg)
    count = ints[at_pos + 4]
    y, z, x, c = ints[at_pos], ints[at_pos + 1], ints[at_pos + 2], ints[at_pos + 3]
    n_blocks = masks.shape[1] // SLOTS

    def fetch(b):
        at = b % BUFFERS
        return pltpu.make_async_copy(masks.at[0, pl.ds(b * SLOTS, SLOTS)], buf.at[at], sem.at[at])

    for b in range(BUFFERS):
        fetch(b).start()

    def row_at(a):
        return ((a % NC) ^ c) * NX + ((a // NC - x) & (NX - 1))

    def col_at(b):
        return (b % NZ - z) & (NZ - 1), (b // NZ - y) & (NY - 1)

    m_ref[...] = jnp.zeros_like(m_ref)

    for a in range(NX * NC):
        for b in range(NY * NZ):
            w_ref[a, b] = 0.0

    def negative(p, _):
        d, e = col_at(ints[at_neg + n_neg + p])
        a = row_at(ints[at_neg + p])
        w_ref[a, d * NY + e] += nw[0, p]
        return 0

    lax.fori_loop(0, n_neg, negative, 0)

    def block(b, _):
        fetch(b).wait()

        def slot(t, _):
            a = row_at(ints[b * SLOTS + t])
            d, e = col_at(ints[n_slots + b * SLOTS + t])
            at = (d, pl.ds(pl.multiple_of(a * T, T), T), pl.ds(pl.multiple_of(e * T, T), T))
            m_ref[at] += buf[b % BUFFERS, t].astype(F32).astype(BF)
            return 0

        lax.fori_loop(0, jnp.clip(count - b * SLOTS, 0, SLOTS), slot, 0)

        @pl.when(b + BUFFERS < n_blocks)
        def _():
            fetch(b + BUFFERS).start()

        return 0

    lax.fori_loop(0, n_blocks, block, 0)


def prep(ints, nw, masks):
    return pl.pallas_call(
        prep_kernel,
        out_shape=(
            jax.ShapeDtypeStruct((NZ, NX * NC * T, NY * T), BF),
            jax.ShapeDtypeStruct((NX * NC, NY * NZ), F32),
        ),
        in_specs=[SMEM, SMEM, pl.BlockSpec(memory_space=pltpu.HBM)],
        out_specs=(VMEM, SMEM),
        scratch_shapes=[pltpu.VMEM((BUFFERS, SLOTS, T, T), jnp.int32), pltpu.SemaphoreType.DMA((BUFFERS,))],
        compiler_params=pltpu.CompilerParams(vmem_limit_bytes=45 * 1024 * 1024),
        cost_estimate=pl.CostEstimate(flops=0, bytes_accessed=16 << 20, transcendentals=0),
        name="prep",
    )(ints, nw, masks)


def dot(a, b, dims):
    return lax.dot_general(a, b, (dims, ((), ())), preferred_element_type=F32)


def row_sums_kernel(r_ref, out):
    def body(h, _):
        for f in range(NX):
            out[h, f : f + 1] = jnp.sum(r_ref[h, f * T : (f + 1) * T].astype(F32), axis=0, keepdims=True)
        return 0

    lax.fori_loop(0, 2, body, 0)


def row_sums(r):
    return pl.pallas_call(
        row_sums_kernel,
        out_shape=jax.ShapeDtypeStruct((2, 8, C), F32),
        in_specs=[VMEM],
        out_specs=VMEM,
        compiler_params=PARAMS,
        name="row_sums",
    )(r)


def chunk_kernel(ds, first, split, w_ref, r_ref, row_sums, *refs):
    n = len(ds)
    k_refs, refs = refs[:n], refs[n:]
    m_ref, refs = refs[0], refs[1:]
    if not first:
        acc_in, refs = refs[0], refs[1:]
    p = len(PIECES)
    rows_out, refs, (g_acc, k_all, col_sums) = refs[0], refs[1:-3], refs[-3:]
    for c in range(n):
        for e in range(NY):
            g_acc[c, e * T : (e + 1) * T] = jnp.zeros((T, C), F32)
            k_all[c, e * T : (e + 1) * T] = k_refs[c][e]
            col_sums[c, e : e + 1] = jnp.sum(k_refs[c][e].astype(F32), axis=0, keepdims=True)

    def body(step, _):
        c, h = step // 2, step % 2
        d = ds[0] if n == 1 else jnp.where(c == 0, ds[0], ds[1])
        x, k = r_ref[h], k_all[c]
        s = dot(x, k, ((1,), (1,)))
        at = pl.ds(pl.multiple_of(h * NX * T, NX * T), NX * T)
        coef = (1.0 / (1.0 - jnp.exp(s))).astype(BF) * m_ref[d, at]
        g = dot(coef, x, ((0,), (0,)))
        r = dot(coef, k, ((1,), (0,)))
        sums = [row_sums[h, f : f + 1] for f in range(NX)]
        weights = [[w_ref[h * NX + f, d * NY + e] for e in range(NY)] for f in range(NX)]
        for e in range(NY):
            v = sum(weights[f][e] * sums[f] for f in range(NX))
            g_acc[c, e * T : (e + 1) * T] += g[e * T : (e + 1) * T] + v
        for f in range(NX):
            v = sum(weights[f][e] * col_sums[c, e : e + 1] for e in range(NY))
            rows = r[f * T : (f + 1) * T] + v
            base = 0.0 if first and n == 1 else (rows_out if first else acc_in)[h, f * T : (f + 1) * T]
            rows_out[h, f * T : (f + 1) * T] = rows + base
        return 0

    lax.fori_loop(0, 2 * n, body, 0)
    for c in range(n):
        for e in range(NY):
            done = g_acc[c, e * T : (e + 1) * T].astype(BF)
            if split:
                refs[e // 2][e % 2] = done
                continue
            for q, (lo, hi) in enumerate(PIECES):
                refs[c * p + q][e] = done[:, lo:hi]


def chunk(ds, w, rows, ks, m, acc, split=False):
    n, p = len(ds), len(PIECES)
    first = acc is None
    args = [w, *rows, *ks, m] + ([] if first else [acc])
    shapes = [((2, NX * T, C), F32)]
    if split:
        shapes += [((2, T, C), BF)] * 2
    else:
        shapes += [((NY, T, hi - lo), BF) for _ in ds for lo, hi in PIECES]
    out = pl.pallas_call(
        functools.partial(chunk_kernel, ds, first, split),
        out_shape=[jax.ShapeDtypeStruct(*s) for s in shapes],
        in_specs=[SMEM] + [VMEM] * (len(args) - 1),
        out_specs=[VMEM] * len(shapes),
        scratch_shapes=[pltpu.VMEM((n, NY * T, C), F32), pltpu.VMEM((n, NY * T, C), BF), pltpu.VMEM((n, 8, C), F32)],
        input_output_aliases={} if first else {len(args) - 1: 0},
        compiler_params=PARAMS,
        cost_estimate=pl.CostEstimate(
            flops=n * 6 * 1024 * 512 * 512, bytes_accessed=(n * 2 + 6) << 20, transcendentals=n * 1024 * 512
        ),
        name="chunk",
    )(*args)
    if split:
        return out
    return out[0], *[out[1 + c * p : 1 + (c + 1) * p] for c in range(n)]


def first_hop_kernel(up_in, down_in, *refs):
    p = len(PIECES)
    ups, downs, up_outs, down_outs = refs[:p], refs[p : 2 * p], refs[2 * p : 3 * p], refs[3 * p :]
    for q, (lo, hi) in enumerate(PIECES):
        up_outs[q][:2] = (ups[q][:2].astype(F32) + up_in[:, :, lo:hi].astype(F32)).astype(BF)
        up_outs[q][2:] = ups[q][2:]
        down_outs[q][:2] = downs[q][:2]
        down_outs[q][2:] = (downs[q][2:].astype(F32) + down_in[:, :, lo:hi].astype(F32)).astype(BF)


def first_hop(up_in, down_in, ups, downs):
    own = [*ups, *downs]
    out = pl.pallas_call(
        first_hop_kernel,
        out_shape=[jax.ShapeDtypeStruct(x.shape, BF) for x in own],
        in_specs=[VMEM] * (2 + len(own)),
        out_specs=[VMEM] * len(own),
        compiler_params=PARAMS,
        cost_estimate=pl.CostEstimate(flops=1 << 20, bytes_accessed=3 << 20, transcendentals=0),
        name="first_hop",
    )(up_in, down_in, *own)
    return list(out[: len(ups)]), list(out[len(ups) :])


def hop_kernel(up, down, up_in, down_in, up_out, down_out):
    up_out[...] = (up[...].astype(F32) + up_in[...].astype(F32)).astype(BF)
    down_out[...] = (down[...].astype(F32) + down_in[...].astype(F32)).astype(BF)


def hop(kernel, up, down, up_in, down_in):
    return pl.pallas_call(
        kernel,
        out_shape=[jax.ShapeDtypeStruct(up.shape, BF)] * 2,
        in_specs=[VMEM] * 4,
        out_specs=[VMEM] * 2,
        compiler_params=PARAMS,
        cost_estimate=pl.CostEstimate(flops=1 << 20, bytes_accessed=3 << 20, transcendentals=0),
        name="hop",
    )(up, down, up_in, down_in)


def last_hop_kernel(*refs):
    p = len(PIECES)
    keep, *sends = refs[3 * p :]
    for q, (lo, hi) in enumerate(PIECES):
        for e in range(NY):
            s = sum(refs[k * p + q][e].astype(F32) for k in range(3))
            if e:
                sends[e - 1][:, lo:hi] = s.astype(BF)
            else:
                keep[:, lo:hi] = s


def last_hop(own, up_in, down_in):
    args = [*own, *up_in, *down_in]
    return pl.pallas_call(
        last_hop_kernel,
        out_shape=[jax.ShapeDtypeStruct((T, C), F32)] + [jax.ShapeDtypeStruct((T, C), BF)] * (NY - 1),
        in_specs=[VMEM] * len(args),
        out_specs=[VMEM] * NY,
        compiler_params=PARAMS,
        cost_estimate=pl.CostEstimate(flops=1 << 20, bytes_accessed=2 << 20, transcendentals=0),
        name="last_hop",
    )(*args)


def row_hop_kernel(keep, arrived, own, *sends):
    for f in range(NX):
        s = keep[0, f * T : (f + 1) * T] + arrived[f * T : (f + 1) * T]
        if f:
            sends[f - 1][...] = s.astype(BF)
        else:
            own[...] = s


def row_hop(keep, arrived):
    return pl.pallas_call(
        row_hop_kernel,
        out_shape=[jax.ShapeDtypeStruct((T, C), F32)] + [jax.ShapeDtypeStruct((T, C), BF)] * (NX - 1),
        in_specs=[VMEM] * 2,
        out_specs=[VMEM] * NX,
        compiler_params=PARAMS,
        cost_estimate=pl.CostEstimate(flops=1 << 19, bytes_accessed=3 << 20, transcendentals=0),
        name="row_hop",
    )(keep, arrived)


def final_kernel(*refs):
    out = refs[-1]
    total = refs[0][...]
    for part in refs[1:-1]:
        total = total + part[...].astype(F32)
    out[...] = total


def final(*terms):
    return pl.pallas_call(
        final_kernel,
        out_shape=jax.ShapeDtypeStruct((T, C), F32),
        in_specs=[VMEM] * len(terms),
        out_specs=VMEM,
        compiler_params=PARAMS,
        name="final",
    )(*terms)


def tie(x, *tokens):
    return lax.optimization_barrier((x, *tokens))[0]


def local(membership, tile_count, tile_rows, tile_cols, edge_masks, neg_rows, neg_cols, neg_weight):
    i, j = lax.axis_index("row"), lax.axis_index("col")
    pos = jnp.stack([i // NZ, i % NZ, j // NC, j % NC]).astype(jnp.int32)
    ints = jnp.concatenate([tile_rows[0], tile_cols[0], neg_rows[0], neg_cols[0], pos, tile_count])
    shard = membership.astype(BF)
    next_y, last_y = from_y(shard, 1), from_y(shard, -1)
    half = T // 2
    far_y = jnp.concatenate([from_y(next_y[:half], 1), from_y(last_y[half:], -1)])
    stack = [shard, next_y, far_y, last_y]
    first = jnp.stack(stack)
    same = jnp.stack([shard] + [from_x(shard, k) for k in (1, 2, 3)])
    m, w = prep(tie(ints, first), neg_weight, edge_masks)
    p = range(len(PIECES))

    above, below = [first], [first]

    def step(*token):
        up, down = tie((above[-1], below[-1]), *token)
        above.append(from_z(up, 1))
        below.append(from_z(down, -1))

    step()
    r = jnp.stack([same, from_core(tie(same, m))]).reshape(2, NX * T, C)
    rows = r, row_sums(r)
    step(m)
    acc, g0 = chunk((0,), tie(w, above[1]), rows, [first], m, None)
    acc, g1, g7 = chunk((1, 7), w, rows, [above[1], below[1]], m, acc)
    step(acc)
    acc, g2, g6 = chunk((2, 6), w, rows, [above[2], below[2]], m, acc)
    up, down = tie((above[3], below[3]), acc)
    far_up, far_down = from_z(up[:2], 1), from_z(down[2:], -1)
    acc, g3, g5 = chunk((3, 5), w, rows, [above[3], below[3]], m, acc)
    far = jnp.concatenate([tie(far_up, acc), far_down])
    acc, *g4 = chunk((4,), w, rows, [far], m, acc, split=True)

    def arrive(up, down):
        return [from_z(up[q], -1) for q in p], [from_z(down[q], 1) for q in p]

    def hops(kernel, up_in, down_in, up_own, down_own):
        pairs = [hop(kernel, up_own[q], down_own[q], up_in[q], down_in[q]) for q in p]
        return [x[0] for x in pairs], [x[1] for x in pairs]

    up_in, down_in = from_z(g4[0], -1), from_z(g4[1], 1)
    row_own, *row_sends = row_hop(acc, from_core(acc[1]))
    up, down = first_hop(*tie((up_in, down_in), row_own), g3, g5)
    up_in, down_in = arrive(up, down)
    row_parts = [row_own] + [from_x(row_sends[k - 1], -k) for k in (1, 2, 3)]
    up_in[1], down_in[1] = tie((up_in[1], down_in[1]), *row_parts)
    up, down = hops(hop_kernel, up_in, down_in, g2, g6)
    up, down = hops(hop_kernel, *arrive(up, down), g1, g7)
    up_in, down_in = arrive(up, down)
    own, *sends = last_hop(g0, up_in, down_in)
    return final(*row_parts, own, *[from_y(sends[k - 1], -k) for k in (1, 2, 3)])


def solution(mesh):
    placed = (
        P(("row", "col"), None),
        P(("row", "col")),
        P(("row", "col"), None),
        P(("row", "col"), None),
        P(("row", "col"), None, None, None),
        P(("row", "col"), None),
        P(("row", "col"), None),
        P(("row", "col"), None),
    )
    return jax.shard_map(
        local, mesh=mesh, in_specs=placed, out_specs=P(("row", "col"), None), check_vma=False
    )
```

profile of v0, /device:TPU:24, one launch (start us, length us, event | category | flops | bytes accessed | tf_op | source)
XLA Modules:
  0.0 130.6 jit_solution(9677290294541829662)
XLA Ops:
  0.0 1.0 convert_element_type.3
  1.0 0.8 collective-permute-start
  1.8 2.5 %collective-permute-start.2 = (bf16[128,512]{1,0:T(8,128)(2,1)S(1)}, bf16[128,512]{1,0:T(8,128)(2,1)S(1)}, u32[]{:S(2)}, u32[]{:S(2)}) collective-permute-start(bf16[128,512]{1,0:T(8,128)(2,1)S(1)} %convert_element_type.3), channel_id=1, source_target_pairs={{192,0},{200,8},{208,16},{216,24},{224,32},{232,40},{240,48},{248,... | collective-permute-start | bytes 393224 | tf_op jit(solution)/shard_map/ppermute | solution.py:25
  4.3 2.8 %collective-permute-start.4 = (bf16[128,512]{1,0:T(8,128)(2,1)S(1)}, bf16[128,512]{1,0:T(8,128)(2,1)S(1)}, u32[]{:S(2)}, u32[]{:S(2)}) collective-permute-start(bf16[128,512]{1,0:T(8,128)(2,1)S(1)} %convert_element_type.3), channel_id=1, source_target_pairs={{2,0},{3,1},{4,2},{5,3},{6,4},{7,5},{0,6},{1,7},{10,8},{11,9},{12,... | collective-permute-start | bytes 393224 | tf_op jit(solution)/shard_map/ppermute | solution.py:35
  7.1 0.8 collective-permute-start.5
  7.9 0.9 collective-permute-start.6
  8.9 3.3 %collective-permute-start.3 = (bf16[64,512]{1,0:T(8,128)(2,1)S(1)}, bf16[64,512]{1,0:T(8,128)(2,1)S(1)}, u32[]{:S(2)}, u32[]{:S(2)}) collective-permute-start(bf16[64,512]{1,0:T(8,128)(2,1)S(1)} %slice.21), channel_id=1, source_target_pairs={{192,0},{200,8},{208,16},{216,24},{224,32},{232,40},{240,48},{248,... | collective-permute-start | bytes 196616 | tf_op jit(solution)/shard_map/ppermute | solution.py:25
  12.2 1.0 convert_bitcast_fusion
  13.8 0.8 concatenate.10.ints
  14.6 1.1 collective-permute-done.6
  15.8 0.1 fusion.3
  15.9 5.9 %collective-permute-start.8 = (bf16[4,128,512]{2,1,0:T(8,128)(2,1)S(1)}, bf16[4,128,512]{2,1,0:T(8,128)(2,1)S(1)}, u32[]{:S(2)}, u32[]{:S(2)}) collective-permute-start(bf16[4,128,512]{2,1,0:T(8,128)(2,1)S(1)} %get-tuple-element.69.refs_0_), channel_id=1, source_target_pairs={{8,0},{16,8},{24,16},{32,24},{40,32},{48,40},{56,48},{0,56},{72,64... | collective-permute-start | bytes 1572872 | tf_op jit(solution)/shard_map/ppermute | solution.py:30
  21.8 5.3 %prep.1 = (bf16[8,1024,512]{2,1,0:T(8,128)(2,1)S(1)}, f32[8,32]{1,0:T(8,128)S(1)}) custom-call(s32[325]{0:T(512)S(1)} %concatenate.10.ints, f32[1,32]{1,0:T(1,128)S(1)} %copy-done, s32[1,128,128,128]{3,2,1,0:T(8,128)} %masks.1), custom_call_target="tpu_custom_call" | custom-call | bytes 16777216 | tf_op jit(solution)/shard_map/prep/pallas_call | solution.py:99
  27.1 0.1 collective-permute-start.7
  27.2 5.1 %collective-permute-done.8.refs_0_ = bf16[4,128,512]{2,1,0:T(8,128)(2,1)S(1)} collective-permute-done((bf16[4,128,512]{2,1,0:T(8,128)(2,1)S(1)}, bf16[4,128,512]{2,1,0:T(8,128)(2,1)S(1)}, u32[]{:S(2)}, u32[]{:S(2)}) %collective-permute-start.8) | collective-permute-done | bytes 524320 | tf_op jit(solution)/shard_map/ppermute | solution.py:30
  32.4 3.4 %collective-permute-done.9.refs_1_ = bf16[4,128,512]{2,1,0:T(8,128)(2,1)S(1)} collective-permute-done((bf16[4,128,512]{2,1,0:T(8,128)(2,1)S(1)}, bf16[4,128,512]{2,1,0:T(8,128)(2,1)S(1)}, u32[]{:S(2)}, u32[]{:S(2)}) %collective-permute-start.9) | collective-permute-done | bytes 524320 | tf_op jit(solution)/shard_map/ppermute | solution.py:30
  35.8 0.3 collective-permute-start.10
  36.1 1.7 %collective-permute-start.11 = (bf16[4,128,512]{2,1,0:T(8,128)(2,1)S(1)}, bf16[4,128,512]{2,1,0:T(8,128)(2,1)S(1)}, u32[]{:S(2)}, u32[]{:S(2)}) collective-permute-start(bf16[4,128,512]{2,1,0:T(8,128)(2,1)S(1)} %collective-permute-done.9.refs_1_), channel_id=1, source_target_pairs={{56,0},{0,8},{8,16},{16,24},{24,32},{32,40},{40,48},{48,56},{120,6... | collective-permute-start | bytes 1572872 | tf_op jit(solution)/shard_map/ppermute | solution.py:30
  37.8 0.1 pad_maximum_fusion.r_ref
  37.9 0.2 row_sums.1
  38.1 3.3 %chunk.5 = (f32[2,512,512]{2,1,0:T(8,128)S(1)}, bf16[4,128,256]{2,1,0:T(8,128)(2,1)S(1)}, bf16[4,128,256]{2,1,0:T(8,128)(2,1)S(1)}) custom-call(f32[8,32]{1,0:T(8,128)S(1)} %get-tuple-element.72.w_ref, bf16[2,512,512]{2,1,0:T(8,128)(2,1)S(1)} %pad_maximum_fusion.r_ref, f32[2,8,512]{2,1,0:T(8,128)S(1)} %row_sums.1, ...), custom_call_target="tpu_custom_call" | custom-call | flops 1610612736 | bytes 8388608 | tf_op jit(solution)/shard_map/chunk/pallas_call | solution.py:193
  41.4 6.1 %chunk.6 = (f32[2,512,512]{2,1,0:T(8,128)S(1)}, bf16[4,128,256]{2,1,0:T(8,128)(2,1)S(1)}, bf16[4,128,256]{2,1,0:T(8,128)(2,1)S(1)}, bf16[4,128,256]{2,1,0:T(8,128)(2,1)S(1)}, bf16[4,128,256]{2,1,0:T(8,128)(2,1)S(1)}) custom-call(f32[8,32]{1,0:T(8,128)S(1)} %get-tuple-element.72.w_ref, ...), custom_call_target="tpu_custom_call", output_to_operand_aliasing={{0}: (6, {})} | custom-call | flops 3221225472 | bytes 10485760 | tf_op jit(solution)/shard_map/chunk/pallas_call | solution.py:193
  47.5 0.1 collective-permute-done.10.refs_0_
  47.6 1.5 %collective-permute-done.11.refs_1_ = bf16[4,128,512]{2,1,0:T(8,128)(2,1)S(1)} collective-permute-done((bf16[4,128,512]{2,1,0:T(8,128)(2,1)S(1)}, bf16[4,128,512]{2,1,0:T(8,128)(2,1)S(1)}, u32[]{:S(2)}, u32[]{:S(2)}) %collective-permute-start.11) | collective-permute-done | bytes 524320 | tf_op jit(solution)/shard_map/ppermute | solution.py:30
  49.1 0.3 collective-permute-start.12
  49.4 1.7 %collective-permute-start.13 = (bf16[4,128,512]{2,1,0:T(8,128)(2,1)S(1)}, bf16[4,128,512]{2,1,0:T(8,128)(2,1)S(1)}, u32[]{:S(2)}, u32[]{:S(2)}) collective-permute-start(bf16[4,128,512]{2,1,0:T(8,128)(2,1)S(1)} %collective-permute-done.11.refs_1_), channel_id=1, source_target_pairs={{56,0},{0,8},{8,16},{16,24},{24,32},{32,40},{40,48},{48,56},{120,6... | collective-permute-start | bytes 1572872 | tf_op jit(solution)/shard_map/ppermute | solution.py:30
  51.1 6.1 %chunk.7 = (f32[2,512,512]{2,1,0:T(8,128)S(1)}, bf16[4,128,256]{2,1,0:T(8,128)(2,1)S(1)}, bf16[4,128,256]{2,1,0:T(8,128)(2,1)S(1)}, bf16[4,128,256]{2,1,0:T(8,128)(2,1)S(1)}, bf16[4,128,256]{2,1,0:T(8,128)(2,1)S(1)}) custom-call(f32[8,32]{1,0:T(8,128)S(1)} %get-tuple-element.72.w_ref, ...), custom_call_target="tpu_custom_call", output_to_operand_aliasing={{0}: (6, {})} | custom-call | flops 3221225472 | bytes 10485760 | tf_op jit(solution)/shard_map/chunk/pallas_call | solution.py:193
  57.2 2.8 %collective-permute-done.12.refs_0_ = bf16[4,128,512]{2,1,0:T(8,128)(2,1)S(1)} collective-permute-done((bf16[4,128,512]{2,1,0:T(8,128)(2,1)S(1)}, bf16[4,128,512]{2,1,0:T(8,128)(2,1)S(1)}, u32[]{:S(2)}, u32[]{:S(2)}) %collective-permute-start.12) | collective-permute-done | bytes 524320 | tf_op jit(solution)/shard_map/ppermute | solution.py:30
  60.0 1.6 %collective-permute-done.13.refs_1_ = bf16[4,128,512]{2,1,0:T(8,128)(2,1)S(1)} collective-permute-done((bf16[4,128,512]{2,1,0:T(8,128)(2,1)S(1)}, bf16[4,128,512]{2,1,0:T(8,128)(2,1)S(1)}, u32[]{:S(2)}, u32[]{:S(2)}) %collective-permute-start.13) | collective-permute-done | bytes 524320 | tf_op jit(solution)/shard_map/ppermute | solution.py:30
  61.6 0.4 collective-permute-start.14
  61.9 1.8 %collective-permute-start.15 = (bf16[2,128,512]{2,1,0:T(8,128)(2,1)S(1)}, bf16[2,128,512]{2,1,0:T(8,128)(2,1)S(1)}, u32[]{:S(2)}, u32[]{:S(2)}) collective-permute-start(bf16[2,128,512]{2,1,0:T(8,128)(2,1)S(1)} %slice.18), channel_id=1, source_target_pairs={{56,0},{0,8},{8,16},{16,24},{24,32},{32,40},{40,48},{48,56},{120,6... | collective-permute-start | bytes 786440 | tf_op jit(solution)/shard_map/ppermute | solution.py:30
  63.8 6.1 %chunk.8 = (f32[2,512,512]{2,1,0:T(8,128)S(1)}, bf16[4,128,256]{2,1,0:T(8,128)(2,1)S(1)}, bf16[4,128,256]{2,1,0:T(8,128)(2,1)S(1)}, bf16[4,128,256]{2,1,0:T(8,128)(2,1)S(1)}, bf16[4,128,256]{2,1,0:T(8,128)(2,1)S(1)}) custom-call(f32[8,32]{1,0:T(8,128)S(1)} %get-tuple-element.72.w_ref, ...), custom_call_target="tpu_custom_call", output_to_operand_aliasing={{0}: (6, {})} | custom-call | flops 3221225472 | bytes 10485760 | tf_op jit(solution)/shard_map/chunk/pallas_call | solution.py:193
  69.9 3.4 %chunk.9 = (f32[2,512,512]{2,1,0:T(8,128)S(1)}, bf16[2,128,512]{2,1,0:T(8,128)(2,1)S(1)}, bf16[2,128,512]{2,1,0:T(8,128)(2,1)S(1)}) custom-call(f32[8,32]{1,0:T(8,128)S(1)} %get-tuple-element.72.w_ref, bf16[2,512,512]{2,1,0:T(8,128)(2,1)S(1)} %pad_maximum_fusion.r_ref, f32[2,8,512]{2,1,0:T(8,128)S(1)} %row_sums.1, ...), custom_call_target="tpu_custom_call", output_to_operand_aliasing={{0}: (5, {})} | custom-call | flops 1610612736 | bytes 8388608 | tf_op jit(solution)/shard_map/chunk/pallas_call | solution.py:193
  73.5 0.3 collective-permute-start.20
  73.8 3.0 %collective-permute-start.21 = (bf16[2,128,512]{2,1,0:T(8,128)(2,1)S(1)}, bf16[2,128,512]{2,1,0:T(8,128)(2,1)S(1)}, u32[]{:S(2)}, u32[]{:S(2)}) collective-permute-start(bf16[2,128,512]{2,1,0:T(8,128)(2,1)S(1)} %get-tuple-element.94), channel_id=1, source_target_pairs={{8,0},{16,8},{24,16},{32,24},{40,32},{48,40},{56,48},{0,56},{72,64... | collective-permute-start | bytes 786440 | tf_op jit(solution)/shard_map/ppermute | solution.py:30
  76.8 0.1 row_hop.1
  77.0 6.4 %collective-permute-done.20.up_in = bf16[2,128,512]{2,1,0:T(8,128)(2,1)S(1)} collective-permute-done((bf16[2,128,512]{2,1,0:T(8,128)(2,1)S(1)}, bf16[2,128,512]{2,1,0:T(8,128)(2,1)S(1)}, u32[]{:S(2)}, u32[]{:S(2)}) %collective-permute-start.20) | collective-permute-done | bytes 262176 | tf_op jit(solution)/shard_map/ppermute | solution.py:30
  83.4 0.1 collective-permute-start.18
  83.5 0.1 first_hop.1
  83.7 3.2 %collective-permute-start.28 = (bf16[4,128,256]{2,1,0:T(8,128)(2,1)S(1)}, bf16[4,128,256]{2,1,0:T(8,128)(2,1)S(1)}, u32[]{:S(2)}, u32[]{:S(2)}) collective-permute-start(bf16[4,128,256]{2,1,0:T(8,128)(2,1)S(1)} %get-tuple-element.111), channel_id=1, source_target_pairs={{8,0},{16,8},{24,16},{32,24},{40,32},{48,40},{56,48},{0,56},{72,64... | collective-permute-start | bytes 786440 | tf_op jit(solution)/shard_map/ppermute | solution.py:30
  87.0 3.2 %collective-permute-start.23 = (bf16[4,128,256]{2,1,0:T(8,128)(2,1)S(1)}, bf16[4,128,256]{2,1,0:T(8,128)(2,1)S(1)}, u32[]{:S(2)}, u32[]{:S(2)}) collective-permute-start(bf16[4,128,256]{2,1,0:T(8,128)(2,1)S(1)} %get-tuple-element.102), channel_id=1, source_target_pairs={{8,0},{16,8},{24,16},{32,24},{40,32},{48,40},{56,48},{0,56},{72,64... | collective-permute-start | bytes 786440 | tf_op jit(solution)/shard_map/ppermute | solution.py:30
  90.2 1.1 collective-permute-start.19
  91.3 3.9 %collective-permute-done.19.refs_3_ = bf16[128,512]{1,0:T(8,128)(2,1)S(1)} collective-permute-done((bf16[128,512]{1,0:T(8,128)(2,1)S(1)}, bf16[128,512]{1,0:T(8,128)(2,1)S(1)}, u32[]{:S(2)}, u32[]{:S(2)}) %collective-permute-start.19) | collective-permute-done | bytes 131104 | tf_op jit(solution)/shard_map/ppermute | solution.py:35
  95.2 0.1 hop.6
  95.4 3.2 %collective-permute-start.30 = (bf16[4,128,256]{2,1,0:T(8,128)(2,1)S(1)}, bf16[4,128,256]{2,1,0:T(8,128)(2,1)S(1)}, u32[]{:S(2)}, u32[]{:S(2)}) collective-permute-start(bf16[4,128,256]{2,1,0:T(8,128)(2,1)S(1)} %get-tuple-element.115), channel_id=1, source_target_pairs={{8,0},{16,8},{24,16},{32,24},{40,32},{48,40},{56,48},{0,56},{72,64... | collective-permute-start | bytes 786440 | tf_op jit(solution)/shard_map/ppermute | solution.py:30
  98.6 1.2 collective-permute-done.22.up_in
  99.8 0.1 hop.4
  100.0 3.2 %collective-permute-start.25 = (bf16[4,128,256]{2,1,0:T(8,128)(2,1)S(1)}, bf16[4,128,256]{2,1,0:T(8,128)(2,1)S(1)}, u32[]{:S(2)}, u32[]{:S(2)}) collective-permute-start(bf16[4,128,256]{2,1,0:T(8,128)(2,1)S(1)} %get-tuple-element.104), channel_id=1, source_target_pairs={{8,0},{16,8},{24,16},{32,24},{40,32},{48,40},{56,48},{0,56},{72,64... | collective-permute-start | bytes 786440 | tf_op jit(solution)/shard_map/ppermute | solution.py:30
  103.2 2.6 %collective-permute-done.29.up_in = bf16[4,128,256]{2,1,0:T(8,128)(2,1)S(1)} collective-permute-done((bf16[4,128,256]{2,1,0:T(8,128)(2,1)S(1)}, bf16[4,128,256]{2,1,0:T(8,128)(2,1)S(1)}, u32[]{:S(2)}, u32[]{:S(2)}) %collective-permute-start.29) | collective-permute-done | bytes 262176 | tf_op jit(solution)/shard_map/ppermute | solution.py:30
  105.8 0.1 hop.7
  106.0 3.3 %collective-permute-start.33 = (bf16[4,128,256]{2,1,0:T(8,128)(2,1)S(1)}, bf16[4,128,256]{2,1,0:T(8,128)(2,1)S(1)}, u32[]{:S(2)}, u32[]{:S(2)}) collective-permute-start(bf16[4,128,256]{2,1,0:T(8,128)(2,1)S(1)} %get-tuple-element.118), channel_id=1, source_target_pairs={{8,0},{16,8},{24,16},{32,24},{40,32},{48,40},{56,48},{0,56},{72,64... | collective-permute-start | bytes 786440 | tf_op jit(solution)/shard_map/ppermute | solution.py:30
  109.4 2.1 %collective-permute-done.24.up_in = bf16[4,128,256]{2,1,0:T(8,128)(2,1)S(1)} collective-permute-done((bf16[4,128,256]{2,1,0:T(8,128)(2,1)S(1)}, bf16[4,128,256]{2,1,0:T(8,128)(2,1)S(1)}, u32[]{:S(2)}, u32[]{:S(2)}) %collective-permute-start.24) | collective-permute-done | bytes 262176 | tf_op jit(solution)/shard_map/ppermute | solution.py:30
  111.5 0.1 hop.5
  111.7 3.3 %collective-permute-start.32 = (bf16[4,128,256]{2,1,0:T(8,128)(2,1)S(1)}, bf16[4,128,256]{2,1,0:T(8,128)(2,1)S(1)}, u32[]{:S(2)}, u32[]{:S(2)}) collective-permute-start(bf16[4,128,256]{2,1,0:T(8,128)(2,1)S(1)} %get-tuple-element.117), channel_id=1, source_target_pairs={{8,0},{16,8},{24,16},{32,24},{40,32},{48,40},{56,48},{0,56},{72,64... | collective-permute-start | bytes 786440 | tf_op jit(solution)/shard_map/ppermute | solution.py:30
  115.0 2.1 %collective-permute-done.31.refs_3_ = bf16[4,128,256]{2,1,0:T(8,128)(2,1)S(1)} collective-permute-done((bf16[4,128,256]{2,1,0:T(8,128)(2,1)S(1)}, bf16[4,128,256]{2,1,0:T(8,128)(2,1)S(1)}, u32[]{:S(2)}, u32[]{:S(2)}) %collective-permute-start.31) | collective-permute-done | bytes 262176 | tf_op jit(solution)/shard_map/ppermute | solution.py:30
  117.1 3.7 %collective-permute-done.26.refs_2_ = bf16[4,128,256]{2,1,0:T(8,128)(2,1)S(1)} collective-permute-done((bf16[4,128,256]{2,1,0:T(8,128)(2,1)S(1)}, bf16[4,128,256]{2,1,0:T(8,128)(2,1)S(1)}, u32[]{:S(2)}, u32[]{:S(2)}) %collective-permute-start.26) | collective-permute-done | bytes 262176 | tf_op jit(solution)/shard_map/ppermute | solution.py:30
  120.8 0.2 last_hop.1
  121.0 0.9 collective-permute-start.34
  121.9 0.8 collective-permute-start.35
  122.7 0.4 collective-permute-start.36
  123.1 3.0 %collective-permute-done.34.refs_5_ = bf16[128,512]{1,0:T(8,128)(2,1)S(1)} collective-permute-done((bf16[128,512]{1,0:T(8,128)(2,1)S(1)}, bf16[128,512]{1,0:T(8,128)(2,1)S(1)}, u32[]{:S(2)}, u32[]{:S(2)}) %collective-permute-start.34) | collective-permute-done | bytes 131104 | tf_op jit(solution)/shard_map/ppermute | solution.py:25
  126.1 2.4 %collective-permute-done.35.refs_6_ = bf16[128,512]{1,0:T(8,128)(2,1)S(1)} collective-permute-done((bf16[128,512]{1,0:T(8,128)(2,1)S(1)}, bf16[128,512]{1,0:T(8,128)(2,1)S(1)}, u32[]{:S(2)}, u32[]{:S(2)}) %collective-permute-start.35) | collective-permute-done | bytes 131104 | tf_op jit(solution)/shard_map/ppermute | solution.py:25
  128.5 1.3 collective-permute-done.36.refs_7_
  129.8 0.8 final.1
  (39 shorter events, 0.9 us)
Async XLA Ops:
  0.0 21.8 %copy-start = (f32[1,32]{1,0:T(1,128)S(1)}, f32[1,32]{1,0:T(1,128)}, u32[]{:S(2)}) copy-start(f32[1,32]{1,0:T(1,128)} %nw.1) | copy-start | bytes 388
  1.0 7.8 %collective-permute-start = (bf16[128,512]{1,0:T(8,128)(2,1)S(1)}, bf16[128,512]{1,0:T(8,128)(2,1)S(1)}, u32[]{:S(2)}, u32[]{:S(2)}) collective-permute-start(bf16[128,512]{1,0:T(8,128)(2,1)S(1)} %convert_element_type.3), channel_id=1, source_target_pairs={{64,0},{72,8},{80,16},{88,24},{96,32},{104,40},{112,48},{120,56},{... | collective-permute-start | bytes 393224 | tf_op jit(solution)/shard_map/ppermute | solution.py:25
  1.8 7.0 %collective-permute-start.2 = (bf16[128,512]{1,0:T(8,128)(2,1)S(1)}, bf16[128,512]{1,0:T(8,128)(2,1)S(1)}, u32[]{:S(2)}, u32[]{:S(2)}) collective-permute-start(bf16[128,512]{1,0:T(8,128)(2,1)S(1)} %convert_element_type.3), channel_id=1, source_target_pairs={{192,0},{200,8},{208,16},{216,24},{224,32},{232,40},{240,48},{248,... | collective-permute-start | bytes 393224 | tf_op jit(solution)/shard_map/ppermute | solution.py:25
  4.3 10.3 %collective-permute-start.4 = (bf16[128,512]{1,0:T(8,128)(2,1)S(1)}, bf16[128,512]{1,0:T(8,128)(2,1)S(1)}, u32[]{:S(2)}, u32[]{:S(2)}) collective-permute-start(bf16[128,512]{1,0:T(8,128)(2,1)S(1)} %convert_element_type.3), channel_id=1, source_target_pairs={{2,0},{3,1},{4,2},{5,3},{6,4},{7,5},{0,6},{1,7},{10,8},{11,9},{12,... | collective-permute-start | bytes 393224 | tf_op jit(solution)/shard_map/ppermute | solution.py:35
  7.1 7.6 %collective-permute-start.5 = (bf16[128,512]{1,0:T(8,128)(2,1)S(1)}, bf16[128,512]{1,0:T(8,128)(2,1)S(1)}, u32[]{:S(2)}, u32[]{:S(2)}) collective-permute-start(bf16[128,512]{1,0:T(8,128)(2,1)S(1)} %convert_element_type.3), channel_id=1, source_target_pairs={{4,0},{5,1},{6,2},{7,3},{0,4},{1,5},{2,6},{3,7},{12,8},{13,9},{14,... | collective-permute-start | bytes 393224 | tf_op jit(solution)/shard_map/ppermute | solution.py:35
  7.9 7.9 %collective-permute-start.6 = (bf16[128,512]{1,0:T(8,128)(2,1)S(1)}, bf16[128,512]{1,0:T(8,128)(2,1)S(1)}, u32[]{:S(2)}, u32[]{:S(2)}) collective-permute-start(bf16[128,512]{1,0:T(8,128)(2,1)S(1)} %convert_element_type.3), channel_id=1, source_target_pairs={{6,0},{7,1},{0,2},{1,3},{2,4},{3,5},{4,6},{5,7},{14,8},{15,9},{8,1... | collective-permute-start | bytes 393224 | tf_op jit(solution)/shard_map/ppermute | solution.py:35
  8.8 5.8 %collective-permute-start.1 = (bf16[64,512]{1,0:T(8,128)(2,1)S(1)}, bf16[64,512]{1,0:T(8,128)(2,1)S(1)}, u32[]{:S(2)}, u32[]{:S(2)}) collective-permute-start(bf16[64,512]{1,0:T(8,128)(2,1)S(1)} %slice.20), channel_id=1, source_target_pairs={{64,0},{72,8},{80,16},{88,24},{96,32},{104,40},{112,48},{120,56},{... | collective-permute-start | bytes 196616 | tf_op jit(solution)/shard_map/ppermute | solution.py:25
  8.9 5.7 %collective-permute-start.3 = (bf16[64,512]{1,0:T(8,128)(2,1)S(1)}, bf16[64,512]{1,0:T(8,128)(2,1)S(1)}, u32[]{:S(2)}, u32[]{:S(2)}) collective-permute-start(bf16[64,512]{1,0:T(8,128)(2,1)S(1)} %slice.21), channel_id=1, source_target_pairs={{192,0},{200,8},{208,16},{216,24},{224,32},{232,40},{240,48},{248,... | collective-permute-start | bytes 196616 | tf_op jit(solution)/shard_map/ppermute | solution.py:25
  15.9 16.5 %collective-permute-start.8 = (bf16[4,128,512]{2,1,0:T(8,128)(2,1)S(1)}, bf16[4,128,512]{2,1,0:T(8,128)(2,1)S(1)}, u32[]{:S(2)}, u32[]{:S(2)}) collective-permute-start(bf16[4,128,512]{2,1,0:T(8,128)(2,1)S(1)} %get-tuple-element.69.refs_0_), channel_id=1, source_target_pairs={{8,0},{16,8},{24,16},{32,24},{40,32},{48,40},{56,48},{0,56},{72,64... | collective-permute-start | bytes 1572872 | tf_op jit(solution)/shard_map/ppermute | solution.py:30
  21.8 13.9 %collective-permute-start.9 = (bf16[4,128,512]{2,1,0:T(8,128)(2,1)S(1)}, bf16[4,128,512]{2,1,0:T(8,128)(2,1)S(1)}, u32[]{:S(2)}, u32[]{:S(2)}) collective-permute-start(bf16[4,128,512]{2,1,0:T(8,128)(2,1)S(1)} %get-tuple-element.69.refs_0_), channel_id=1, source_target_pairs={{56,0},{0,8},{8,16},{16,24},{24,32},{32,40},{40,48},{48,56},{120,6... | collective-permute-start | bytes 1572872 | tf_op jit(solution)/shard_map/ppermute | solution.py:30
  27.1 10.7 %collective-permute-start.7 = (bf16[4,128,512]{2,1,0:T(8,128)(2,1)S(1)}, bf16[4,128,512]{2,1,0:T(8,128)(2,1)S(1)}, u32[]{:S(2)}, u32[]{:S(2)}) collective-permute-start(bf16[4,128,512]{2,1,0:T(8,128)(2,1)S(1)} %get-tuple-element.67), channel_id=1, source_target_pairs={{1,0},{0,1},{3,2},{2,3},{5,4},{4,5},{7,6},{6,7},{9,8},{8,9},{11,10... | collective-permute-start | bytes 1572872 | tf_op jit(solution)/shard_map/ppermute | solution.py:40
  35.8 11.8 %collective-permute-start.10 = (bf16[4,128,512]{2,1,0:T(8,128)(2,1)S(1)}, bf16[4,128,512]{2,1,0:T(8,128)(2,1)S(1)}, u32[]{:S(2)}, u32[]{:S(2)}) collective-permute-start(bf16[4,128,512]{2,1,0:T(8,128)(2,1)S(1)} %collective-permute-done.8.refs_0_), channel_id=1, source_target_pairs={{8,0},{16,8},{24,16},{32,24},{40,32},{48,40},{56,48},{0,56},{72,64... | collective-permute-start | bytes 1572872 | tf_op jit(solution)/shard_map/ppermute | solution.py:30
  36.1 13.0 %collective-permute-start.11 = (bf16[4,128,512]{2,1,0:T(8,128)(2,1)S(1)}, bf16[4,128,512]{2,1,0:T(8,128)(2,1)S(1)}, u32[]{:S(2)}, u32[]{:S(2)}) collective-permute-start(bf16[4,128,512]{2,1,0:T(8,128)(2,1)S(1)} %collective-permute-done.9.refs_1_), channel_id=1, source_target_pairs={{56,0},{0,8},{8,16},{16,24},{24,32},{32,40},{40,48},{48,56},{120,6... | collective-permute-start | bytes 1572872 | tf_op jit(solution)/shard_map/ppermute | solution.py:30
  49.1 10.9 %collective-permute-start.12 = (bf16[4,128,512]{2,1,0:T(8,128)(2,1)S(1)}, bf16[4,128,512]{2,1,0:T(8,128)(2,1)S(1)}, u32[]{:S(2)}, u32[]{:S(2)}) collective-permute-start(bf16[4,128,512]{2,1,0:T(8,128)(2,1)S(1)} %collective-permute-done.10.refs_0_), channel_id=1, source_target_pairs={{8,0},{16,8},{24,16},{32,24},{40,32},{48,40},{56,48},{0,56},{72,64... | collective-permute-start | bytes 1572872 | tf_op jit(solution)/shard_map/ppermute | solution.py:30
  49.4 12.2 %collective-permute-start.13 = (bf16[4,128,512]{2,1,0:T(8,128)(2,1)S(1)}, bf16[4,128,512]{2,1,0:T(8,128)(2,1)S(1)}, u32[]{:S(2)}, u32[]{:S(2)}) collective-permute-start(bf16[4,128,512]{2,1,0:T(8,128)(2,1)S(1)} %collective-permute-done.11.refs_1_), channel_id=1, source_target_pairs={{56,0},{0,8},{8,16},{16,24},{24,32},{32,40},{40,48},{48,56},{120,6... | collective-permute-start | bytes 1572872 | tf_op jit(solution)/shard_map/ppermute | solution.py:30
  61.6 8.3 %collective-permute-start.14 = (bf16[2,128,512]{2,1,0:T(8,128)(2,1)S(1)}, bf16[2,128,512]{2,1,0:T(8,128)(2,1)S(1)}, u32[]{:S(2)}, u32[]{:S(2)}) collective-permute-start(bf16[2,128,512]{2,1,0:T(8,128)(2,1)S(1)} %slice.17), channel_id=1, source_target_pairs={{8,0},{16,8},{24,16},{32,24},{40,32},{48,40},{56,48},{0,56},{72,64... | collective-permute-start | bytes 786440 | tf_op jit(solution)/shard_map/ppermute | solution.py:30
  61.9 7.9 %collective-permute-start.15 = (bf16[2,128,512]{2,1,0:T(8,128)(2,1)S(1)}, bf16[2,128,512]{2,1,0:T(8,128)(2,1)S(1)}, u32[]{:S(2)}, u32[]{:S(2)}) collective-permute-start(bf16[2,128,512]{2,1,0:T(8,128)(2,1)S(1)} %slice.18), channel_id=1, source_target_pairs={{56,0},{0,8},{8,16},{16,24},{24,32},{32,40},{40,48},{48,56},{120,6... | collective-permute-start | bytes 786440 | tf_op jit(solution)/shard_map/ppermute | solution.py:30
  73.4 3.4 %collective-permute-start.16 = (f32[512,512]{1,0:T(8,128)S(1)}, f32[512,512]{1,0:T(8,128)S(1)}, u32[]{:S(2)}, u32[]{:S(2)}) collective-permute-start(f32[512,512]{1,0:T(8,128)S(1)} %slice_bitcast_fusion), channel_id=1, source_target_pairs={{1,0},{0,1},{3,2},{2,3},{5,4},{4,5},{7,6},{6,7},{9,8},{8,9},{11,10... | collective-permute-start | bytes 3145736 | tf_op jit(solution)/shard_map/ppermute | solution.py:40
  73.5 9.9 %collective-permute-start.20 = (bf16[2,128,512]{2,1,0:T(8,128)(2,1)S(1)}, bf16[2,128,512]{2,1,0:T(8,128)(2,1)S(1)}, u32[]{:S(2)}, u32[]{:S(2)}) collective-permute-start(bf16[2,128,512]{2,1,0:T(8,128)(2,1)S(1)} %get-tuple-element.93), channel_id=1, source_target_pairs={{56,0},{0,8},{8,16},{16,24},{24,32},{32,40},{40,48},{48,56},{120,6... | collective-permute-start | bytes 786440 | tf_op jit(solution)/shard_map/ppermute | solution.py:30
  73.8 9.6 %collective-permute-start.21 = (bf16[2,128,512]{2,1,0:T(8,128)(2,1)S(1)}, bf16[2,128,512]{2,1,0:T(8,128)(2,1)S(1)}, u32[]{:S(2)}, u32[]{:S(2)}) collective-permute-start(bf16[2,128,512]{2,1,0:T(8,128)(2,1)S(1)} %get-tuple-element.94), channel_id=1, source_target_pairs={{8,0},{16,8},{24,16},{32,24},{40,32},{48,40},{56,48},{0,56},{72,64... | collective-permute-start | bytes 786440 | tf_op jit(solution)/shard_map/ppermute | solution.py:30
  76.9 10.1 %collective-permute-start.17 = (bf16[128,512]{1,0:T(8,128)(2,1)S(1)}, bf16[128,512]{1,0:T(8,128)(2,1)S(1)}, u32[]{:S(2)}, u32[]{:S(2)}) collective-permute-start(bf16[128,512]{1,0:T(8,128)(2,1)S(1)} %get-tuple-element.84), channel_id=1, source_target_pairs={{6,0},{7,1},{0,2},{1,3},{2,4},{3,5},{4,6},{5,7},{14,8},{15,9},{8,1... | collective-permute-start | bytes 393224 | tf_op jit(solution)/shard_map/ppermute | solution.py:35
  83.4 6.8 %collective-permute-start.18 = (bf16[128,512]{1,0:T(8,128)(2,1)S(1)}, bf16[128,512]{1,0:T(8,128)(2,1)S(1)}, u32[]{:S(2)}, u32[]{:S(2)}) collective-permute-start(bf16[128,512]{1,0:T(8,128)(2,1)S(1)} %get-tuple-element.85), channel_id=1, source_target_pairs={{4,0},{5,1},{6,2},{7,3},{0,4},{1,5},{2,6},{3,7},{12,8},{13,9},{14,... | collective-permute-start | bytes 393224 | tf_op jit(solution)/shard_map/ppermute | solution.py:35
  83.6 11.5 %collective-permute-start.27 = (bf16[4,128,256]{2,1,0:T(8,128)(2,1)S(1)}, bf16[4,128,256]{2,1,0:T(8,128)(2,1)S(1)}, u32[]{:S(2)}, u32[]{:S(2)}) collective-permute-start(bf16[4,128,256]{2,1,0:T(8,128)(2,1)S(1)} %get-tuple-element.110), channel_id=1, source_target_pairs={{56,0},{0,8},{8,16},{16,24},{24,32},{32,40},{40,48},{48,56},{120,6... | collective-permute-start | bytes 786440 | tf_op jit(solution)/shard_map/ppermute | solution.py:30
  83.7 11.4 %collective-permute-start.28 = (bf16[4,128,256]{2,1,0:T(8,128)(2,1)S(1)}, bf16[4,128,256]{2,1,0:T(8,128)(2,1)S(1)}, u32[]{:S(2)}, u32[]{:S(2)}) collective-permute-start(bf16[4,128,256]{2,1,0:T(8,128)(2,1)S(1)} %get-tuple-element.111), channel_id=1, source_target_pairs={{8,0},{16,8},{24,16},{32,24},{40,32},{48,40},{56,48},{0,56},{72,64... | collective-permute-start | bytes 786440 | tf_op jit(solution)/shard_map/ppermute | solution.py:30
  87.0 12.8 %collective-permute-start.22 = (bf16[4,128,256]{2,1,0:T(8,128)(2,1)S(1)}, bf16[4,128,256]{2,1,0:T(8,128)(2,1)S(1)}, u32[]{:S(2)}, u32[]{:S(2)}) collective-permute-start(bf16[4,128,256]{2,1,0:T(8,128)(2,1)S(1)} %get-tuple-element.101), channel_id=1, source_target_pairs={{56,0},{0,8},{8,16},{16,24},{24,32},{32,40},{40,48},{48,56},{120,6... | collective-permute-start | bytes 786440 | tf_op jit(solution)/shard_map/ppermute | solution.py:30
  87.0 12.8 %collective-permute-start.23 = (bf16[4,128,256]{2,1,0:T(8,128)(2,1)S(1)}, bf16[4,128,256]{2,1,0:T(8,128)(2,1)S(1)}, u32[]{:S(2)}, u32[]{:S(2)}) collective-permute-start(bf16[4,128,256]{2,1,0:T(8,128)(2,1)S(1)} %get-tuple-element.102), channel_id=1, source_target_pairs={{8,0},{16,8},{24,16},{32,24},{40,32},{48,40},{56,48},{0,56},{72,64... | collective-permute-start | bytes 786440 | tf_op jit(solution)/shard_map/ppermute | solution.py:30
  90.2 5.0 %collective-permute-start.19 = (bf16[128,512]{1,0:T(8,128)(2,1)S(1)}, bf16[128,512]{1,0:T(8,128)(2,1)S(1)}, u32[]{:S(2)}, u32[]{:S(2)}) collective-permute-start(bf16[128,512]{1,0:T(8,128)(2,1)S(1)} %get-tuple-element.86), channel_id=1, source_target_pairs={{2,0},{3,1},{4,2},{5,3},{6,4},{7,5},{0,6},{1,7},{10,8},{11,9},{12,... | collective-permute-start | bytes 393224 | tf_op jit(solution)/shard_map/ppermute | solution.py:35
  95.3 10.5 %collective-permute-start.29 = (bf16[4,128,256]{2,1,0:T(8,128)(2,1)S(1)}, bf16[4,128,256]{2,1,0:T(8,128)(2,1)S(1)}, u32[]{:S(2)}, u32[]{:S(2)}) collective-permute-start(bf16[4,128,256]{2,1,0:T(8,128)(2,1)S(1)} %get-tuple-element.114), channel_id=1, source_target_pairs={{56,0},{0,8},{8,16},{16,24},{24,32},{32,40},{40,48},{48,56},{120,6... | collective-permute-start | bytes 786440 | tf_op jit(solution)/shard_map/ppermute | solution.py:30
  95.4 10.4 %collective-permute-start.30 = (bf16[4,128,256]{2,1,0:T(8,128)(2,1)S(1)}, bf16[4,128,256]{2,1,0:T(8,128)(2,1)S(1)}, u32[]{:S(2)}, u32[]{:S(2)}) collective-permute-start(bf16[4,128,256]{2,1,0:T(8,128)(2,1)S(1)} %get-tuple-element.115), channel_id=1, source_target_pairs={{8,0},{16,8},{24,16},{32,24},{40,32},{48,40},{56,48},{0,56},{72,64... | collective-permute-start | bytes 786440 | tf_op jit(solution)/shard_map/ppermute | solution.py:30
  99.9 11.5 %collective-permute-start.24 = (bf16[4,128,256]{2,1,0:T(8,128)(2,1)S(1)}, bf16[4,128,256]{2,1,0:T(8,128)(2,1)S(1)}, u32[]{:S(2)}, u32[]{:S(2)}) collective-permute-start(bf16[4,128,256]{2,1,0:T(8,128)(2,1)S(1)} %get-tuple-element.103), channel_id=1, source_target_pairs={{56,0},{0,8},{8,16},{16,24},{24,32},{32,40},{40,48},{48,56},{120,6... | collective-permute-start | bytes 786440 | tf_op jit(solution)/shard_map/ppermute | solution.py:30
  100.0 11.5 %collective-permute-start.25 = (bf16[4,128,256]{2,1,0:T(8,128)(2,1)S(1)}, bf16[4,128,256]{2,1,0:T(8,128)(2,1)S(1)}, u32[]{:S(2)}, u32[]{:S(2)}) collective-permute-start(bf16[4,128,256]{2,1,0:T(8,128)(2,1)S(1)} %get-tuple-element.104), channel_id=1, source_target_pairs={{8,0},{16,8},{24,16},{32,24},{40,32},{48,40},{56,48},{0,56},{72,64... | collective-permute-start | bytes 786440 | tf_op jit(solution)/shard_map/ppermute | solution.py:30
  106.0 11.1 %collective-permute-start.31 = (bf16[4,128,256]{2,1,0:T(8,128)(2,1)S(1)}, bf16[4,128,256]{2,1,0:T(8,128)(2,1)S(1)}, u32[]{:S(2)}, u32[]{:S(2)}) collective-permute-start(bf16[4,128,256]{2,1,0:T(8,128)(2,1)S(1)} %get-tuple-element.116), channel_id=1, source_target_pairs={{56,0},{0,8},{8,16},{16,24},{24,32},{32,40},{40,48},{48,56},{120,6... | collective-permute-start | bytes 786440 | tf_op jit(solution)/shard_map/ppermute | solution.py:30
  106.0 11.0 %collective-permute-start.33 = (bf16[4,128,256]{2,1,0:T(8,128)(2,1)S(1)}, bf16[4,128,256]{2,1,0:T(8,128)(2,1)S(1)}, u32[]{:S(2)}, u32[]{:S(2)}) collective-permute-start(bf16[4,128,256]{2,1,0:T(8,128)(2,1)S(1)} %get-tuple-element.118), channel_id=1, source_target_pairs={{8,0},{16,8},{24,16},{32,24},{40,32},{48,40},{56,48},{0,56},{72,64... | collective-permute-start | bytes 786440 | tf_op jit(solution)/shard_map/ppermute | solution.py:30
  111.6 9.2 %collective-permute-start.26 = (bf16[4,128,256]{2,1,0:T(8,128)(2,1)S(1)}, bf16[4,128,256]{2,1,0:T(8,128)(2,1)S(1)}, u32[]{:S(2)}, u32[]{:S(2)}) collective-permute-start(bf16[4,128,256]{2,1,0:T(8,128)(2,1)S(1)} %get-tuple-element.105), channel_id=1, source_target_pairs={{56,0},{0,8},{8,16},{16,24},{24,32},{32,40},{40,48},{48,56},{120,6... | collective-permute-start | bytes 786440 | tf_op jit(solution)/shard_map/ppermute | solution.py:30
  111.7 9.1 %collective-permute-start.32 = (bf16[4,128,256]{2,1,0:T(8,128)(2,1)S(1)}, bf16[4,128,256]{2,1,0:T(8,128)(2,1)S(1)}, u32[]{:S(2)}, u32[]{:S(2)}) collective-permute-start(bf16[4,128,256]{2,1,0:T(8,128)(2,1)S(1)} %get-tuple-element.117), channel_id=1, source_target_pairs={{8,0},{16,8},{24,16},{32,24},{40,32},{48,40},{56,48},{0,56},{72,64... | collective-permute-start | bytes 786440 | tf_op jit(solution)/shard_map/ppermute | solution.py:30
  121.0 5.1 %collective-permute-start.34 = (bf16[128,512]{1,0:T(8,128)(2,1)S(1)}, bf16[128,512]{1,0:T(8,128)(2,1)S(1)}, u32[]{:S(2)}, u32[]{:S(2)}) collective-permute-start(bf16[128,512]{1,0:T(8,128)(2,1)S(1)} %get-tuple-element.120), channel_id=1, source_target_pairs={{192,0},{200,8},{208,16},{216,24},{224,32},{232,40},{240,48},{248,... | collective-permute-start | bytes 393224 | tf_op jit(solution)/shard_map/ppermute | solution.py:25
  121.9 6.6 %collective-permute-start.35 = (bf16[128,512]{1,0:T(8,128)(2,1)S(1)}, bf16[128,512]{1,0:T(8,128)(2,1)S(1)}, u32[]{:S(2)}, u32[]{:S(2)}) collective-permute-start(bf16[128,512]{1,0:T(8,128)(2,1)S(1)} %get-tuple-element.121), channel_id=1, source_target_pairs={{128,0},{136,8},{144,16},{152,24},{160,32},{168,40},{176,48},{184,... | collective-permute-start | bytes 393224 | tf_op jit(solution)/shard_map/ppermute | solution.py:25
  122.7 7.1 %collective-permute-start.36 = (bf16[128,512]{1,0:T(8,128)(2,1)S(1)}, bf16[128,512]{1,0:T(8,128)(2,1)S(1)}, u32[]{:S(2)}, u32[]{:S(2)}) collective-permute-start(bf16[128,512]{1,0:T(8,128)(2,1)S(1)} %get-tuple-element.122), channel_id=1, source_target_pairs={{64,0},{72,8},{80,16},{88,24},{96,32},{104,40},{112,48},{120,56},{... | collective-permute-start | bytes 393224 | tf_op jit(solution)/shard_map/ppermute | solution.py:25
where the time goes:
time: 132 us; the launch traced here: 131 us
  starting transfers between devices  50.1 us (38%)
  waiting for transfers between devices  44.3 us (34%)
  Pallas kernels  32.1 us (24%)
  other arithmetic  2.22 us (2%)
    ppermute x22, starting transfers between devices, from_z(): return lax.ppermute(x, 'row', perm)  35.4 us
    ppermute x22, waiting for transfers between devices, from_z(): return lax.ppermute(x, 'row', perm)  32.6 us
    pallas_call x5, Pallas kernels, chunk(): pl.pallas_call(functools.partial(chunk_kernel, ds, first, split), out_sha...  24.9 us
    ppermute x7, starting transfers between devices, from_y(): return lax.ppermute(x, 'row', perm)  8.79 us
    ppermute x7, waiting for transfers between devices, from_y(): return lax.ppermute(x, 'row', perm)  6.69 us
    ppermute x6, starting transfers between devices, from_x(): return lax.ppermute(x, 'col', perm)  5.73 us
    pallas_call x1, Pallas kernels, prep(): pl.pallas_call(prep_kernel, out_shape=(jax.ShapeDtypeStruct((NZ, NX * NC...  5.29 us
    ppermute x6, waiting for transfers between devices, from_x(): return lax.ppermute(x, 'col', perm)  4.99 us
  transfers between devices with their start and end apart: 37, of which 17 were waited for; matrix products, arithmetic and copies ran while one was open for 1% of the time, Pallas kernels for 21%

commit v1 on v0

--- a/solution.py
+++ b/solution.py
@@ -18,6 +18,7 @@
 SLOTS = 16
 BUFFERS = 4
 PIECES = ((0, 256), (256, 512))
+FAR = NZ // 2
 
 
 def from_y(x, k):
@@ -135,7 +136,7 @@
     )(r)
 
 
-def chunk_kernel(ds, first, split, w_ref, r_ref, row_sums, *refs):
+def chunk_kernel(ds, first, w_ref, r_ref, row_sums, *refs):
     n = len(ds)
     k_refs, refs = refs[:n], refs[n:]
     m_ref, refs = refs[0], refs[1:]
@@ -143,11 +144,19 @@
         acc_in, refs = refs[0], refs[1:]
     p = len(PIECES)
     rows_out, refs, (g_acc, k_all, col_sums) = refs[0], refs[1:-3], refs[-3:]
-    for c in range(n):
-        for e in range(NY):
-            g_acc[c, e * T : (e + 1) * T] = jnp.zeros((T, C), F32)
-            k_all[c, e * T : (e + 1) * T] = k_refs[c][e]
-            col_sums[c, e : e + 1] = jnp.sum(k_refs[c][e].astype(F32), axis=0, keepdims=True)
+
+    def begin(e, _):
+        at = pl.ds(pl.multiple_of(e * T, T), T)
+        for h in range(2):
+            rows_out[h, at] = jnp.zeros((T, C), F32) if first else acc_in[h, at]
+        for c in range(n):
+            k = k_refs[c][e]
+            k_all[c, at] = k
+            g_acc[c, at] = jnp.zeros((T, C), F32)
+            col_sums[c, pl.ds(e, 1)] = jnp.sum(k.astype(F32), axis=0, keepdims=True)
+        return 0
+
+    lax.fori_loop(0, NY, begin, 0)
 
     def body(step, _):
         c, h = step // 2, step % 2
@@ -166,32 +175,29 @@
         for f in range(NX):
             v = sum(weights[f][e] * col_sums[c, e : e + 1] for e in range(NY))
             rows = r[f * T : (f + 1) * T] + v
-            base = 0.0 if first and n == 1 else (rows_out if first else acc_in)[h, f * T : (f + 1) * T]
-            rows_out[h, f * T : (f + 1) * T] = rows + base
+            rows_out[h, f * T : (f + 1) * T] += rows
         return 0
 
     lax.fori_loop(0, 2 * n, body, 0)
-    for c in range(n):
-        for e in range(NY):
-            done = g_acc[c, e * T : (e + 1) * T].astype(BF)
-            if split:
-                refs[e // 2][e % 2] = done
-                continue
+
+    def end(e, _):
+        for c in range(n):
+            done = g_acc[c, pl.ds(pl.multiple_of(e * T, T), T)].astype(BF)
             for q, (lo, hi) in enumerate(PIECES):
                 refs[c * p + q][e] = done[:, lo:hi]
-
-
-def chunk(ds, w, rows, ks, m, acc, split=False):
+        return 0
+
+    lax.fori_loop(0, NY, end, 0)
+
+
+def chunk(ds, w, rows, ks, m, acc):
     n, p = len(ds), len(PIECES)
     first = acc is None
     args = [w, *rows, *ks, m] + ([] if first else [acc])
     shapes = [((2, NX * T, C), F32)]
-    if split:
-        shapes += [((2, T, C), BF)] * 2
-    else:
-        shapes += [((NY, T, hi - lo), BF) for _ in ds for lo, hi in PIECES]
+    shapes += [((NY, T, hi - lo), BF) for _ in ds for lo, hi in PIECES]
     out = pl.pallas_call(
-        functools.partial(chunk_kernel, ds, first, split),
+        functools.partial(chunk_kernel, ds, first),
         out_shape=[jax.ShapeDtypeStruct(*s) for s in shapes],
         in_specs=[SMEM] + [VMEM] * (len(args) - 1),
         out_specs=[VMEM] * len(shapes),
@@ -203,9 +209,68 @@
         ),
         name="chunk",
     )(*args)
-    if split:
-        return out
     return out[0], *[out[1 + c * p : 1 + (c + 1) * p] for c in range(n)]
+
+
+def far_cols_kernel(w_ref, r_ref, row_sums, k_ref, m_ref, g_up, g_down, coef_ref, g_acc):
+    g_acc[...] = jnp.zeros_like(g_acc)
+
+    def body(h, _):
+        x, k = r_ref[h], k_ref[...].reshape(NY * T, C)
+        s = dot(x, k, ((1,), (1,)))
+        at = pl.ds(pl.multiple_of(h * NX * T, NX * T), NX * T)
+        coef = (1.0 / (1.0 - jnp.exp(s))).astype(BF) * m_ref[FAR, at]
+        coef_ref[h] = coef
+        g = dot(coef, x, ((0,), (0,)))
+        for e in range(NY):
+            v = sum(w_ref[h * NX + f, FAR * NY + e] * row_sums[h, f : f + 1] for f in range(NX))
+            g_acc[e * T : (e + 1) * T] += g[e * T : (e + 1) * T] + v
+        return 0
+
+    lax.fori_loop(0, 2, body, 0)
+    for e in range(NY):
+        (g_up, g_down)[e // 2][e % 2] = g_acc[e * T : (e + 1) * T].astype(BF)
+
+
+def far_cols(w, rows, k, m):
+    return pl.pallas_call(
+        far_cols_kernel,
+        out_shape=[jax.ShapeDtypeStruct((2, T, C), BF)] * 2 + [jax.ShapeDtypeStruct((2, NX * T, NY * T), BF)],
+        in_specs=[SMEM] + [VMEM] * 4,
+        out_specs=[VMEM] * 3,
+        scratch_shapes=[pltpu.VMEM((NY * T, C), F32)],
+        compiler_params=PARAMS,
+        cost_estimate=pl.CostEstimate(flops=4 * 1024 * 512 * 512, bytes_accessed=4 << 20, transcendentals=1024 * 512),
+        name="far_cols",
+    )(w, *rows, k, m)
+
+
+def far_rows_kernel(w_ref, coef_ref, k_ref, acc_in, keep, send, col_sums):
+    for e in range(NY):
+        col_sums[e : e + 1] = jnp.sum(k_ref[e].astype(F32), axis=0, keepdims=True)
+
+    for h in range(2):
+        r = dot(coef_ref[h], k_ref[...].reshape(NY * T, C), ((1,), (0,)))
+        for f in range(NX):
+            v = sum(w_ref[h * NX + f, FAR * NY + e] * col_sums[e : e + 1] for e in range(NY))
+            total = r[f * T : (f + 1) * T] + v + acc_in[h, f * T : (f + 1) * T]
+            if h:
+                send[f] = total.astype(BF)
+            else:
+                keep[f] = total
+
+
+def far_rows(w, coef, k, acc):
+    return pl.pallas_call(
+        far_rows_kernel,
+        out_shape=[jax.ShapeDtypeStruct((NX, T, C), F32), jax.ShapeDtypeStruct((NX, T, C), BF)],
+        in_specs=[SMEM] + [VMEM] * 3,
+        out_specs=[VMEM, VMEM],
+        scratch_shapes=[pltpu.VMEM((8, C), F32)],
+        compiler_params=PARAMS,
+        cost_estimate=pl.CostEstimate(flops=2 * 1024 * 512 * 512, bytes_accessed=8 << 20, transcendentals=0),
+        name="far_rows",
+    )(w, coef, k, acc)
 
 
 def first_hop_kernel(up_in, down_in, *refs):
@@ -276,7 +341,7 @@
 
 def row_hop_kernel(keep, arrived, own, *sends):
     for f in range(NX):
-        s = keep[0, f * T : (f + 1) * T] + arrived[f * T : (f + 1) * T]
+        s = keep[f] + arrived[f].astype(F32)
         if f:
             sends[f - 1][...] = s.astype(BF)
         else:
@@ -330,6 +395,7 @@
     first = jnp.stack(stack)
     same = jnp.stack([shard] + [from_x(shard, k) for k in (1, 2, 3)])
     m, w = prep(tie(ints, first), neg_weight, edge_masks)
+    same = jnp.stack([shard] + [from_x(shard, k) for k in (1, 2, 3)])
     p = range(len(PIECES))
 
     above, below = [first], [first]
@@ -351,7 +417,7 @@
     far_up, far_down = from_z(up[:2], 1), from_z(down[2:], -1)
     acc, g3, g5 = chunk((3, 5), w, rows, [above[3], below[3]], m, acc)
     far = jnp.concatenate([tie(far_up, acc), far_down])
-    acc, *g4 = chunk((4,), w, rows, [far], m, acc, split=True)
+    *g4, coef = far_cols(w, rows, far, m)
 
     def arrive(up, down):
         return [from_z(up[q], -1) for q in p], [from_z(down[q], 1) for q in p]
@@ -361,14 +427,17 @@
         return [x[0] for x in pairs], [x[1] for x in pairs]
 
     up_in, down_in = from_z(g4[0], -1), from_z(g4[1], 1)
-    row_own, *row_sends = row_hop(acc, from_core(acc[1]))
-    up, down = first_hop(*tie((up_in, down_in), row_own), g3, g5)
+    row_keep, row_send = far_rows(w, coef, far, acc)
+    row_own, *row_sends = row_hop(row_keep, from_core(row_send))
+    up, down = first_hop(up_in, down_in, g3, g5)
+    up_in, down_in = arrive(up, down)
+    up, down = hops(hop_kernel, up_in, down_in, g2, g6)
+    up_in, down_in = arrive(up, down)
+    up_in[0], down_in[0] = tie((up_in[0], down_in[0]), row_own)
+    up, down = hops(hop_kernel, up_in, down_in, g1, g7)
     up_in, down_in = arrive(up, down)
     row_parts = [row_own] + [from_x(row_sends[k - 1], -k) for k in (1, 2, 3)]
     up_in[1], down_in[1] = tie((up_in[1], down_in[1]), *row_parts)
-    up, down = hops(hop_kernel, up_in, down_in, g2, g6)
-    up, down = hops(hop_kernel, *arrive(up, down), g1, g7)
-    up_in, down_in = arrive(up, down)
     own, *sends = last_hop(g0, up_in, down_in)
     return final(*row_parts, own, *[from_y(sends[k - 1], -k) for k in (1, 2, 3)])
 

time: 132 us -> 127 us (0.962)
  starting transfers between devices: 50.1 us -> 46.2 us
    ppermute x22, starting transfers between devices: 35.4 us -> 32.7 us  [from_z(): return lax.ppermute(x, 'row', perm)]
    ppermute x22, waiting for transfers between devices: 32.6 us -> 30.9 us  [from_z(): return lax.ppermute(x, 'row', perm)]
    pallas_call x5 -> x6, Pallas kernels: 24.9 us -> 25.8 us  [the longest x4 21.8 us: chunk(): pl.pallas_call(functools.partial(chunk_kernel, ds, first), out_shape=[jax...]
  transfers between devices with their start and end apart: 37 -> 37, of which waited for: 17 -> 16; matrix products, arithmetic and copies ran while one was open for 1% -> 2% of each run, Pallas kernels for 21% -> 23%
where the time goes in v1:
time: 127 us; the launch traced here: 126 us
  starting transfers between devices  46.2 us (36%)
  waiting for transfers between devices  43 us (34%)
  Pallas kernels  33.2 us (26%)
  other arithmetic  2.17 us (2%)
    ppermute x22, starting transfers between devices, from_z(): return lax.ppermute(x, 'row', perm)  32.7 us
    ppermute x22, waiting for transfers between devices, from_z(): return lax.ppermute(x, 'row', perm)  30.9 us
    pallas_call x4, Pallas kernels, chunk(): pl.pallas_call(functools.partial(chunk_kernel, ds, first), out_shape=[jax...  21.8 us
    ppermute x7, starting transfers between devices, from_y(): return lax.ppermute(x, 'row', perm)  8.78 us
    ppermute x6, waiting for transfers between devices, from_x(): return lax.ppermute(x, 'col', perm)  6.1 us
    ppermute x7, waiting for transfers between devices, from_y(): return lax.ppermute(x, 'row', perm)  5.96 us
    pallas_call x1, Pallas kernels, prep(): pl.pallas_call(prep_kernel, out_shape=(jax.ShapeDtypeStruct((NZ, NX * NC...  5.57 us
    ppermute x6, starting transfers between devices, from_x(): return lax.ppermute(x, 'col', perm)  4.53 us
  transfers between devices with their start and end apart: 37, of which 16 were waited for; matrix products, arithmetic and copies ran while one was open for 2% of the time, Pallas kernels for 23%

profile of v1, /device:TPU:24, one launch (start us, length us, event | category | flops | bytes accessed | tf_op | source)
XLA Modules:
  0.0 126.4 jit_solution(15270371540918049998)
XLA Ops:
  0.0 1.0 convert_element_type.3
  1.0 0.8 collective-permute-start
  1.8 2.5 %collective-permute-start.2 = (bf16[128,512]{1,0:T(8,128)(2,1)S(1)}, bf16[128,512]{1,0:T(8,128)(2,1)S(1)}, u32[]{:S(2)}, u32[]{:S(2)}) collective-permute-start(bf16[128,512]{1,0:T(8,128)(2,1)S(1)} %convert_element_type.3), channel_id=1, source_target_pairs={{192,0},{200,8},{208,16},{216,24},{224,32},{232,40},{240,48},{248,... | collective-permute-start | bytes 393224 | tf_op jit(solution)/shard_map/ppermute | solution.py:26
  4.3 2.8 %collective-permute-start.4 = (bf16[128,512]{1,0:T(8,128)(2,1)S(1)}, bf16[128,512]{1,0:T(8,128)(2,1)S(1)}, u32[]{:S(2)}, u32[]{:S(2)}) collective-permute-start(bf16[128,512]{1,0:T(8,128)(2,1)S(1)} %convert_element_type.3), channel_id=1, source_target_pairs={{2,0},{3,1},{4,2},{5,3},{6,4},{7,5},{0,6},{1,7},{10,8},{11,9},{12,... | collective-permute-start | bytes 393224 | tf_op jit(solution)/shard_map/ppermute | solution.py:36
  7.1 0.8 collective-permute-start.5
  7.9 0.9 collective-permute-start.6
  8.8 0.1 collective-permute-start.1
  8.9 3.3 %collective-permute-start.3 = (bf16[64,512]{1,0:T(8,128)(2,1)S(1)}, bf16[64,512]{1,0:T(8,128)(2,1)S(1)}, u32[]{:S(2)}, u32[]{:S(2)}) collective-permute-start(bf16[64,512]{1,0:T(8,128)(2,1)S(1)} %slice.17), channel_id=1, source_target_pairs={{192,0},{200,8},{208,16},{216,24},{224,32},{232,40},{240,48},{248,... | collective-permute-start | bytes 196616 | tf_op jit(solution)/shard_map/ppermute | solution.py:26
  12.2 1.0 convert_bitcast_fusion
  13.8 0.8 concatenate.10.ints
  14.6 1.1 collective-permute-done.6
  15.8 0.1 fusion.3
  15.9 5.9 %collective-permute-start.8 = (bf16[4,128,512]{2,1,0:T(8,128)(2,1)S(1)}, bf16[4,128,512]{2,1,0:T(8,128)(2,1)S(1)}, u32[]{:S(2)}, u32[]{:S(2)}) collective-permute-start(bf16[4,128,512]{2,1,0:T(8,128)(2,1)S(1)} %get-tuple-element.71.refs_0_), channel_id=1, source_target_pairs={{8,0},{16,8},{24,16},{32,24},{40,32},{48,40},{56,48},{0,56},{72,64... | collective-permute-start | bytes 1572872 | tf_op jit(solution)/shard_map/ppermute | solution.py:31
  21.8 5.6 %prep.1 = (bf16[8,1024,512]{2,1,0:T(8,128)(2,1)S(1)}, f32[8,32]{1,0:T(8,128)S(1)}) custom-call(s32[325]{0:T(512)S(1)} %concatenate.10.ints, f32[1,32]{1,0:T(1,128)S(1)} %copy-done, s32[1,128,128,128]{3,2,1,0:T(8,128)} %masks.1), custom_call_target="tpu_custom_call" | custom-call | bytes 16777216 | tf_op jit(solution)/shard_map/prep/pallas_call | solution.py:100
  27.4 0.1 collective-permute-start.7
  27.5 4.9 %collective-permute-done.8.refs_0_ = bf16[4,128,512]{2,1,0:T(8,128)(2,1)S(1)} collective-permute-done((bf16[4,128,512]{2,1,0:T(8,128)(2,1)S(1)}, bf16[4,128,512]{2,1,0:T(8,128)(2,1)S(1)}, u32[]{:S(2)}, u32[]{:S(2)}) %collective-permute-start.8) | collective-permute-done | bytes 524320 | tf_op jit(solution)/shard_map/ppermute | solution.py:31
  32.4 3.4 %collective-permute-done.9.refs_1_ = bf16[4,128,512]{2,1,0:T(8,128)(2,1)S(1)} collective-permute-done((bf16[4,128,512]{2,1,0:T(8,128)(2,1)S(1)}, bf16[4,128,512]{2,1,0:T(8,128)(2,1)S(1)}, u32[]{:S(2)}, u32[]{:S(2)}) %collective-permute-start.9) | collective-permute-done | bytes 524320 | tf_op jit(solution)/shard_map/ppermute | solution.py:31
  35.8 0.3 collective-permute-start.10
  36.1 1.7 %collective-permute-start.11 = (bf16[4,128,512]{2,1,0:T(8,128)(2,1)S(1)}, bf16[4,128,512]{2,1,0:T(8,128)(2,1)S(1)}, u32[]{:S(2)}, u32[]{:S(2)}) collective-permute-start(bf16[4,128,512]{2,1,0:T(8,128)(2,1)S(1)} %collective-permute-done.9.refs_1_), channel_id=1, source_target_pairs={{56,0},{0,8},{8,16},{16,24},{24,32},{32,40},{40,48},{48,56},{120,6... | collective-permute-start | bytes 1572872 | tf_op jit(solution)/shard_map/ppermute | solution.py:31
  37.8 0.1 pad_maximum_fusion.r_ref
  37.9 0.2 row_sums.1
  38.1 3.4 %chunk.4 = (f32[2,512,512]{2,1,0:T(8,128)S(1)}, bf16[4,128,256]{2,1,0:T(8,128)(2,1)S(1)}, bf16[4,128,256]{2,1,0:T(8,128)(2,1)S(1)}) custom-call(f32[8,32]{1,0:T(8,128)S(1)} %get-tuple-element.74.w_ref, bf16[2,512,512]{2,1,0:T(8,128)(2,1)S(1)} %pad_maximum_fusion.r_ref, f32[2,8,512]{2,1,0:T(8,128)S(1)} %row_sums.1, ...), custom_call_target="tpu_custom_call" | custom-call | flops 1610612736 | bytes 8388608 | tf_op jit(solution)/shard_map/chunk/pallas_call | solution.py:199
  41.5 6.1 %chunk.5 = (f32[2,512,512]{2,1,0:T(8,128)S(1)}, bf16[4,128,256]{2,1,0:T(8,128)(2,1)S(1)}, bf16[4,128,256]{2,1,0:T(8,128)(2,1)S(1)}, bf16[4,128,256]{2,1,0:T(8,128)(2,1)S(1)}, bf16[4,128,256]{2,1,0:T(8,128)(2,1)S(1)}) custom-call(f32[8,32]{1,0:T(8,128)S(1)} %get-tuple-element.74.w_ref, ...), custom_call_target="tpu_custom_call", output_to_operand_aliasing={{0}: (6, {})} | custom-call | flops 3221225472 | bytes 10485760 | tf_op jit(solution)/shard_map/chunk/pallas_call | solution.py:199
  47.7 1.4 %collective-permute-done.11.refs_1_ = bf16[4,128,512]{2,1,0:T(8,128)(2,1)S(1)} collective-permute-done((bf16[4,128,512]{2,1,0:T(8,128)(2,1)S(1)}, bf16[4,128,512]{2,1,0:T(8,128)(2,1)S(1)}, u32[]{:S(2)}, u32[]{:S(2)}) %collective-permute-start.11) | collective-permute-done | bytes 524320 | tf_op jit(solution)/shard_map/ppermute | solution.py:31
  49.1 0.4 collective-permute-start.12
  49.5 1.7 %collective-permute-start.13 = (bf16[4,128,512]{2,1,0:T(8,128)(2,1)S(1)}, bf16[4,128,512]{2,1,0:T(8,128)(2,1)S(1)}, u32[]{:S(2)}, u32[]{:S(2)}) collective-permute-start(bf16[4,128,512]{2,1,0:T(8,128)(2,1)S(1)} %collective-permute-done.11.refs_1_), channel_id=1, source_target_pairs={{56,0},{0,8},{8,16},{16,24},{24,32},{32,40},{40,48},{48,56},{120,6... | collective-permute-start | bytes 1572872 | tf_op jit(solution)/shard_map/ppermute | solution.py:31
  51.1 6.1 %chunk.6 = (f32[2,512,512]{2,1,0:T(8,128)S(1)}, bf16[4,128,256]{2,1,0:T(8,128)(2,1)S(1)}, bf16[4,128,256]{2,1,0:T(8,128)(2,1)S(1)}, bf16[4,128,256]{2,1,0:T(8,128)(2,1)S(1)}, bf16[4,128,256]{2,1,0:T(8,128)(2,1)S(1)}) custom-call(f32[8,32]{1,0:T(8,128)S(1)} %get-tuple-element.74.w_ref, ...), custom_call_target="tpu_custom_call", output_to_operand_aliasing={{0}: (6, {})} | custom-call | flops 3221225472 | bytes 10485760 | tf_op jit(solution)/shard_map/chunk/pallas_call | solution.py:199
  57.2 2.7 %collective-permute-done.12.refs_0_ = bf16[4,128,512]{2,1,0:T(8,128)(2,1)S(1)} collective-permute-done((bf16[4,128,512]{2,1,0:T(8,128)(2,1)S(1)}, bf16[4,128,512]{2,1,0:T(8,128)(2,1)S(1)}, u32[]{:S(2)}, u32[]{:S(2)}) %collective-permute-start.12) | collective-permute-done | bytes 524320 | tf_op jit(solution)/shard_map/ppermute | solution.py:31
  60.0 1.9 %collective-permute-done.13.refs_1_ = bf16[4,128,512]{2,1,0:T(8,128)(2,1)S(1)} collective-permute-done((bf16[4,128,512]{2,1,0:T(8,128)(2,1)S(1)}, bf16[4,128,512]{2,1,0:T(8,128)(2,1)S(1)}, u32[]{:S(2)}, u32[]{:S(2)}) %collective-permute-start.13) | collective-permute-done | bytes 524320 | tf_op jit(solution)/shard_map/ppermute | solution.py:31
  62.0 0.4 collective-permute-start.14
  62.3 1.8 %collective-permute-start.15 = (bf16[2,128,512]{2,1,0:T(8,128)(2,1)S(1)}, bf16[2,128,512]{2,1,0:T(8,128)(2,1)S(1)}, u32[]{:S(2)}, u32[]{:S(2)}) collective-permute-start(bf16[2,128,512]{2,1,0:T(8,128)(2,1)S(1)} %slice.15), channel_id=1, source_target_pairs={{56,0},{0,8},{8,16},{16,24},{24,32},{32,40},{40,48},{48,56},{120,6... | collective-permute-start | bytes 786440 | tf_op jit(solution)/shard_map/ppermute | solution.py:31
  64.2 6.1 %chunk.7 = (f32[2,512,512]{2,1,0:T(8,128)S(1)}, bf16[4,128,256]{2,1,0:T(8,128)(2,1)S(1)}, bf16[4,128,256]{2,1,0:T(8,128)(2,1)S(1)}, bf16[4,128,256]{2,1,0:T(8,128)(2,1)S(1)}, bf16[4,128,256]{2,1,0:T(8,128)(2,1)S(1)}) custom-call(f32[8,32]{1,0:T(8,128)S(1)} %get-tuple-element.74.w_ref, ...), custom_call_target="tpu_custom_call", output_to_operand_aliasing={{0}: (6, {})} | custom-call | flops 3221225472 | bytes 10485760 | tf_op jit(solution)/shard_map/chunk/pallas_call | solution.py:199
  70.4 2.6 %far_cols.1 = (bf16[2,128,512]{2,1,0:T(8,128)(2,1)S(1)}, bf16[2,128,512]{2,1,0:T(8,128)(2,1)S(1)}, bf16[2,512,512]{2,1,0:T(8,128)(2,1)S(1)}) custom-call(f32[8,32]{1,0:T(8,128)S(1)} %get-tuple-element.74.w_ref, bf16[2,512,512]{2,1,0:T(8,128)(2,1)S(1)} %pad_maximum_fusion.r_ref, f32[2,8,512]{2,1,0:T(8,128)S(1)} %row_sums.1, ...), custom_call_target="tpu_custom_call" | custom-call | flops 1073741824 | bytes 4194304 | tf_op jit(solution)/shard_map/far_cols/pallas_call | solution.py:236
  73.0 0.3 collective-permute-start.20
  73.2 3.0 %collective-permute-start.21 = (bf16[2,128,512]{2,1,0:T(8,128)(2,1)S(1)}, bf16[2,128,512]{2,1,0:T(8,128)(2,1)S(1)}, u32[]{:S(2)}, u32[]{:S(2)}) collective-permute-start(bf16[2,128,512]{2,1,0:T(8,128)(2,1)S(1)} %get-tuple-element.98), channel_id=1, source_target_pairs={{8,0},{16,8},{24,16},{32,24},{40,32},{48,40},{56,48},{0,56},{72,64... | collective-permute-start | bytes 786440 | tf_op jit(solution)/shard_map/ppermute | solution.py:31
  76.3 1.3 %far_rows.1 = (f32[4,128,512]{2,1,0:T(8,128)S(1)}, bf16[4,128,512]{2,1,0:T(8,128)(2,1)S(1)}) custom-call(f32[8,32]{1,0:T(8,128)S(1)} %get-tuple-element.74.w_ref, bf16[2,512,512]{2,1,0:T(8,128)(2,1)S(1)} %get-tuple-element.84.coef_ref, bf16[4,128,512]{2,1,0:T(8,128)(2,1)S(1)} %constant_dynamic-update-slice_fusion.k_ref, ...), custom_call_target="tpu_custom_call" | custom-call | flops 536870912 | bytes 8388608 | tf_op jit(solution)/shard_map/far_rows/pallas_call | solution.py:264
  77.6 0.1 collective-permute-start.16
  77.7 2.9 %collective-permute-done.20.up_in = bf16[2,128,512]{2,1,0:T(8,128)(2,1)S(1)} collective-permute-done((bf16[2,128,512]{2,1,0:T(8,128)(2,1)S(1)}, bf16[2,128,512]{2,1,0:T(8,128)(2,1)S(1)}, u32[]{:S(2)}, u32[]{:S(2)}) %collective-permute-start.20) | collective-permute-done | bytes 262176 | tf_op jit(solution)/shard_map/ppermute | solution.py:31
  80.6 0.1 first_hop.1
  80.9 3.3 %collective-permute-start.28 = (bf16[4,128,256]{2,1,0:T(8,128)(2,1)S(1)}, bf16[4,128,256]{2,1,0:T(8,128)(2,1)S(1)}, u32[]{:S(2)}, u32[]{:S(2)}) collective-permute-start(bf16[4,128,256]{2,1,0:T(8,128)(2,1)S(1)} %get-tuple-element.115), channel_id=1, source_target_pairs={{8,0},{16,8},{24,16},{32,24},{40,32},{48,40},{56,48},{0,56},{72,64... | collective-permute-start | bytes 786440 | tf_op jit(solution)/shard_map/ppermute | solution.py:31
  84.2 3.2 %collective-permute-start.23 = (bf16[4,128,256]{2,1,0:T(8,128)(2,1)S(1)}, bf16[4,128,256]{2,1,0:T(8,128)(2,1)S(1)}, u32[]{:S(2)}, u32[]{:S(2)}) collective-permute-start(bf16[4,128,256]{2,1,0:T(8,128)(2,1)S(1)} %get-tuple-element.104), channel_id=1, source_target_pairs={{8,0},{16,8},{24,16},{32,24},{40,32},{48,40},{56,48},{0,56},{72,64... | collective-permute-start | bytes 786440 | tf_op jit(solution)/shard_map/ppermute | solution.py:31
  87.4 3.9 %collective-permute-done.27.up_in = bf16[4,128,256]{2,1,0:T(8,128)(2,1)S(1)} collective-permute-done((bf16[4,128,256]{2,1,0:T(8,128)(2,1)S(1)}, bf16[4,128,256]{2,1,0:T(8,128)(2,1)S(1)}, u32[]{:S(2)}, u32[]{:S(2)}) %collective-permute-start.27) | collective-permute-done | bytes 262176 | tf_op jit(solution)/shard_map/ppermute | solution.py:31
  91.3 0.1 hop.6
  91.4 0.3 collective-permute-start.29
  91.7 3.4 %collective-permute-start.30 = (bf16[4,128,256]{2,1,0:T(8,128)(2,1)S(1)}, bf16[4,128,256]{2,1,0:T(8,128)(2,1)S(1)}, u32[]{:S(2)}, u32[]{:S(2)}) collective-permute-start(bf16[4,128,256]{2,1,0:T(8,128)(2,1)S(1)} %get-tuple-element.117), channel_id=1, source_target_pairs={{8,0},{16,8},{24,16},{32,24},{40,32},{48,40},{56,48},{0,56},{72,64... | collective-permute-start | bytes 786440 | tf_op jit(solution)/shard_map/ppermute | solution.py:31
  95.1 1.8 %collective-permute-done.22.up_in = bf16[4,128,256]{2,1,0:T(8,128)(2,1)S(1)} collective-permute-done((bf16[4,128,256]{2,1,0:T(8,128)(2,1)S(1)}, bf16[4,128,256]{2,1,0:T(8,128)(2,1)S(1)}, u32[]{:S(2)}, u32[]{:S(2)}) %collective-permute-start.22) | collective-permute-done | bytes 262176 | tf_op jit(solution)/shard_map/ppermute | solution.py:31
  96.9 0.1 hop.4
  97.1 3.4 %collective-permute-start.25 = (bf16[4,128,256]{2,1,0:T(8,128)(2,1)S(1)}, bf16[4,128,256]{2,1,0:T(8,128)(2,1)S(1)}, u32[]{:S(2)}, u32[]{:S(2)}) collective-permute-start(bf16[4,128,256]{2,1,0:T(8,128)(2,1)S(1)} %get-tuple-element.106), channel_id=1, source_target_pairs={{8,0},{16,8},{24,16},{32,24},{40,32},{48,40},{56,48},{0,56},{72,64... | collective-permute-start | bytes 786440 | tf_op jit(solution)/shard_map/ppermute | solution.py:31
  100.5 0.1 row_hop.1
  100.7 1.8 %collective-permute-done.29.up_in = bf16[4,128,256]{2,1,0:T(8,128)(2,1)S(1)} collective-permute-done((bf16[4,128,256]{2,1,0:T(8,128)(2,1)S(1)}, bf16[4,128,256]{2,1,0:T(8,128)(2,1)S(1)}, u32[]{:S(2)}, u32[]{:S(2)}) %collective-permute-start.29) | collective-permute-done | bytes 262176 | tf_op jit(solution)/shard_map/ppermute | solution.py:31
  102.5 0.1 hop.7
  102.8 5.4 %collective-permute-done.24.up_in = bf16[4,128,256]{2,1,0:T(8,128)(2,1)S(1)} collective-permute-done((bf16[4,128,256]{2,1,0:T(8,128)(2,1)S(1)}, bf16[4,128,256]{2,1,0:T(8,128)(2,1)S(1)}, u32[]{:S(2)}, u32[]{:S(2)}) %collective-permute-start.24) | collective-permute-done | bytes 262176 | tf_op jit(solution)/shard_map/ppermute | solution.py:31
  108.2 0.1 hop.5
  108.3 2.1 %collective-permute-start.26 = (bf16[4,128,256]{2,1,0:T(8,128)(2,1)S(1)}, bf16[4,128,256]{2,1,0:T(8,128)(2,1)S(1)}, u32[]{:S(2)}, u32[]{:S(2)}) collective-permute-start(bf16[4,128,256]{2,1,0:T(8,128)(2,1)S(1)} %get-tuple-element.109), channel_id=1, source_target_pairs={{56,0},{0,8},{8,16},{16,24},{24,32},{32,40},{40,48},{48,56},{120,6... | collective-permute-start | bytes 786440 | tf_op jit(solution)/shard_map/ppermute | solution.py:31
  110.4 1.2 collective-permute-start.33
  111.6 5.0 %collective-permute-done.19.refs_3_ = bf16[128,512]{1,0:T(8,128)(2,1)S(1)} collective-permute-done((bf16[128,512]{1,0:T(8,128)(2,1)S(1)}, bf16[128,512]{1,0:T(8,128)(2,1)S(1)}, u32[]{:S(2)}, u32[]{:S(2)}) %collective-permute-start.19) | collective-permute-done | bytes 131104 | tf_op jit(solution)/shard_map/ppermute | solution.py:36
  116.6 0.7 collective-permute-done.33.refs_4_
  117.3 0.2 last_hop.1
  117.6 1.6 %collective-permute-start.35 = (bf16[128,512]{1,0:T(8,128)(2,1)S(1)}, bf16[128,512]{1,0:T(8,128)(2,1)S(1)}, u32[]{:S(2)}, u32[]{:S(2)}) collective-permute-start(bf16[128,512]{1,0:T(8,128)(2,1)S(1)} %get-tuple-element.125), channel_id=1, source_target_pairs={{128,0},{136,8},{144,16},{152,24},{160,32},{168,40},{176,48},{184,... | collective-permute-start | bytes 393224 | tf_op jit(solution)/shard_map/ppermute | solution.py:26
  119.2 0.4 collective-permute-start.36
  119.6 2.9 %collective-permute-done.34.refs_5_ = bf16[128,512]{1,0:T(8,128)(2,1)S(1)} collective-permute-done((bf16[128,512]{1,0:T(8,128)(2,1)S(1)}, bf16[128,512]{1,0:T(8,128)(2,1)S(1)}, u32[]{:S(2)}, u32[]{:S(2)}) %collective-permute-start.34) | collective-permute-done | bytes 131104 | tf_op jit(solution)/shard_map/ppermute | solution.py:26
  122.6 1.6 %collective-permute-done.35.refs_6_ = bf16[128,512]{1,0:T(8,128)(2,1)S(1)} collective-permute-done((bf16[128,512]{1,0:T(8,128)(2,1)S(1)}, bf16[128,512]{1,0:T(8,128)(2,1)S(1)}, u32[]{:S(2)}, u32[]{:S(2)}) %collective-permute-start.35) | collective-permute-done | bytes 131104 | tf_op jit(solution)/shard_map/ppermute | solution.py:26
  124.2 1.4 %collective-permute-done.36.refs_7_ = bf16[128,512]{1,0:T(8,128)(2,1)S(1)} collective-permute-done((bf16[128,512]{1,0:T(8,128)(2,1)S(1)}, bf16[128,512]{1,0:T(8,128)(2,1)S(1)}, u32[]{:S(2)}, u32[]{:S(2)}) %collective-permute-start.36) | collective-permute-done | bytes 131104 | tf_op jit(solution)/shard_map/ppermute | solution.py:26
  125.6 0.8 final.1
  (40 shorter events, 0.6 us)
Async XLA Ops:
  0.0 21.8 %copy-start = (f32[1,32]{1,0:T(1,128)S(1)}, f32[1,32]{1,0:T(1,128)}, u32[]{:S(2)}) copy-start(f32[1,32]{1,0:T(1,128)} %nw.1) | copy-start | bytes 388
  1.0 7.8 %collective-permute-start = (bf16[128,512]{1,0:T(8,128)(2,1)S(1)}, bf16[128,512]{1,0:T(8,128)(2,1)S(1)}, u32[]{:S(2)}, u32[]{:S(2)}) collective-permute-start(bf16[128,512]{1,0:T(8,128)(2,1)S(1)} %convert_element_type.3), channel_id=1, source_target_pairs={{64,0},{72,8},{80,16},{88,24},{96,32},{104,40},{112,48},{120,56},{... | collective-permute-start | bytes 393224 | tf_op jit(solution)/shard_map/ppermute | solution.py:26
  1.8 7.0 %collective-permute-start.2 = (bf16[128,512]{1,0:T(8,128)(2,1)S(1)}, bf16[128,512]{1,0:T(8,128)(2,1)S(1)}, u32[]{:S(2)}, u32[]{:S(2)}) collective-permute-start(bf16[128,512]{1,0:T(8,128)(2,1)S(1)} %convert_element_type.3), channel_id=1, source_target_pairs={{192,0},{200,8},{208,16},{216,24},{224,32},{232,40},{240,48},{248,... | collective-permute-start | bytes 393224 | tf_op jit(solution)/shard_map/ppermute | solution.py:26
  4.3 10.3 %collective-permute-start.4 = (bf16[128,512]{1,0:T(8,128)(2,1)S(1)}, bf16[128,512]{1,0:T(8,128)(2,1)S(1)}, u32[]{:S(2)}, u32[]{:S(2)}) collective-permute-start(bf16[128,512]{1,0:T(8,128)(2,1)S(1)} %convert_element_type.3), channel_id=1, source_target_pairs={{2,0},{3,1},{4,2},{5,3},{6,4},{7,5},{0,6},{1,7},{10,8},{11,9},{12,... | collective-permute-start | bytes 393224 | tf_op jit(solution)/shard_map/ppermute | solution.py:36
  7.1 7.6 %collective-permute-start.5 = (bf16[128,512]{1,0:T(8,128)(2,1)S(1)}, bf16[128,512]{1,0:T(8,128)(2,1)S(1)}, u32[]{:S(2)}, u32[]{:S(2)}) collective-permute-start(bf16[128,512]{1,0:T(8,128)(2,1)S(1)} %convert_element_type.3), channel_id=1, source_target_pairs={{4,0},{5,1},{6,2},{7,3},{0,4},{1,5},{2,6},{3,7},{12,8},{13,9},{14,... | collective-permute-start | bytes 393224 | tf_op jit(solution)/shard_map/ppermute | solution.py:36
  7.9 7.9 %collective-permute-start.6 = (bf16[128,512]{1,0:T(8,128)(2,1)S(1)}, bf16[128,512]{1,0:T(8,128)(2,1)S(1)}, u32[]{:S(2)}, u32[]{:S(2)}) collective-permute-start(bf16[128,512]{1,0:T(8,128)(2,1)S(1)} %convert_element_type.3), channel_id=1, source_target_pairs={{6,0},{7,1},{0,2},{1,3},{2,4},{3,5},{4,6},{5,7},{14,8},{15,9},{8,1... | collective-permute-start | bytes 393224 | tf_op jit(solution)/shard_map/ppermute | solution.py:36
  8.8 5.8 %collective-permute-start.1 = (bf16[64,512]{1,0:T(8,128)(2,1)S(1)}, bf16[64,512]{1,0:T(8,128)(2,1)S(1)}, u32[]{:S(2)}, u32[]{:S(2)}) collective-permute-start(bf16[64,512]{1,0:T(8,128)(2,1)S(1)} %slice.16), channel_id=1, source_target_pairs={{64,0},{72,8},{80,16},{88,24},{96,32},{104,40},{112,48},{120,56},{... | collective-permute-start | bytes 196616 | tf_op jit(solution)/shard_map/ppermute | solution.py:26
  8.9 5.7 %collective-permute-start.3 = (bf16[64,512]{1,0:T(8,128)(2,1)S(1)}, bf16[64,512]{1,0:T(8,128)(2,1)S(1)}, u32[]{:S(2)}, u32[]{:S(2)}) collective-permute-start(bf16[64,512]{1,0:T(8,128)(2,1)S(1)} %slice.17), channel_id=1, source_target_pairs={{192,0},{200,8},{208,16},{216,24},{224,32},{232,40},{240,48},{248,... | collective-permute-start | bytes 196616 | tf_op jit(solution)/shard_map/ppermute | solution.py:26
  15.9 16.5 %collective-permute-start.8 = (bf16[4,128,512]{2,1,0:T(8,128)(2,1)S(1)}, bf16[4,128,512]{2,1,0:T(8,128)(2,1)S(1)}, u32[]{:S(2)}, u32[]{:S(2)}) collective-permute-start(bf16[4,128,512]{2,1,0:T(8,128)(2,1)S(1)} %get-tuple-element.71.refs_0_), channel_id=1, source_target_pairs={{8,0},{16,8},{24,16},{32,24},{40,32},{48,40},{56,48},{0,56},{72,64... | collective-permute-start | bytes 1572872 | tf_op jit(solution)/shard_map/ppermute | solution.py:31
  21.8 13.9 %collective-permute-start.9 = (bf16[4,128,512]{2,1,0:T(8,128)(2,1)S(1)}, bf16[4,128,512]{2,1,0:T(8,128)(2,1)S(1)}, u32[]{:S(2)}, u32[]{:S(2)}) collective-permute-start(bf16[4,128,512]{2,1,0:T(8,128)(2,1)S(1)} %get-tuple-element.71.refs_0_), channel_id=1, source_target_pairs={{56,0},{0,8},{8,16},{16,24},{24,32},{32,40},{40,48},{48,56},{120,6... | collective-permute-start | bytes 1572872 | tf_op jit(solution)/shard_map/ppermute | solution.py:31
  27.4 10.4 %collective-permute-start.7 = (bf16[4,128,512]{2,1,0:T(8,128)(2,1)S(1)}, bf16[4,128,512]{2,1,0:T(8,128)(2,1)S(1)}, u32[]{:S(2)}, u32[]{:S(2)}) collective-permute-start(bf16[4,128,512]{2,1,0:T(8,128)(2,1)S(1)} %get-tuple-element.69), channel_id=1, source_target_pairs={{1,0},{0,1},{3,2},{2,3},{5,4},{4,5},{7,6},{6,7},{9,8},{8,9},{11,10... | collective-permute-start | bytes 1572872 | tf_op jit(solution)/shard_map/ppermute | solution.py:41
  35.8 11.9 %collective-permute-start.10 = (bf16[4,128,512]{2,1,0:T(8,128)(2,1)S(1)}, bf16[4,128,512]{2,1,0:T(8,128)(2,1)S(1)}, u32[]{:S(2)}, u32[]{:S(2)}) collective-permute-start(bf16[4,128,512]{2,1,0:T(8,128)(2,1)S(1)} %collective-permute-done.8.refs_0_), channel_id=1, source_target_pairs={{8,0},{16,8},{24,16},{32,24},{40,32},{48,40},{56,48},{0,56},{72,64... | collective-permute-start | bytes 1572872 | tf_op jit(solution)/shard_map/ppermute | solution.py:31
  36.1 13.0 %collective-permute-start.11 = (bf16[4,128,512]{2,1,0:T(8,128)(2,1)S(1)}, bf16[4,128,512]{2,1,0:T(8,128)(2,1)S(1)}, u32[]{:S(2)}, u32[]{:S(2)}) collective-permute-start(bf16[4,128,512]{2,1,0:T(8,128)(2,1)S(1)} %collective-permute-done.9.refs_1_), channel_id=1, source_target_pairs={{56,0},{0,8},{8,16},{16,24},{24,32},{32,40},{40,48},{48,56},{120,6... | collective-permute-start | bytes 1572872 | tf_op jit(solution)/shard_map/ppermute | solution.py:31
  49.1 10.9 %collective-permute-start.12 = (bf16[4,128,512]{2,1,0:T(8,128)(2,1)S(1)}, bf16[4,128,512]{2,1,0:T(8,128)(2,1)S(1)}, u32[]{:S(2)}, u32[]{:S(2)}) collective-permute-start(bf16[4,128,512]{2,1,0:T(8,128)(2,1)S(1)} %collective-permute-done.10.refs_0_), channel_id=1, source_target_pairs={{8,0},{16,8},{24,16},{32,24},{40,32},{48,40},{56,48},{0,56},{72,64... | collective-permute-start | bytes 1572872 | tf_op jit(solution)/shard_map/ppermute | solution.py:31
  49.5 12.5 %collective-permute-start.13 = (bf16[4,128,512]{2,1,0:T(8,128)(2,1)S(1)}, bf16[4,128,512]{2,1,0:T(8,128)(2,1)S(1)}, u32[]{:S(2)}, u32[]{:S(2)}) collective-permute-start(bf16[4,128,512]{2,1,0:T(8,128)(2,1)S(1)} %collective-permute-done.11.refs_1_), channel_id=1, source_target_pairs={{56,0},{0,8},{8,16},{16,24},{24,32},{32,40},{40,48},{48,56},{120,6... | collective-permute-start | bytes 1572872 | tf_op jit(solution)/shard_map/ppermute | solution.py:31
  62.0 8.3 %collective-permute-start.14 = (bf16[2,128,512]{2,1,0:T(8,128)(2,1)S(1)}, bf16[2,128,512]{2,1,0:T(8,128)(2,1)S(1)}, u32[]{:S(2)}, u32[]{:S(2)}) collective-permute-start(bf16[2,128,512]{2,1,0:T(8,128)(2,1)S(1)} %slice.14), channel_id=1, source_target_pairs={{8,0},{16,8},{24,16},{32,24},{40,32},{48,40},{56,48},{0,56},{72,64... | collective-permute-start | bytes 786440 | tf_op jit(solution)/shard_map/ppermute | solution.py:31
  62.3 8.0 %collective-permute-start.15 = (bf16[2,128,512]{2,1,0:T(8,128)(2,1)S(1)}, bf16[2,128,512]{2,1,0:T(8,128)(2,1)S(1)}, u32[]{:S(2)}, u32[]{:S(2)}) collective-permute-start(bf16[2,128,512]{2,1,0:T(8,128)(2,1)S(1)} %slice.15), channel_id=1, source_target_pairs={{56,0},{0,8},{8,16},{16,24},{24,32},{32,40},{40,48},{48,56},{120,6... | collective-permute-start | bytes 786440 | tf_op jit(solution)/shard_map/ppermute | solution.py:31
  73.0 7.7 %collective-permute-start.20 = (bf16[2,128,512]{2,1,0:T(8,128)(2,1)S(1)}, bf16[2,128,512]{2,1,0:T(8,128)(2,1)S(1)}, u32[]{:S(2)}, u32[]{:S(2)}) collective-permute-start(bf16[2,128,512]{2,1,0:T(8,128)(2,1)S(1)} %get-tuple-element.97), channel_id=1, source_target_pairs={{56,0},{0,8},{8,16},{16,24},{24,32},{32,40},{40,48},{48,56},{120,6... | collective-permute-start | bytes 786440 | tf_op jit(solution)/shard_map/ppermute | solution.py:31
  73.2 7.4 %collective-permute-start.21 = (bf16[2,128,512]{2,1,0:T(8,128)(2,1)S(1)}, bf16[2,128,512]{2,1,0:T(8,128)(2,1)S(1)}, u32[]{:S(2)}, u32[]{:S(2)}) collective-permute-start(bf16[2,128,512]{2,1,0:T(8,128)(2,1)S(1)} %get-tuple-element.98), channel_id=1, source_target_pairs={{8,0},{16,8},{24,16},{32,24},{40,32},{48,40},{56,48},{0,56},{72,64... | collective-permute-start | bytes 786440 | tf_op jit(solution)/shard_map/ppermute | solution.py:31
  77.6 22.9 %collective-permute-start.16 = (bf16[4,128,512]{2,1,0:T(8,128)(2,1)S(1)}, bf16[4,128,512]{2,1,0:T(8,128)(2,1)S(1)}, u32[]{:S(2)}, u32[]{:S(2)}) collective-permute-start(bf16[4,128,512]{2,1,0:T(8,128)(2,1)S(1)} %get-tuple-element.86), channel_id=1, source_target_pairs={{1,0},{0,1},{3,2},{2,3},{5,4},{4,5},{7,6},{6,7},{9,8},{8,9},{11,10... | collective-permute-start | bytes 1572872 | tf_op jit(solution)/shard_map/ppermute | solution.py:41
  80.8 10.5 %collective-permute-start.27 = (bf16[4,128,256]{2,1,0:T(8,128)(2,1)S(1)}, bf16[4,128,256]{2,1,0:T(8,128)(2,1)S(1)}, u32[]{:S(2)}, u32[]{:S(2)}) collective-permute-start(bf16[4,128,256]{2,1,0:T(8,128)(2,1)S(1)} %get-tuple-element.114), channel_id=1, source_target_pairs={{56,0},{0,8},{8,16},{16,24},{24,32},{32,40},{40,48},{48,56},{120,6... | collective-permute-start | bytes 786440 | tf_op jit(solution)/shard_map/ppermute | solution.py:31
  80.9 10.4 %collective-permute-start.28 = (bf16[4,128,256]{2,1,0:T(8,128)(2,1)S(1)}, bf16[4,128,256]{2,1,0:T(8,128)(2,1)S(1)}, u32[]{:S(2)}, u32[]{:S(2)}) collective-permute-start(bf16[4,128,256]{2,1,0:T(8,128)(2,1)S(1)} %get-tuple-element.115), channel_id=1, source_target_pairs={{8,0},{16,8},{24,16},{32,24},{40,32},{48,40},{56,48},{0,56},{72,64... | collective-permute-start | bytes 786440 | tf_op jit(solution)/shard_map/ppermute | solution.py:31
  84.2 12.8 %collective-permute-start.22 = (bf16[4,128,256]{2,1,0:T(8,128)(2,1)S(1)}, bf16[4,128,256]{2,1,0:T(8,128)(2,1)S(1)}, u32[]{:S(2)}, u32[]{:S(2)}) collective-permute-start(bf16[4,128,256]{2,1,0:T(8,128)(2,1)S(1)} %get-tuple-element.103), channel_id=1, source_target_pairs={{56,0},{0,8},{8,16},{16,24},{24,32},{32,40},{40,48},{48,56},{120,6... | collective-permute-start | bytes 786440 | tf_op jit(solution)/shard_map/ppermute | solution.py:31
  84.2 12.8 %collective-permute-start.23 = (bf16[4,128,256]{2,1,0:T(8,128)(2,1)S(1)}, bf16[4,128,256]{2,1,0:T(8,128)(2,1)S(1)}, u32[]{:S(2)}, u32[]{:S(2)}) collective-permute-start(bf16[4,128,256]{2,1,0:T(8,128)(2,1)S(1)} %get-tuple-element.104), channel_id=1, source_target_pairs={{8,0},{16,8},{24,16},{32,24},{40,32},{48,40},{56,48},{0,56},{72,64... | collective-permute-start | bytes 786440 | tf_op jit(solution)/shard_map/ppermute | solution.py:31
  91.4 11.1 %collective-permute-start.29 = (bf16[4,128,256]{2,1,0:T(8,128)(2,1)S(1)}, bf16[4,128,256]{2,1,0:T(8,128)(2,1)S(1)}, u32[]{:S(2)}, u32[]{:S(2)}) collective-permute-start(bf16[4,128,256]{2,1,0:T(8,128)(2,1)S(1)} %get-tuple-element.116), channel_id=1, source_target_pairs={{56,0},{0,8},{8,16},{16,24},{24,32},{32,40},{40,48},{48,56},{120,6... | collective-permute-start | bytes 786440 | tf_op jit(solution)/shard_map/ppermute | solution.py:31
  91.7 10.8 %collective-permute-start.30 = (bf16[4,128,256]{2,1,0:T(8,128)(2,1)S(1)}, bf16[4,128,256]{2,1,0:T(8,128)(2,1)S(1)}, u32[]{:S(2)}, u32[]{:S(2)}) collective-permute-start(bf16[4,128,256]{2,1,0:T(8,128)(2,1)S(1)} %get-tuple-element.117), channel_id=1, source_target_pairs={{8,0},{16,8},{24,16},{32,24},{40,32},{48,40},{56,48},{0,56},{72,64... | collective-permute-start | bytes 786440 | tf_op jit(solution)/shard_map/ppermute | solution.py:31
  97.0 11.1 %collective-permute-start.24 = (bf16[4,128,256]{2,1,0:T(8,128)(2,1)S(1)}, bf16[4,128,256]{2,1,0:T(8,128)(2,1)S(1)}, u32[]{:S(2)}, u32[]{:S(2)}) collective-permute-start(bf16[4,128,256]{2,1,0:T(8,128)(2,1)S(1)} %get-tuple-element.105), channel_id=1, source_target_pairs={{56,0},{0,8},{8,16},{16,24},{24,32},{32,40},{40,48},{48,56},{120,6... | collective-permute-start | bytes 786440 | tf_op jit(solution)/shard_map/ppermute | solution.py:31
  97.1 11.0 %collective-permute-start.25 = (bf16[4,128,256]{2,1,0:T(8,128)(2,1)S(1)}, bf16[4,128,256]{2,1,0:T(8,128)(2,1)S(1)}, u32[]{:S(2)}, u32[]{:S(2)}) collective-permute-start(bf16[4,128,256]{2,1,0:T(8,128)(2,1)S(1)} %get-tuple-element.106), channel_id=1, source_target_pairs={{8,0},{16,8},{24,16},{32,24},{40,32},{48,40},{56,48},{0,56},{72,64... | collective-permute-start | bytes 786440 | tf_op jit(solution)/shard_map/ppermute | solution.py:31
  100.6 9.8 %collective-permute-start.17 = (bf16[128,512]{1,0:T(8,128)(2,1)S(1)}, bf16[128,512]{1,0:T(8,128)(2,1)S(1)}, u32[]{:S(2)}, u32[]{:S(2)}) collective-permute-start(bf16[128,512]{1,0:T(8,128)(2,1)S(1)} %get-tuple-element.88), channel_id=1, source_target_pairs={{6,0},{7,1},{0,2},{1,3},{2,4},{3,5},{4,6},{5,7},{14,8},{15,9},{8,1... | collective-permute-start | bytes 393224 | tf_op jit(solution)/shard_map/ppermute | solution.py:36
  102.5 9.1 %collective-permute-start.18 = (bf16[128,512]{1,0:T(8,128)(2,1)S(1)}, bf16[128,512]{1,0:T(8,128)(2,1)S(1)}, u32[]{:S(2)}, u32[]{:S(2)}) collective-permute-start(bf16[128,512]{1,0:T(8,128)(2,1)S(1)} %get-tuple-element.89), channel_id=1, source_target_pairs={{4,0},{5,1},{6,2},{7,3},{0,4},{1,5},{2,6},{3,7},{12,8},{13,9},{14,... | collective-permute-start | bytes 393224 | tf_op jit(solution)/shard_map/ppermute | solution.py:36
  102.7 13.9 %collective-permute-start.31 = (bf16[4,128,256]{2,1,0:T(8,128)(2,1)S(1)}, bf16[4,128,256]{2,1,0:T(8,128)(2,1)S(1)}, u32[]{:S(2)}, u32[]{:S(2)}) collective-permute-start(bf16[4,128,256]{2,1,0:T(8,128)(2,1)S(1)} %get-tuple-element.118), channel_id=1, source_target_pairs={{56,0},{0,8},{8,16},{16,24},{24,32},{32,40},{40,48},{48,56},{120,6... | collective-permute-start | bytes 786440 | tf_op jit(solution)/shard_map/ppermute | solution.py:31
  108.2 8.4 %collective-permute-start.32 = (bf16[4,128,256]{2,1,0:T(8,128)(2,1)S(1)}, bf16[4,128,256]{2,1,0:T(8,128)(2,1)S(1)}, u32[]{:S(2)}, u32[]{:S(2)}) collective-permute-start(bf16[4,128,256]{2,1,0:T(8,128)(2,1)S(1)} %get-tuple-element.119), channel_id=1, source_target_pairs={{8,0},{16,8},{24,16},{32,24},{40,32},{48,40},{56,48},{0,56},{72,64... | collective-permute-start | bytes 786440 | tf_op jit(solution)/shard_map/ppermute | solution.py:31
  108.3 8.3 %collective-permute-start.26 = (bf16[4,128,256]{2,1,0:T(8,128)(2,1)S(1)}, bf16[4,128,256]{2,1,0:T(8,128)(2,1)S(1)}, u32[]{:S(2)}, u32[]{:S(2)}) collective-permute-start(bf16[4,128,256]{2,1,0:T(8,128)(2,1)S(1)} %get-tuple-element.109), channel_id=1, source_target_pairs={{56,0},{0,8},{8,16},{16,24},{24,32},{32,40},{40,48},{48,56},{120,6... | collective-permute-start | bytes 786440 | tf_op jit(solution)/shard_map/ppermute | solution.py:31
  110.4 6.9 %collective-permute-start.33 = (bf16[4,128,256]{2,1,0:T(8,128)(2,1)S(1)}, bf16[4,128,256]{2,1,0:T(8,128)(2,1)S(1)}, u32[]{:S(2)}, u32[]{:S(2)}) collective-permute-start(bf16[4,128,256]{2,1,0:T(8,128)(2,1)S(1)} %get-tuple-element.121), channel_id=1, source_target_pairs={{8,0},{16,8},{24,16},{32,24},{40,32},{48,40},{56,48},{0,56},{72,64... | collective-permute-start | bytes 786440 | tf_op jit(solution)/shard_map/ppermute | solution.py:31
  111.6 5.0 %collective-permute-start.19 = (bf16[128,512]{1,0:T(8,128)(2,1)S(1)}, bf16[128,512]{1,0:T(8,128)(2,1)S(1)}, u32[]{:S(2)}, u32[]{:S(2)}) collective-permute-start(bf16[128,512]{1,0:T(8,128)(2,1)S(1)} %get-tuple-element.90), channel_id=1, source_target_pairs={{2,0},{3,1},{4,2},{5,3},{6,4},{7,5},{0,6},{1,7},{10,8},{11,9},{12,... | collective-permute-start | bytes 393224 | tf_op jit(solution)/shard_map/ppermute | solution.py:36
  117.5 5.0 %collective-permute-start.34 = (bf16[128,512]{1,0:T(8,128)(2,1)S(1)}, bf16[128,512]{1,0:T(8,128)(2,1)S(1)}, u32[]{:S(2)}, u32[]{:S(2)}) collective-permute-start(bf16[128,512]{1,0:T(8,128)(2,1)S(1)} %get-tuple-element.124), channel_id=1, source_target_pairs={{192,0},{200,8},{208,16},{216,24},{224,32},{232,40},{240,48},{248,... | collective-permute-start | bytes 393224 | tf_op jit(solution)/shard_map/ppermute | solution.py:26
  117.6 6.6 %collective-permute-start.35 = (bf16[128,512]{1,0:T(8,128)(2,1)S(1)}, bf16[128,512]{1,0:T(8,128)(2,1)S(1)}, u32[]{:S(2)}, u32[]{:S(2)}) collective-permute-start(bf16[128,512]{1,0:T(8,128)(2,1)S(1)} %get-tuple-element.125), channel_id=1, source_target_pairs={{128,0},{136,8},{144,16},{152,24},{160,32},{168,40},{176,48},{184,... | collective-permute-start | bytes 393224 | tf_op jit(solution)/shard_map/ppermute | solution.py:26
  119.2 6.4 %collective-permute-start.36 = (bf16[128,512]{1,0:T(8,128)(2,1)S(1)}, bf16[128,512]{1,0:T(8,128)(2,1)S(1)}, u32[]{:S(2)}, u32[]{:S(2)}) collective-permute-start(bf16[128,512]{1,0:T(8,128)(2,1)S(1)} %get-tuple-element.126), channel_id=1, source_target_pairs={{64,0},{72,8},{80,16},{88,24},{96,32},{104,40},{112,48},{120,56},{... | collective-permute-start | bytes 393224 | tf_op jit(solution)/shard_map/ppermute | solution.py:26

commit v2 on v1

--- a/solution.py
+++ b/solution.py
@@ -395,7 +395,6 @@
     first = jnp.stack(stack)
     same = jnp.stack([shard] + [from_x(shard, k) for k in (1, 2, 3)])
     m, w = prep(tie(ints, first), neg_weight, edge_masks)
-    same = jnp.stack([shard] + [from_x(shard, k) for k in (1, 2, 3)])
     p = range(len(PIECES))
 
     above, below = [first], [first]
@@ -431,15 +430,15 @@
     row_own, *row_sends = row_hop(row_keep, from_core(row_send))
     up, down = first_hop(up_in, down_in, g3, g5)
     up_in, down_in = arrive(up, down)
+    up_in[1], down_in[1] = tie((up_in[1], down_in[1]), row_own)
     up, down = hops(hop_kernel, up_in, down_in, g2, g6)
-    up_in, down_in = arrive(up, down)
-    up_in[0], down_in[0] = tie((up_in[0], down_in[0]), row_own)
-    up, down = hops(hop_kernel, up_in, down_in, g1, g7)
     up_in, down_in = arrive(up, down)
     row_parts = [row_own] + [from_x(row_sends[k - 1], -k) for k in (1, 2, 3)]
     up_in[1], down_in[1] = tie((up_in[1], down_in[1]), *row_parts)
+    up, down = hops(hop_kernel, up_in, down_in, g1, g7)
+    up_in, down_in = arrive(up, down)
     own, *sends = last_hop(g0, up_in, down_in)
-    return final(*row_parts, own, *[from_y(sends[k - 1], -k) for k in (1, 2, 3)])
+    return final(*row_parts, own, *[from_y(sends[k - 1], -k) for k in (2, 1, 3)])
 
 
 def solution(mesh):

time: 127 us -> 128 us (level)
  starting transfers between devices: 46.2 us -> 49.8 us
  waiting for transfers between devices: 43 us -> 40.2 us
    ppermute x22, waiting for transfers between devices: 30.9 us -> 28.5 us  [from_z(): return lax.ppermute(x, 'row', perm)]
    ppermute x6, starting transfers between devices: 4.53 us -> 6.39 us  [from_x(): return lax.ppermute(x, 'col', perm)]
    ppermute x22, starting transfers between devices: 32.7 us -> 34.3 us  [from_z(): return lax.ppermute(x, 'row', perm)]
  transfers between devices with their start and end apart: 37 -> 37, of which waited for: 16 -> 17; matrix products, arithmetic and copies ran while one was open for 2% -> 1% of each run, Pallas kernels for 23% -> 23%
where the time goes in v2:
time: 128 us; the launch traced here: 127 us
  starting transfers between devices  49.8 us (39%)
  waiting for transfers between devices  40.2 us (31%)
  Pallas kernels  33.3 us (26%)
  other arithmetic  2.17 us (2%)
    ppermute x22, starting transfers between devices, from_z(): return lax.ppermute(x, 'row', perm)  34.3 us
    ppermute x22, waiting for transfers between devices, from_z(): return lax.ppermute(x, 'row', perm)  28.5 us
    pallas_call x4, Pallas kernels, chunk(): pl.pallas_call(functools.partial(chunk_kernel, ds, first), out_shape=[jax...  21.8 us
    ppermute x7, starting transfers between devices, from_y(): return lax.ppermute(x, 'row', perm)  8.96 us
    ppermute x6, starting transfers between devices, from_x(): return lax.ppermute(x, 'col', perm)  6.39 us
    ppermute x7, waiting for transfers between devices, from_y(): return lax.ppermute(x, 'row', perm)  6.18 us
    pallas_call x1, Pallas kernels, prep(): pl.pallas_call(prep_kernel, out_shape=(jax.ShapeDtypeStruct((NZ, NX * NC...  5.69 us
    ppermute x6, waiting for transfers between devices, from_x(): return lax.ppermute(x, 'col', perm)  5.53 us
  transfers between devices with their start and end apart: 37, of which 17 were waited for; matrix products, arithmetic and copies ran while one was open for 1% of the time, Pallas kernels for 23%

profile of v2, /device:TPU:24, one launch (start us, length us, event | category | flops | bytes accessed | tf_op | source)
XLA Modules:
  0.0 127.3 jit_solution(9356796066706860179)
XLA Ops:
  0.0 1.0 convert_element_type.3
  1.0 0.8 collective-permute-start
  1.8 2.5 %collective-permute-start.2 = (bf16[128,512]{1,0:T(8,128)(2,1)S(1)}, bf16[128,512]{1,0:T(8,128)(2,1)S(1)}, u32[]{:S(2)}, u32[]{:S(2)}) collective-permute-start(bf16[128,512]{1,0:T(8,128)(2,1)S(1)} %convert_element_type.3), channel_id=1, source_target_pairs={{192,0},{200,8},{208,16},{216,24},{224,32},{232,40},{240,48},{248,... | collective-permute-start | bytes 393224 | tf_op jit(solution)/shard_map/ppermute | solution.py:26
  4.3 2.8 %collective-permute-start.4 = (bf16[128,512]{1,0:T(8,128)(2,1)S(1)}, bf16[128,512]{1,0:T(8,128)(2,1)S(1)}, u32[]{:S(2)}, u32[]{:S(2)}) collective-permute-start(bf16[128,512]{1,0:T(8,128)(2,1)S(1)} %convert_element_type.3), channel_id=1, source_target_pairs={{2,0},{3,1},{4,2},{5,3},{6,4},{7,5},{0,6},{1,7},{10,8},{11,9},{12,... | collective-permute-start | bytes 393224 | tf_op jit(solution)/shard_map/ppermute | solution.py:36
  7.1 0.8 collective-permute-start.5
  7.9 0.9 collective-permute-start.6
  8.9 3.3 %collective-permute-start.3 = (bf16[64,512]{1,0:T(8,128)(2,1)S(1)}, bf16[64,512]{1,0:T(8,128)(2,1)S(1)}, u32[]{:S(2)}, u32[]{:S(2)}) collective-permute-start(bf16[64,512]{1,0:T(8,128)(2,1)S(1)} %slice.17), channel_id=1, source_target_pairs={{192,0},{200,8},{208,16},{216,24},{224,32},{232,40},{240,48},{248,... | collective-permute-start | bytes 196616 | tf_op jit(solution)/shard_map/ppermute | solution.py:26
  12.2 1.0 convert_bitcast_fusion
  13.8 0.8 concatenate.10.ints
  14.6 1.1 collective-permute-done.6
  15.8 0.1 fusion.3
  15.9 5.9 %collective-permute-start.8 = (bf16[4,128,512]{2,1,0:T(8,128)(2,1)S(1)}, bf16[4,128,512]{2,1,0:T(8,128)(2,1)S(1)}, u32[]{:S(2)}, u32[]{:S(2)}) collective-permute-start(bf16[4,128,512]{2,1,0:T(8,128)(2,1)S(1)} %get-tuple-element.71.refs_0_), channel_id=1, source_target_pairs={{8,0},{16,8},{24,16},{32,24},{40,32},{48,40},{56,48},{0,56},{72,64... | collective-permute-start | bytes 1572872 | tf_op jit(solution)/shard_map/ppermute | solution.py:31
  21.8 5.7 %prep.1 = (bf16[8,1024,512]{2,1,0:T(8,128)(2,1)S(1)}, f32[8,32]{1,0:T(8,128)S(1)}) custom-call(s32[325]{0:T(512)S(1)} %concatenate.10.ints, f32[1,32]{1,0:T(1,128)S(1)} %copy-done, s32[1,128,128,128]{3,2,1,0:T(8,128)} %masks.1), custom_call_target="tpu_custom_call" | custom-call | bytes 16777216 | tf_op jit(solution)/shard_map/prep/pallas_call | solution.py:100
  27.5 0.1 collective-permute-start.7
  27.6 4.7 %collective-permute-done.8.refs_0_ = bf16[4,128,512]{2,1,0:T(8,128)(2,1)S(1)} collective-permute-done((bf16[4,128,512]{2,1,0:T(8,128)(2,1)S(1)}, bf16[4,128,512]{2,1,0:T(8,128)(2,1)S(1)}, u32[]{:S(2)}, u32[]{:S(2)}) %collective-permute-start.8) | collective-permute-done | bytes 524320 | tf_op jit(solution)/shard_map/ppermute | solution.py:31
  32.4 3.4 %collective-permute-done.9.refs_1_ = bf16[4,128,512]{2,1,0:T(8,128)(2,1)S(1)} collective-permute-done((bf16[4,128,512]{2,1,0:T(8,128)(2,1)S(1)}, bf16[4,128,512]{2,1,0:T(8,128)(2,1)S(1)}, u32[]{:S(2)}, u32[]{:S(2)}) %collective-permute-start.9) | collective-permute-done | bytes 524320 | tf_op jit(solution)/shard_map/ppermute | solution.py:31
  35.8 0.3 collective-permute-start.10
  36.1 1.7 %collective-permute-start.11 = (bf16[4,128,512]{2,1,0:T(8,128)(2,1)S(1)}, bf16[4,128,512]{2,1,0:T(8,128)(2,1)S(1)}, u32[]{:S(2)}, u32[]{:S(2)}) collective-permute-start(bf16[4,128,512]{2,1,0:T(8,128)(2,1)S(1)} %collective-permute-done.9.refs_1_), channel_id=1, source_target_pairs={{56,0},{0,8},{8,16},{16,24},{24,32},{32,40},{40,48},{48,56},{120,6... | collective-permute-start | bytes 1572872 | tf_op jit(solution)/shard_map/ppermute | solution.py:31
  37.8 0.1 pad_maximum_fusion.r_ref
  37.9 0.2 row_sums.1
  38.1 3.4 %chunk.4 = (f32[2,512,512]{2,1,0:T(8,128)S(1)}, bf16[4,128,256]{2,1,0:T(8,128)(2,1)S(1)}, bf16[4,128,256]{2,1,0:T(8,128)(2,1)S(1)}) custom-call(f32[8,32]{1,0:T(8,128)S(1)} %get-tuple-element.74.w_ref, bf16[2,512,512]{2,1,0:T(8,128)(2,1)S(1)} %pad_maximum_fusion.r_ref, f32[2,8,512]{2,1,0:T(8,128)S(1)} %row_sums.1, ...), custom_call_target="tpu_custom_call" | custom-call | flops 1610612736 | bytes 8388608 | tf_op jit(solution)/shard_map/chunk/pallas_call | solution.py:199
  41.5 6.1 %chunk.5 = (f32[2,512,512]{2,1,0:T(8,128)S(1)}, bf16[4,128,256]{2,1,0:T(8,128)(2,1)S(1)}, bf16[4,128,256]{2,1,0:T(8,128)(2,1)S(1)}, bf16[4,128,256]{2,1,0:T(8,128)(2,1)S(1)}, bf16[4,128,256]{2,1,0:T(8,128)(2,1)S(1)}) custom-call(f32[8,32]{1,0:T(8,128)S(1)} %get-tuple-element.74.w_ref, ...), custom_call_target="tpu_custom_call", output_to_operand_aliasing={{0}: (6, {})} | custom-call | flops 3221225472 | bytes 10485760 | tf_op jit(solution)/shard_map/chunk/pallas_call | solution.py:199
  47.7 1.4 %collective-permute-done.11.refs_1_ = bf16[4,128,512]{2,1,0:T(8,128)(2,1)S(1)} collective-permute-done((bf16[4,128,512]{2,1,0:T(8,128)(2,1)S(1)}, bf16[4,128,512]{2,1,0:T(8,128)(2,1)S(1)}, u32[]{:S(2)}, u32[]{:S(2)}) %collective-permute-start.11) | collective-permute-done | bytes 524320 | tf_op jit(solution)/shard_map/ppermute | solution.py:31
  49.1 0.4 collective-permute-start.12
  49.5 1.7 %collective-permute-start.13 = (bf16[4,128,512]{2,1,0:T(8,128)(2,1)S(1)}, bf16[4,128,512]{2,1,0:T(8,128)(2,1)S(1)}, u32[]{:S(2)}, u32[]{:S(2)}) collective-permute-start(bf16[4,128,512]{2,1,0:T(8,128)(2,1)S(1)} %collective-permute-done.11.refs_1_), channel_id=1, source_target_pairs={{56,0},{0,8},{8,16},{16,24},{24,32},{32,40},{40,48},{48,56},{120,6... | collective-permute-start | bytes 1572872 | tf_op jit(solution)/shard_map/ppermute | solution.py:31
  51.1 6.1 %chunk.6 = (f32[2,512,512]{2,1,0:T(8,128)S(1)}, bf16[4,128,256]{2,1,0:T(8,128)(2,1)S(1)}, bf16[4,128,256]{2,1,0:T(8,128)(2,1)S(1)}, bf16[4,128,256]{2,1,0:T(8,128)(2,1)S(1)}, bf16[4,128,256]{2,1,0:T(8,128)(2,1)S(1)}) custom-call(f32[8,32]{1,0:T(8,128)S(1)} %get-tuple-element.74.w_ref, ...), custom_call_target="tpu_custom_call", output_to_operand_aliasing={{0}: (6, {})} | custom-call | flops 3221225472 | bytes 10485760 | tf_op jit(solution)/shard_map/chunk/pallas_call | solution.py:199
  57.2 2.7 %collective-permute-done.12.refs_0_ = bf16[4,128,512]{2,1,0:T(8,128)(2,1)S(1)} collective-permute-done((bf16[4,128,512]{2,1,0:T(8,128)(2,1)S(1)}, bf16[4,128,512]{2,1,0:T(8,128)(2,1)S(1)}, u32[]{:S(2)}, u32[]{:S(2)}) %collective-permute-start.12) | collective-permute-done | bytes 524320 | tf_op jit(solution)/shard_map/ppermute | solution.py:31
  60.0 1.9 %collective-permute-done.13.refs_1_ = bf16[4,128,512]{2,1,0:T(8,128)(2,1)S(1)} collective-permute-done((bf16[4,128,512]{2,1,0:T(8,128)(2,1)S(1)}, bf16[4,128,512]{2,1,0:T(8,128)(2,1)S(1)}, u32[]{:S(2)}, u32[]{:S(2)}) %collective-permute-start.13) | collective-permute-done | bytes 524320 | tf_op jit(solution)/shard_map/ppermute | solution.py:31
  62.0 0.4 collective-permute-start.14
  62.3 1.8 %collective-permute-start.15 = (bf16[2,128,512]{2,1,0:T(8,128)(2,1)S(1)}, bf16[2,128,512]{2,1,0:T(8,128)(2,1)S(1)}, u32[]{:S(2)}, u32[]{:S(2)}) collective-permute-start(bf16[2,128,512]{2,1,0:T(8,128)(2,1)S(1)} %slice.15), channel_id=1, source_target_pairs={{56,0},{0,8},{8,16},{16,24},{24,32},{32,40},{40,48},{48,56},{120,6... | collective-permute-start | bytes 786440 | tf_op jit(solution)/shard_map/ppermute | solution.py:31
  64.2 6.1 %chunk.7 = (f32[2,512,512]{2,1,0:T(8,128)S(1)}, bf16[4,128,256]{2,1,0:T(8,128)(2,1)S(1)}, bf16[4,128,256]{2,1,0:T(8,128)(2,1)S(1)}, bf16[4,128,256]{2,1,0:T(8,128)(2,1)S(1)}, bf16[4,128,256]{2,1,0:T(8,128)(2,1)S(1)}) custom-call(f32[8,32]{1,0:T(8,128)S(1)} %get-tuple-element.74.w_ref, ...), custom_call_target="tpu_custom_call", output_to_operand_aliasing={{0}: (6, {})} | custom-call | flops 3221225472 | bytes 10485760 | tf_op jit(solution)/shard_map/chunk/pallas_call | solution.py:199
  70.4 2.6 %far_cols.1 = (bf16[2,128,512]{2,1,0:T(8,128)(2,1)S(1)}, bf16[2,128,512]{2,1,0:T(8,128)(2,1)S(1)}, bf16[2,512,512]{2,1,0:T(8,128)(2,1)S(1)}) custom-call(f32[8,32]{1,0:T(8,128)S(1)} %get-tuple-element.74.w_ref, bf16[2,512,512]{2,1,0:T(8,128)(2,1)S(1)} %pad_maximum_fusion.r_ref, f32[2,8,512]{2,1,0:T(8,128)S(1)} %row_sums.1, ...), custom_call_target="tpu_custom_call" | custom-call | flops 1073741824 | bytes 4194304 | tf_op jit(solution)/shard_map/far_cols/pallas_call | solution.py:236
  73.0 0.3 collective-permute-start.20
  73.2 3.0 %collective-permute-start.21 = (bf16[2,128,512]{2,1,0:T(8,128)(2,1)S(1)}, bf16[2,128,512]{2,1,0:T(8,128)(2,1)S(1)}, u32[]{:S(2)}, u32[]{:S(2)}) collective-permute-start(bf16[2,128,512]{2,1,0:T(8,128)(2,1)S(1)} %get-tuple-element.98), channel_id=1, source_target_pairs={{8,0},{16,8},{24,16},{32,24},{40,32},{48,40},{56,48},{0,56},{72,64... | collective-permute-start | bytes 786440 | tf_op jit(solution)/shard_map/ppermute | solution.py:31
  76.3 1.3 %far_rows.1 = (f32[4,128,512]{2,1,0:T(8,128)S(1)}, bf16[4,128,512]{2,1,0:T(8,128)(2,1)S(1)}) custom-call(f32[8,32]{1,0:T(8,128)S(1)} %get-tuple-element.74.w_ref, bf16[2,512,512]{2,1,0:T(8,128)(2,1)S(1)} %get-tuple-element.84.coef_ref, bf16[4,128,512]{2,1,0:T(8,128)(2,1)S(1)} %constant_dynamic-update-slice_fusion.k_ref, ...), custom_call_target="tpu_custom_call" | custom-call | flops 536870912 | bytes 8388608 | tf_op jit(solution)/shard_map/far_rows/pallas_call | solution.py:264
  77.6 0.1 collective-permute-start.16
  77.7 2.9 %collective-permute-done.20.up_in = bf16[2,128,512]{2,1,0:T(8,128)(2,1)S(1)} collective-permute-done((bf16[2,128,512]{2,1,0:T(8,128)(2,1)S(1)}, bf16[2,128,512]{2,1,0:T(8,128)(2,1)S(1)}, u32[]{:S(2)}, u32[]{:S(2)}) %collective-permute-start.20) | collective-permute-done | bytes 262176 | tf_op jit(solution)/shard_map/ppermute | solution.py:31
  80.6 0.1 first_hop.1
  80.9 3.3 %collective-permute-start.23 = (bf16[4,128,256]{2,1,0:T(8,128)(2,1)S(1)}, bf16[4,128,256]{2,1,0:T(8,128)(2,1)S(1)}, u32[]{:S(2)}, u32[]{:S(2)}) collective-permute-start(bf16[4,128,256]{2,1,0:T(8,128)(2,1)S(1)} %get-tuple-element.104), channel_id=1, source_target_pairs={{8,0},{16,8},{24,16},{32,24},{40,32},{48,40},{56,48},{0,56},{72,64... | collective-permute-start | bytes 786440 | tf_op jit(solution)/shard_map/ppermute | solution.py:31
  84.2 3.2 %collective-permute-start.28 = (bf16[4,128,256]{2,1,0:T(8,128)(2,1)S(1)}, bf16[4,128,256]{2,1,0:T(8,128)(2,1)S(1)}, u32[]{:S(2)}, u32[]{:S(2)}) collective-permute-start(bf16[4,128,256]{2,1,0:T(8,128)(2,1)S(1)} %get-tuple-element.113), channel_id=1, source_target_pairs={{8,0},{16,8},{24,16},{32,24},{40,32},{48,40},{56,48},{0,56},{72,64... | collective-permute-start | bytes 786440 | tf_op jit(solution)/shard_map/ppermute | solution.py:31
  87.4 3.9 %collective-permute-done.22.up_in = bf16[4,128,256]{2,1,0:T(8,128)(2,1)S(1)} collective-permute-done((bf16[4,128,256]{2,1,0:T(8,128)(2,1)S(1)}, bf16[4,128,256]{2,1,0:T(8,128)(2,1)S(1)}, u32[]{:S(2)}, u32[]{:S(2)}) %collective-permute-start.22) | collective-permute-done | bytes 262176 | tf_op jit(solution)/shard_map/ppermute | solution.py:31
  91.3 0.1 hop.4
  91.4 0.3 collective-permute-start.24
  91.7 3.4 %collective-permute-start.25 = (bf16[4,128,256]{2,1,0:T(8,128)(2,1)S(1)}, bf16[4,128,256]{2,1,0:T(8,128)(2,1)S(1)}, u32[]{:S(2)}, u32[]{:S(2)}) collective-permute-start(bf16[4,128,256]{2,1,0:T(8,128)(2,1)S(1)} %get-tuple-element.106), channel_id=1, source_target_pairs={{8,0},{16,8},{24,16},{32,24},{40,32},{48,40},{56,48},{0,56},{72,64... | collective-permute-start | bytes 786440 | tf_op jit(solution)/shard_map/ppermute | solution.py:31
  95.2 1.7 %collective-permute-done.27.up_in = bf16[4,128,256]{2,1,0:T(8,128)(2,1)S(1)} collective-permute-done((bf16[4,128,256]{2,1,0:T(8,128)(2,1)S(1)}, bf16[4,128,256]{2,1,0:T(8,128)(2,1)S(1)}, u32[]{:S(2)}, u32[]{:S(2)}) %collective-permute-start.27) | collective-permute-done | bytes 262176 | tf_op jit(solution)/shard_map/ppermute | solution.py:31
  96.9 0.1 hop.6
  97.1 3.4 %collective-permute-start.30 = (bf16[4,128,256]{2,1,0:T(8,128)(2,1)S(1)}, bf16[4,128,256]{2,1,0:T(8,128)(2,1)S(1)}, u32[]{:S(2)}, u32[]{:S(2)}) collective-permute-start(bf16[4,128,256]{2,1,0:T(8,128)(2,1)S(1)} %get-tuple-element.117), channel_id=1, source_target_pairs={{8,0},{16,8},{24,16},{32,24},{40,32},{48,40},{56,48},{0,56},{72,64... | collective-permute-start | bytes 786440 | tf_op jit(solution)/shard_map/ppermute | solution.py:31
  100.5 1.4 %collective-permute-done.24.up_in = bf16[4,128,256]{2,1,0:T(8,128)(2,1)S(1)} collective-permute-done((bf16[4,128,256]{2,1,0:T(8,128)(2,1)S(1)}, bf16[4,128,256]{2,1,0:T(8,128)(2,1)S(1)}, u32[]{:S(2)}, u32[]{:S(2)}) %collective-permute-start.24) | collective-permute-done | bytes 262176 | tf_op jit(solution)/shard_map/ppermute | solution.py:31
  102.0 1.9 %collective-permute-start.19 = (bf16[128,512]{1,0:T(8,128)(2,1)S(1)}, bf16[128,512]{1,0:T(8,128)(2,1)S(1)}, u32[]{:S(2)}, u32[]{:S(2)}) collective-permute-start(bf16[128,512]{1,0:T(8,128)(2,1)S(1)} %get-tuple-element.90), channel_id=1, source_target_pairs={{2,0},{3,1},{4,2},{5,3},{6,4},{7,5},{0,6},{1,7},{10,8},{11,9},{12,... | collective-permute-start | bytes 393224 | tf_op jit(solution)/shard_map/ppermute | solution.py:36
  103.9 0.1 hop.5
  104.0 2.7 %collective-permute-done.17.refs_1_ = bf16[128,512]{1,0:T(8,128)(2,1)S(1)} collective-permute-done((bf16[128,512]{1,0:T(8,128)(2,1)S(1)}, bf16[128,512]{1,0:T(8,128)(2,1)S(1)}, u32[]{:S(2)}, u32[]{:S(2)}) %collective-permute-start.17) | collective-permute-done | bytes 131104 | tf_op jit(solution)/shard_map/ppermute | solution.py:36
  106.7 1.7 %collective-permute-done.18.refs_2_ = bf16[128,512]{1,0:T(8,128)(2,1)S(1)} collective-permute-done((bf16[128,512]{1,0:T(8,128)(2,1)S(1)}, bf16[128,512]{1,0:T(8,128)(2,1)S(1)}, u32[]{:S(2)}, u32[]{:S(2)}) %collective-permute-start.18) | collective-permute-done | bytes 131104 | tf_op jit(solution)/shard_map/ppermute | solution.py:36
  108.4 1.7 %collective-permute-start.32 = (bf16[4,128,256]{2,1,0:T(8,128)(2,1)S(1)}, bf16[4,128,256]{2,1,0:T(8,128)(2,1)S(1)}, u32[]{:S(2)}, u32[]{:S(2)}) collective-permute-start(bf16[4,128,256]{2,1,0:T(8,128)(2,1)S(1)} %get-tuple-element.121), channel_id=1, source_target_pairs={{8,0},{16,8},{24,16},{32,24},{40,32},{48,40},{56,48},{0,56},{72,64... | collective-permute-start | bytes 786440 | tf_op jit(solution)/shard_map/ppermute | solution.py:31
  110.1 0.1 hop.7
  110.2 0.4 collective-permute-start.31
  110.6 2.9 %collective-permute-start.33 = (bf16[4,128,256]{2,1,0:T(8,128)(2,1)S(1)}, bf16[4,128,256]{2,1,0:T(8,128)(2,1)S(1)}, u32[]{:S(2)}, u32[]{:S(2)}) collective-permute-start(bf16[4,128,256]{2,1,0:T(8,128)(2,1)S(1)} %get-tuple-element.122), channel_id=1, source_target_pairs={{8,0},{16,8},{24,16},{32,24},{40,32},{48,40},{56,48},{0,56},{72,64... | collective-permute-start | bytes 786440 | tf_op jit(solution)/shard_map/ppermute | solution.py:31
  113.5 0.9 collective-permute-done.26.refs_2_
  114.4 0.4 collective-permute-done.32.refs_4_
  114.8 3.1 %collective-permute-done.31.refs_3_ = bf16[4,128,256]{2,1,0:T(8,128)(2,1)S(1)} collective-permute-done((bf16[4,128,256]{2,1,0:T(8,128)(2,1)S(1)}, bf16[4,128,256]{2,1,0:T(8,128)(2,1)S(1)}, u32[]{:S(2)}, u32[]{:S(2)}) %collective-permute-start.31) | collective-permute-done | bytes 262176 | tf_op jit(solution)/shard_map/ppermute | solution.py:31
  117.9 0.2 last_hop.1
  118.2 2.2 %collective-permute-start.35 = (bf16[128,512]{1,0:T(8,128)(2,1)S(1)}, bf16[128,512]{1,0:T(8,128)(2,1)S(1)}, u32[]{:S(2)}, u32[]{:S(2)}) collective-permute-start(bf16[128,512]{1,0:T(8,128)(2,1)S(1)} %get-tuple-element.125), channel_id=1, source_target_pairs={{192,0},{200,8},{208,16},{216,24},{224,32},{232,40},{240,48},{248,... | collective-permute-start | bytes 393224 | tf_op jit(solution)/shard_map/ppermute | solution.py:26
  120.3 4.3 %collective-permute-done.34.refs_5_ = bf16[128,512]{1,0:T(8,128)(2,1)S(1)} collective-permute-done((bf16[128,512]{1,0:T(8,128)(2,1)S(1)}, bf16[128,512]{1,0:T(8,128)(2,1)S(1)}, u32[]{:S(2)}, u32[]{:S(2)}) %collective-permute-start.34) | collective-permute-done | bytes 131104 | tf_op jit(solution)/shard_map/ppermute | solution.py:26
  124.6 1.9 %collective-permute-done.36.refs_7_ = bf16[128,512]{1,0:T(8,128)(2,1)S(1)} collective-permute-done((bf16[128,512]{1,0:T(8,128)(2,1)S(1)}, bf16[128,512]{1,0:T(8,128)(2,1)S(1)}, u32[]{:S(2)}, u32[]{:S(2)}) %collective-permute-start.36) | collective-permute-done | bytes 131104 | tf_op jit(solution)/shard_map/ppermute | solution.py:26
  126.5 0.8 final.1
  (40 shorter events, 0.7 us)
Async XLA Ops:
  0.0 21.8 %copy-start = (f32[1,32]{1,0:T(1,128)S(1)}, f32[1,32]{1,0:T(1,128)}, u32[]{:S(2)}) copy-start(f32[1,32]{1,0:T(1,128)} %nw.1) | copy-start | bytes 388
  1.0 7.8 %collective-permute-start = (bf16[128,512]{1,0:T(8,128)(2,1)S(1)}, bf16[128,512]{1,0:T(8,128)(2,1)S(1)}, u32[]{:S(2)}, u32[]{:S(2)}) collective-permute-start(bf16[128,512]{1,0:T(8,128)(2,1)S(1)} %convert_element_type.3), channel_id=1, source_target_pairs={{64,0},{72,8},{80,16},{88,24},{96,32},{104,40},{112,48},{120,56},{... | collective-permute-start | bytes 393224 | tf_op jit(solution)/shard_map/ppermute | solution.py:26
  1.8 7.0 %collective-permute-start.2 = (bf16[128,512]{1,0:T(8,128)(2,1)S(1)}, bf16[128,512]{1,0:T(8,128)(2,1)S(1)}, u32[]{:S(2)}, u32[]{:S(2)}) collective-permute-start(bf16[128,512]{1,0:T(8,128)(2,1)S(1)} %convert_element_type.3), channel_id=1, source_target_pairs={{192,0},{200,8},{208,16},{216,24},{224,32},{232,40},{240,48},{248,... | collective-permute-start | bytes 393224 | tf_op jit(solution)/shard_map/ppermute | solution.py:26
  4.3 10.3 %collective-permute-start.4 = (bf16[128,512]{1,0:T(8,128)(2,1)S(1)}, bf16[128,512]{1,0:T(8,128)(2,1)S(1)}, u32[]{:S(2)}, u32[]{:S(2)}) collective-permute-start(bf16[128,512]{1,0:T(8,128)(2,1)S(1)} %convert_element_type.3), channel_id=1, source_target_pairs={{2,0},{3,1},{4,2},{5,3},{6,4},{7,5},{0,6},{1,7},{10,8},{11,9},{12,... | collective-permute-start | bytes 393224 | tf_op jit(solution)/shard_map/ppermute | solution.py:36
  7.1 7.6 %collective-permute-start.5 = (bf16[128,512]{1,0:T(8,128)(2,1)S(1)}, bf16[128,512]{1,0:T(8,128)(2,1)S(1)}, u32[]{:S(2)}, u32[]{:S(2)}) collective-permute-start(bf16[128,512]{1,0:T(8,128)(2,1)S(1)} %convert_element_type.3), channel_id=1, source_target_pairs={{4,0},{5,1},{6,2},{7,3},{0,4},{1,5},{2,6},{3,7},{12,8},{13,9},{14,... | collective-permute-start | bytes 393224 | tf_op jit(solution)/shard_map/ppermute | solution.py:36
  7.9 7.9 %collective-permute-start.6 = (bf16[128,512]{1,0:T(8,128)(2,1)S(1)}, bf16[128,512]{1,0:T(8,128)(2,1)S(1)}, u32[]{:S(2)}, u32[]{:S(2)}) collective-permute-start(bf16[128,512]{1,0:T(8,128)(2,1)S(1)} %convert_element_type.3), channel_id=1, source_target_pairs={{6,0},{7,1},{0,2},{1,3},{2,4},{3,5},{4,6},{5,7},{14,8},{15,9},{8,1... | collective-permute-start | bytes 393224 | tf_op jit(solution)/shard_map/ppermute | solution.py:36
  8.8 5.8 %collective-permute-start.1 = (bf16[64,512]{1,0:T(8,128)(2,1)S(1)}, bf16[64,512]{1,0:T(8,128)(2,1)S(1)}, u32[]{:S(2)}, u32[]{:S(2)}) collective-permute-start(bf16[64,512]{1,0:T(8,128)(2,1)S(1)} %slice.16), channel_id=1, source_target_pairs={{64,0},{72,8},{80,16},{88,24},{96,32},{104,40},{112,48},{120,56},{... | collective-permute-start | bytes 196616 | tf_op jit(solution)/shard_map/ppermute | solution.py:26
  8.9 5.7 %collective-permute-start.3 = (bf16[64,512]{1,0:T(8,128)(2,1)S(1)}, bf16[64,512]{1,0:T(8,128)(2,1)S(1)}, u32[]{:S(2)}, u32[]{:S(2)}) collective-permute-start(bf16[64,512]{1,0:T(8,128)(2,1)S(1)} %slice.17), channel_id=1, source_target_pairs={{192,0},{200,8},{208,16},{216,24},{224,32},{232,40},{240,48},{248,... | collective-permute-start | bytes 196616 | tf_op jit(solution)/shard_map/ppermute | solution.py:26
  15.9 16.5 %collective-permute-start.8 = (bf16[4,128,512]{2,1,0:T(8,128)(2,1)S(1)}, bf16[4,128,512]{2,1,0:T(8,128)(2,1)S(1)}, u32[]{:S(2)}, u32[]{:S(2)}) collective-permute-start(bf16[4,128,512]{2,1,0:T(8,128)(2,1)S(1)} %get-tuple-element.71.refs_0_), channel_id=1, source_target_pairs={{8,0},{16,8},{24,16},{32,24},{40,32},{48,40},{56,48},{0,56},{72,64... | collective-permute-start | bytes 1572872 | tf_op jit(solution)/shard_map/ppermute | solution.py:31
  21.8 13.9 %collective-permute-start.9 = (bf16[4,128,512]{2,1,0:T(8,128)(2,1)S(1)}, bf16[4,128,512]{2,1,0:T(8,128)(2,1)S(1)}, u32[]{:S(2)}, u32[]{:S(2)}) collective-permute-start(bf16[4,128,512]{2,1,0:T(8,128)(2,1)S(1)} %get-tuple-element.71.refs_0_), channel_id=1, source_target_pairs={{56,0},{0,8},{8,16},{16,24},{24,32},{32,40},{40,48},{48,56},{120,6... | collective-permute-start | bytes 1572872 | tf_op jit(solution)/shard_map/ppermute | solution.py:31
  27.5 10.3 %collective-permute-start.7 = (bf16[4,128,512]{2,1,0:T(8,128)(2,1)S(1)}, bf16[4,128,512]{2,1,0:T(8,128)(2,1)S(1)}, u32[]{:S(2)}, u32[]{:S(2)}) collective-permute-start(bf16[4,128,512]{2,1,0:T(8,128)(2,1)S(1)} %get-tuple-element.69), channel_id=1, source_target_pairs={{1,0},{0,1},{3,2},{2,3},{5,4},{4,5},{7,6},{6,7},{9,8},{8,9},{11,10... | collective-permute-start | bytes 1572872 | tf_op jit(solution)/shard_map/ppermute | solution.py:41
  35.8 11.9 %collective-permute-start.10 = (bf16[4,128,512]{2,1,0:T(8,128)(2,1)S(1)}, bf16[4,128,512]{2,1,0:T(8,128)(2,1)S(1)}, u32[]{:S(2)}, u32[]{:S(2)}) collective-permute-start(bf16[4,128,512]{2,1,0:T(8,128)(2,1)S(1)} %collective-permute-done.8.refs_0_), channel_id=1, source_target_pairs={{8,0},{16,8},{24,16},{32,24},{40,32},{48,40},{56,48},{0,56},{72,64... | collective-permute-start | bytes 1572872 | tf_op jit(solution)/shard_map/ppermute | solution.py:31
  36.1 13.0 %collective-permute-start.11 = (bf16[4,128,512]{2,1,0:T(8,128)(2,1)S(1)}, bf16[4,128,512]{2,1,0:T(8,128)(2,1)S(1)}, u32[]{:S(2)}, u32[]{:S(2)}) collective-permute-start(bf16[4,128,512]{2,1,0:T(8,128)(2,1)S(1)} %collective-permute-done.9.refs_1_), channel_id=1, source_target_pairs={{56,0},{0,8},{8,16},{16,24},{24,32},{32,40},{40,48},{48,56},{120,6... | collective-permute-start | bytes 1572872 | tf_op jit(solution)/shard_map/ppermute | solution.py:31
  49.1 10.9 %collective-permute-start.12 = (bf16[4,128,512]{2,1,0:T(8,128)(2,1)S(1)}, bf16[4,128,512]{2,1,0:T(8,128)(2,1)S(1)}, u32[]{:S(2)}, u32[]{:S(2)}) collective-permute-start(bf16[4,128,512]{2,1,0:T(8,128)(2,1)S(1)} %collective-permute-done.10.refs_0_), channel_id=1, source_target_pairs={{8,0},{16,8},{24,16},{32,24},{40,32},{48,40},{56,48},{0,56},{72,64... | collective-permute-start | bytes 1572872 | tf_op jit(solution)/shard_map/ppermute | solution.py:31
  49.5 12.5 %collective-permute-start.13 = (bf16[4,128,512]{2,1,0:T(8,128)(2,1)S(1)}, bf16[4,128,512]{2,1,0:T(8,128)(2,1)S(1)}, u32[]{:S(2)}, u32[]{:S(2)}) collective-permute-start(bf16[4,128,512]{2,1,0:T(8,128)(2,1)S(1)} %collective-permute-done.11.refs_1_), channel_id=1, source_target_pairs={{56,0},{0,8},{8,16},{16,24},{24,32},{32,40},{40,48},{48,56},{120,6... | collective-permute-start | bytes 1572872 | tf_op jit(solution)/shard_map/ppermute | solution.py:31
  62.0 8.3 %collective-permute-start.14 = (bf16[2,128,512]{2,1,0:T(8,128)(2,1)S(1)}, bf16[2,128,512]{2,1,0:T(8,128)(2,1)S(1)}, u32[]{:S(2)}, u32[]{:S(2)}) collective-permute-start(bf16[2,128,512]{2,1,0:T(8,128)(2,1)S(1)} %slice.14), channel_id=1, source_target_pairs={{8,0},{16,8},{24,16},{32,24},{40,32},{48,40},{56,48},{0,56},{72,64... | collective-permute-start | bytes 786440 | tf_op jit(solution)/shard_map/ppermute | solution.py:31
  62.3 8.0 %collective-permute-start.15 = (bf16[2,128,512]{2,1,0:T(8,128)(2,1)S(1)}, bf16[2,128,512]{2,1,0:T(8,128)(2,1)S(1)}, u32[]{:S(2)}, u32[]{:S(2)}) collective-permute-start(bf16[2,128,512]{2,1,0:T(8,128)(2,1)S(1)} %slice.15), channel_id=1, source_target_pairs={{56,0},{0,8},{8,16},{16,24},{24,32},{32,40},{40,48},{48,56},{120,6... | collective-permute-start | bytes 786440 | tf_op jit(solution)/shard_map/ppermute | solution.py:31
  73.0 7.7 %collective-permute-start.20 = (bf16[2,128,512]{2,1,0:T(8,128)(2,1)S(1)}, bf16[2,128,512]{2,1,0:T(8,128)(2,1)S(1)}, u32[]{:S(2)}, u32[]{:S(2)}) collective-permute-start(bf16[2,128,512]{2,1,0:T(8,128)(2,1)S(1)} %get-tuple-element.97), channel_id=1, source_target_pairs={{56,0},{0,8},{8,16},{16,24},{24,32},{32,40},{40,48},{48,56},{120,6... | collective-permute-start | bytes 786440 | tf_op jit(solution)/shard_map/ppermute | solution.py:31
  73.2 7.4 %collective-permute-start.21 = (bf16[2,128,512]{2,1,0:T(8,128)(2,1)S(1)}, bf16[2,128,512]{2,1,0:T(8,128)(2,1)S(1)}, u32[]{:S(2)}, u32[]{:S(2)}) collective-permute-start(bf16[2,128,512]{2,1,0:T(8,128)(2,1)S(1)} %get-tuple-element.98), channel_id=1, source_target_pairs={{8,0},{16,8},{24,16},{32,24},{40,32},{48,40},{56,48},{0,56},{72,64... | collective-permute-start | bytes 786440 | tf_op jit(solution)/shard_map/ppermute | solution.py:31
  77.6 17.5 %collective-permute-start.16 = (bf16[4,128,512]{2,1,0:T(8,128)(2,1)S(1)}, bf16[4,128,512]{2,1,0:T(8,128)(2,1)S(1)}, u32[]{:S(2)}, u32[]{:S(2)}) collective-permute-start(bf16[4,128,512]{2,1,0:T(8,128)(2,1)S(1)} %get-tuple-element.86), channel_id=1, source_target_pairs={{1,0},{0,1},{3,2},{2,3},{5,4},{4,5},{7,6},{6,7},{9,8},{8,9},{11,10... | collective-permute-start | bytes 1572872 | tf_op jit(solution)/shard_map/ppermute | solution.py:41
  80.8 10.5 %collective-permute-start.22 = (bf16[4,128,256]{2,1,0:T(8,128)(2,1)S(1)}, bf16[4,128,256]{2,1,0:T(8,128)(2,1)S(1)}, u32[]{:S(2)}, u32[]{:S(2)}) collective-permute-start(bf16[4,128,256]{2,1,0:T(8,128)(2,1)S(1)} %get-tuple-element.103), channel_id=1, source_target_pairs={{56,0},{0,8},{8,16},{16,24},{24,32},{32,40},{40,48},{48,56},{120,6... | collective-permute-start | bytes 786440 | tf_op jit(solution)/shard_map/ppermute | solution.py:31
  80.9 10.4 %collective-permute-start.23 = (bf16[4,128,256]{2,1,0:T(8,128)(2,1)S(1)}, bf16[4,128,256]{2,1,0:T(8,128)(2,1)S(1)}, u32[]{:S(2)}, u32[]{:S(2)}) collective-permute-start(bf16[4,128,256]{2,1,0:T(8,128)(2,1)S(1)} %get-tuple-element.104), channel_id=1, source_target_pairs={{8,0},{16,8},{24,16},{32,24},{40,32},{48,40},{56,48},{0,56},{72,64... | collective-permute-start | bytes 786440 | tf_op jit(solution)/shard_map/ppermute | solution.py:31
  84.2 12.8 %collective-permute-start.27 = (bf16[4,128,256]{2,1,0:T(8,128)(2,1)S(1)}, bf16[4,128,256]{2,1,0:T(8,128)(2,1)S(1)}, u32[]{:S(2)}, u32[]{:S(2)}) collective-permute-start(bf16[4,128,256]{2,1,0:T(8,128)(2,1)S(1)} %get-tuple-element.112), channel_id=1, source_target_pairs={{56,0},{0,8},{8,16},{16,24},{24,32},{32,40},{40,48},{48,56},{120,6... | collective-permute-start | bytes 786440 | tf_op jit(solution)/shard_map/ppermute | solution.py:31
  84.2 12.8 %collective-permute-start.28 = (bf16[4,128,256]{2,1,0:T(8,128)(2,1)S(1)}, bf16[4,128,256]{2,1,0:T(8,128)(2,1)S(1)}, u32[]{:S(2)}, u32[]{:S(2)}) collective-permute-start(bf16[4,128,256]{2,1,0:T(8,128)(2,1)S(1)} %get-tuple-element.113), channel_id=1, source_target_pairs={{8,0},{16,8},{24,16},{32,24},{40,32},{48,40},{56,48},{0,56},{72,64... | collective-permute-start | bytes 786440 | tf_op jit(solution)/shard_map/ppermute | solution.py:31
  91.4 10.5 %collective-permute-start.24 = (bf16[4,128,256]{2,1,0:T(8,128)(2,1)S(1)}, bf16[4,128,256]{2,1,0:T(8,128)(2,1)S(1)}, u32[]{:S(2)}, u32[]{:S(2)}) collective-permute-start(bf16[4,128,256]{2,1,0:T(8,128)(2,1)S(1)} %get-tuple-element.105), channel_id=1, source_target_pairs={{56,0},{0,8},{8,16},{16,24},{24,32},{32,40},{40,48},{48,56},{120,6... | collective-permute-start | bytes 786440 | tf_op jit(solution)/shard_map/ppermute | solution.py:31
  91.7 10.3 %collective-permute-start.25 = (bf16[4,128,256]{2,1,0:T(8,128)(2,1)S(1)}, bf16[4,128,256]{2,1,0:T(8,128)(2,1)S(1)}, u32[]{:S(2)}, u32[]{:S(2)}) collective-permute-start(bf16[4,128,256]{2,1,0:T(8,128)(2,1)S(1)} %get-tuple-element.106), channel_id=1, source_target_pairs={{8,0},{16,8},{24,16},{32,24},{40,32},{48,40},{56,48},{0,56},{72,64... | collective-permute-start | bytes 786440 | tf_op jit(solution)/shard_map/ppermute | solution.py:31
  97.0 13.0 %collective-permute-start.29 = (bf16[4,128,256]{2,1,0:T(8,128)(2,1)S(1)}, bf16[4,128,256]{2,1,0:T(8,128)(2,1)S(1)}, u32[]{:S(2)}, u32[]{:S(2)}) collective-permute-start(bf16[4,128,256]{2,1,0:T(8,128)(2,1)S(1)} %get-tuple-element.116), channel_id=1, source_target_pairs={{56,0},{0,8},{8,16},{16,24},{24,32},{32,40},{40,48},{48,56},{120,6... | collective-permute-start | bytes 786440 | tf_op jit(solution)/shard_map/ppermute | solution.py:31
  97.1 12.9 %collective-permute-start.30 = (bf16[4,128,256]{2,1,0:T(8,128)(2,1)S(1)}, bf16[4,128,256]{2,1,0:T(8,128)(2,1)S(1)}, u32[]{:S(2)}, u32[]{:S(2)}) collective-permute-start(bf16[4,128,256]{2,1,0:T(8,128)(2,1)S(1)} %get-tuple-element.117), channel_id=1, source_target_pairs={{8,0},{16,8},{24,16},{32,24},{40,32},{48,40},{56,48},{0,56},{72,64... | collective-permute-start | bytes 786440 | tf_op jit(solution)/shard_map/ppermute | solution.py:31
  100.5 6.2 %collective-permute-start.17 = (bf16[128,512]{1,0:T(8,128)(2,1)S(1)}, bf16[128,512]{1,0:T(8,128)(2,1)S(1)}, u32[]{:S(2)}, u32[]{:S(2)}) collective-permute-start(bf16[128,512]{1,0:T(8,128)(2,1)S(1)} %get-tuple-element.88), channel_id=1, source_target_pairs={{6,0},{7,1},{0,2},{1,3},{2,4},{3,5},{4,6},{5,7},{14,8},{15,9},{8,1... | collective-permute-start | bytes 393224 | tf_op jit(solution)/shard_map/ppermute | solution.py:36
  101.9 6.5 %collective-permute-start.18 = (bf16[128,512]{1,0:T(8,128)(2,1)S(1)}, bf16[128,512]{1,0:T(8,128)(2,1)S(1)}, u32[]{:S(2)}, u32[]{:S(2)}) collective-permute-start(bf16[128,512]{1,0:T(8,128)(2,1)S(1)} %get-tuple-element.89), channel_id=1, source_target_pairs={{4,0},{5,1},{6,2},{7,3},{0,4},{1,5},{2,6},{3,7},{12,8},{13,9},{14,... | collective-permute-start | bytes 393224 | tf_op jit(solution)/shard_map/ppermute | solution.py:36
  102.0 8.1 %collective-permute-start.19 = (bf16[128,512]{1,0:T(8,128)(2,1)S(1)}, bf16[128,512]{1,0:T(8,128)(2,1)S(1)}, u32[]{:S(2)}, u32[]{:S(2)}) collective-permute-start(bf16[128,512]{1,0:T(8,128)(2,1)S(1)} %get-tuple-element.90), channel_id=1, source_target_pairs={{2,0},{3,1},{4,2},{5,3},{6,4},{7,5},{0,6},{1,7},{10,8},{11,9},{12,... | collective-permute-start | bytes 393224 | tf_op jit(solution)/shard_map/ppermute | solution.py:36
  106.7 7.7 %collective-permute-start.26 = (bf16[4,128,256]{2,1,0:T(8,128)(2,1)S(1)}, bf16[4,128,256]{2,1,0:T(8,128)(2,1)S(1)}, u32[]{:S(2)}, u32[]{:S(2)}) collective-permute-start(bf16[4,128,256]{2,1,0:T(8,128)(2,1)S(1)} %get-tuple-element.107), channel_id=1, source_target_pairs={{56,0},{0,8},{8,16},{16,24},{24,32},{32,40},{40,48},{48,56},{120,6... | collective-permute-start | bytes 786440 | tf_op jit(solution)/shard_map/ppermute | solution.py:31
  108.4 6.4 %collective-permute-start.32 = (bf16[4,128,256]{2,1,0:T(8,128)(2,1)S(1)}, bf16[4,128,256]{2,1,0:T(8,128)(2,1)S(1)}, u32[]{:S(2)}, u32[]{:S(2)}) collective-permute-start(bf16[4,128,256]{2,1,0:T(8,128)(2,1)S(1)} %get-tuple-element.121), channel_id=1, source_target_pairs={{8,0},{16,8},{24,16},{32,24},{40,32},{48,40},{56,48},{0,56},{72,64... | collective-permute-start | bytes 786440 | tf_op jit(solution)/shard_map/ppermute | solution.py:31
  110.2 7.7 %collective-permute-start.31 = (bf16[4,128,256]{2,1,0:T(8,128)(2,1)S(1)}, bf16[4,128,256]{2,1,0:T(8,128)(2,1)S(1)}, u32[]{:S(2)}, u32[]{:S(2)}) collective-permute-start(bf16[4,128,256]{2,1,0:T(8,128)(2,1)S(1)} %get-tuple-element.120), channel_id=1, source_target_pairs={{56,0},{0,8},{8,16},{16,24},{24,32},{32,40},{40,48},{48,56},{120,6... | collective-permute-start | bytes 786440 | tf_op jit(solution)/shard_map/ppermute | solution.py:31
  110.6 7.2 %collective-permute-start.33 = (bf16[4,128,256]{2,1,0:T(8,128)(2,1)S(1)}, bf16[4,128,256]{2,1,0:T(8,128)(2,1)S(1)}, u32[]{:S(2)}, u32[]{:S(2)}) collective-permute-start(bf16[4,128,256]{2,1,0:T(8,128)(2,1)S(1)} %get-tuple-element.122), channel_id=1, source_target_pairs={{8,0},{16,8},{24,16},{32,24},{40,32},{48,40},{56,48},{0,56},{72,64... | collective-permute-start | bytes 786440 | tf_op jit(solution)/shard_map/ppermute | solution.py:31
  118.1 6.6 %collective-permute-start.34 = (bf16[128,512]{1,0:T(8,128)(2,1)S(1)}, bf16[128,512]{1,0:T(8,128)(2,1)S(1)}, u32[]{:S(2)}, u32[]{:S(2)}) collective-permute-start(bf16[128,512]{1,0:T(8,128)(2,1)S(1)} %get-tuple-element.124), channel_id=1, source_target_pairs={{128,0},{136,8},{144,16},{152,24},{160,32},{168,40},{176,48},{184,... | collective-permute-start | bytes 393224 | tf_op jit(solution)/shard_map/ppermute | solution.py:26
  118.2 6.5 %collective-permute-start.35 = (bf16[128,512]{1,0:T(8,128)(2,1)S(1)}, bf16[128,512]{1,0:T(8,128)(2,1)S(1)}, u32[]{:S(2)}, u32[]{:S(2)}) collective-permute-start(bf16[128,512]{1,0:T(8,128)(2,1)S(1)} %get-tuple-element.125), channel_id=1, source_target_pairs={{192,0},{200,8},{208,16},{216,24},{224,32},{232,40},{240,48},{248,... | collective-permute-start | bytes 393224 | tf_op jit(solution)/shard_map/ppermute | solution.py:26
  120.3 6.2 %collective-permute-start.36 = (bf16[128,512]{1,0:T(8,128)(2,1)S(1)}, bf16[128,512]{1,0:T(8,128)(2,1)S(1)}, u32[]{:S(2)}, u32[]{:S(2)}) collective-permute-start(bf16[128,512]{1,0:T(8,128)(2,1)S(1)} %get-tuple-element.126), channel_id=1, source_target_pairs={{64,0},{72,8},{80,16},{88,24},{96,32},{104,40},{112,48},{120,56},{... | collective-permute-start | bytes 393224 | tf_op jit(solution)/shard_map/ppermute | solution.py:26

commit v3 on v2

--- a/solution.py
+++ b/solution.py
@@ -61,7 +61,11 @@
     def col_at(b):
         return (b % NZ - z) & (NZ - 1), (b // NZ - y) & (NY - 1)
 
-    m_ref[...] = jnp.zeros_like(m_ref)
+    def clear(k, _):
+        m_ref[k // 8, pl.ds(pl.multiple_of(k % 8 * T, T), T)] = jnp.zeros((T, NY * T), BF)
+        return 0
+
+    lax.fori_loop(0, NZ * NX * NC, clear, 0)
 
     for a in range(NX * NC):
         for b in range(NY * NZ):
@@ -314,29 +318,26 @@
     )(up, down, up_in, down_in)
 
 
-def last_hop_kernel(*refs):
-    p = len(PIECES)
-    keep, *sends = refs[3 * p :]
-    for q, (lo, hi) in enumerate(PIECES):
-        for e in range(NY):
-            s = sum(refs[k * p + q][e].astype(F32) for k in range(3))
-            if e:
-                sends[e - 1][:, lo:hi] = s.astype(BF)
-            else:
-                keep[:, lo:hi] = s
+def last_hop_kernel(own, up_in, down_in, keep, *sends):
+    for e in range(NY):
+        s = own[e].astype(F32) + up_in[e].astype(F32) + down_in[e].astype(F32)
+        if e:
+            sends[e - 1][...] = s.astype(BF)
+        else:
+            keep[...] = s
 
 
 def last_hop(own, up_in, down_in):
-    args = [*own, *up_in, *down_in]
+    shape = own.shape[1:]
     return pl.pallas_call(
         last_hop_kernel,
-        out_shape=[jax.ShapeDtypeStruct((T, C), F32)] + [jax.ShapeDtypeStruct((T, C), BF)] * (NY - 1),
-        in_specs=[VMEM] * len(args),
+        out_shape=[jax.ShapeDtypeStruct(shape, F32)] + [jax.ShapeDtypeStruct(shape, BF)] * (NY - 1),
+        in_specs=[VMEM] * 3,
         out_specs=[VMEM] * NY,
         compiler_params=PARAMS,
         cost_estimate=pl.CostEstimate(flops=1 << 20, bytes_accessed=2 << 20, transcendentals=0),
         name="last_hop",
-    )(*args)
+    )(own, up_in, down_in)
 
 
 def row_hop_kernel(keep, arrived, own, *sends):
@@ -362,10 +363,15 @@
 
 def final_kernel(*refs):
     out = refs[-1]
-    total = refs[0][...]
-    for part in refs[1:-1]:
-        total = total + part[...].astype(F32)
-    out[...] = total
+    rows = refs[0][...]
+    for part in refs[1:NX]:
+        rows = rows + part[...].astype(F32)
+    for q, (lo, hi) in enumerate(PIECES):
+        own, *sent = refs[NX + q * NY : NX + (q + 1) * NY]
+        cols = own[...]
+        for part in sent:
+            cols = cols + part[...].astype(F32)
+        out[:, lo:hi] = rows[:, lo:hi] + cols
 
 
 def final(*terms):
@@ -389,8 +395,7 @@
     ints = jnp.concatenate([tile_rows[0], tile_cols[0], neg_rows[0], neg_cols[0], pos, tile_count])
     shard = membership.astype(BF)
     next_y, last_y = from_y(shard, 1), from_y(shard, -1)
-    half = T // 2
-    far_y = jnp.concatenate([from_y(next_y[:half], 1), from_y(last_y[half:], -1)])
+    far_y = from_y(next_y, 1)
     stack = [shard, next_y, far_y, last_y]
     first = jnp.stack(stack)
     same = jnp.stack([shard] + [from_x(shard, k) for k in (1, 2, 3)])
@@ -437,8 +442,11 @@
     up_in[1], down_in[1] = tie((up_in[1], down_in[1]), *row_parts)
     up, down = hops(hop_kernel, up_in, down_in, g1, g7)
     up_in, down_in = arrive(up, down)
-    own, *sends = last_hop(g0, up_in, down_in)
-    return final(*row_parts, own, *[from_y(sends[k - 1], -k) for k in (2, 1, 3)])
+    col_parts = []
+    for q in p:
+        own, *sends = last_hop(g0[q], up_in[q], down_in[q])
+        col_parts += [own] + [from_y(sends[k - 1], -k) for k in (2, 1, 3)]
+    return final(*row_parts, *col_parts)
 
 
 def solution(mesh):

time: 128 us -> 130 us (1.016)
  starting transfers between devices: 49.8 us -> 55 us
  waiting for transfers between devices: 40.2 us -> 36.7 us
    ppermute x22, waiting for transfers between devices: 28.5 us -> 24.2 us  [from_z(): return lax.ppermute(x, 'row', perm)]
    ppermute x6, starting transfers between devices: 6.39 us -> 8.74 us  [from_x(): return lax.ppermute(x, 'col', perm)]
    ppermute x6, waiting for transfers between devices: 5.53 us -> 7.4 us  [from_x(): return lax.ppermute(x, 'col', perm)]
    ppermute x7 -> x9, starting transfers between devices: 8.96 us -> 10.7 us  [from_y(): return lax.ppermute(x, 'row', perm)]
    ppermute x7 -> x9, waiting for transfers between devices: 6.18 us -> 5.12 us  [from_y(): return lax.ppermute(x, 'row', perm)]
  transfers between devices with their start and end apart: 37 -> 39, of which waited for: 17 -> 20; matrix products, arithmetic and copies ran while one was open for 1% -> 1% of each run, Pallas kernels for 23% -> 24%
where the time goes in v3:
time: 130 us; the launch traced here: 129 us
  starting transfers between devices  55 us (42%)
  waiting for transfers between devices  36.7 us (28%)
  Pallas kernels  33.9 us (26%)
  other arithmetic  2.17 us (2%)
    ppermute x22, starting transfers between devices, from_z(): return lax.ppermute(x, 'row', perm)  35.4 us
    ppermute x22, waiting for transfers between devices, from_z(): return lax.ppermute(x, 'row', perm)  24.2 us
    pallas_call x4, Pallas kernels, chunk(): pl.pallas_call(functools.partial(chunk_kernel, ds, first), out_shape=[jax...  21.8 us
    ppermute x9, starting transfers between devices, from_y(): return lax.ppermute(x, 'row', perm)  10.7 us
    ppermute x6, starting transfers between devices, from_x(): return lax.ppermute(x, 'col', perm)  8.74 us
    ppermute x6, waiting for transfers between devices, from_x(): return lax.ppermute(x, 'col', perm)  7.4 us
    pallas_call x1, Pallas kernels, prep(): pl.pallas_call(prep_kernel, out_shape=(jax.ShapeDtypeStruct((NZ, NX * NC...  6.2 us
    ppermute x9, waiting for transfers between devices, from_y(): return lax.ppermute(x, 'row', perm)  5.12 us
  transfers between devices with their start and end apart: 39, of which 20 were waited for; matrix products, arithmetic and copies ran while one was open for 1% of the time, Pallas kernels for 24%

profile of v3, /device:TPU:24, one launch (start us, length us, event | category | flops | bytes accessed | tf_op | source)
XLA Modules:
  0.0 129.5 jit_solution(2936138942858707652)
XLA Ops:
  0.0 1.0 convert_element_type.3
  1.0 0.8 collective-permute-start
  1.8 2.5 %collective-permute-start.2 = (bf16[128,512]{1,0:T(8,128)(2,1)S(1)}, bf16[128,512]{1,0:T(8,128)(2,1)S(1)}, u32[]{:S(2)}, u32[]{:S(2)}) collective-permute-start(bf16[128,512]{1,0:T(8,128)(2,1)S(1)} %convert_element_type.3), channel_id=1, source_target_pairs={{192,0},{200,8},{208,16},{216,24},{224,32},{232,40},{240,48},{248,... | collective-permute-start | bytes 393224 | tf_op jit(solution)/shard_map/ppermute | solution.py:26
  4.3 2.8 %collective-permute-start.3 = (bf16[128,512]{1,0:T(8,128)(2,1)S(1)}, bf16[128,512]{1,0:T(8,128)(2,1)S(1)}, u32[]{:S(2)}, u32[]{:S(2)}) collective-permute-start(bf16[128,512]{1,0:T(8,128)(2,1)S(1)} %convert_element_type.3), channel_id=1, source_target_pairs={{2,0},{3,1},{4,2},{5,3},{6,4},{7,5},{0,6},{1,7},{10,8},{11,9},{12,... | collective-permute-start | bytes 393224 | tf_op jit(solution)/shard_map/ppermute | solution.py:36
  7.1 0.8 collective-permute-start.4
  7.9 0.9 collective-permute-start.5
  9.4 0.8 concatenate.7.ints
  10.3 1.0 convert_bitcast_fusion
  11.2 0.8 collective-permute-done.3
  12.1 2.3 %collective-permute-done.4 = bf16[128,512]{1,0:T(8,128)(2,1)S(1)} collective-permute-done((bf16[128,512]{1,0:T(8,128)(2,1)S(1)}, bf16[128,512]{1,0:T(8,128)(2,1)S(1)}, u32[]{:S(2)}, u32[]{:S(2)}) %collective-permute-start.4) | collective-permute-done | bytes 131104 | tf_op jit(solution)/shard_map/ppermute | solution.py:36
  14.4 1.3 %collective-permute-done.5 = bf16[128,512]{1,0:T(8,128)(2,1)S(1)} collective-permute-done((bf16[128,512]{1,0:T(8,128)(2,1)S(1)}, bf16[128,512]{1,0:T(8,128)(2,1)S(1)}, u32[]{:S(2)}, u32[]{:S(2)}) %collective-permute-start.5) | collective-permute-done | bytes 131104 | tf_op jit(solution)/shard_map/ppermute | solution.py:36
  15.8 0.7 collective-permute-done.1
  16.4 0.1 fusion.3
  16.6 5.9 %collective-permute-start.7 = (bf16[4,128,512]{2,1,0:T(8,128)(2,1)S(1)}, bf16[4,128,512]{2,1,0:T(8,128)(2,1)S(1)}, u32[]{:S(2)}, u32[]{:S(2)}) collective-permute-start(bf16[4,128,512]{2,1,0:T(8,128)(2,1)S(1)} %get-tuple-element.75.refs_0_), channel_id=1, source_target_pairs={{8,0},{16,8},{24,16},{32,24},{40,32},{48,40},{56,48},{0,56},{72,64... | collective-permute-start | bytes 1572872 | tf_op jit(solution)/shard_map/ppermute | solution.py:31
  22.5 6.2 %prep.1 = (bf16[8,1024,512]{2,1,0:T(8,128)(2,1)S(1)}, f32[8,32]{1,0:T(8,128)S(1)}) custom-call(s32[325]{0:T(512)S(1)} %concatenate.7.ints, f32[1,32]{1,0:T(1,128)S(1)} %copy-done, s32[1,128,128,128]{3,2,1,0:T(8,128)} %masks.1), custom_call_target="tpu_custom_call" | custom-call | bytes 16777216 | tf_op jit(solution)/shard_map/prep/pallas_call | solution.py:104
  28.8 3.6 %collective-permute-done.7.refs_0_ = bf16[4,128,512]{2,1,0:T(8,128)(2,1)S(1)} collective-permute-done((bf16[4,128,512]{2,1,0:T(8,128)(2,1)S(1)}, bf16[4,128,512]{2,1,0:T(8,128)(2,1)S(1)}, u32[]{:S(2)}, u32[]{:S(2)}) %collective-permute-start.7) | collective-permute-done | bytes 524320 | tf_op jit(solution)/shard_map/ppermute | solution.py:31
  32.4 3.4 %collective-permute-done.8.refs_1_ = bf16[4,128,512]{2,1,0:T(8,128)(2,1)S(1)} collective-permute-done((bf16[4,128,512]{2,1,0:T(8,128)(2,1)S(1)}, bf16[4,128,512]{2,1,0:T(8,128)(2,1)S(1)}, u32[]{:S(2)}, u32[]{:S(2)}) %collective-permute-start.8) | collective-permute-done | bytes 524320 | tf_op jit(solution)/shard_map/ppermute | solution.py:31
  35.8 3.2 %collective-permute-start.9 = (bf16[4,128,512]{2,1,0:T(8,128)(2,1)S(1)}, bf16[4,128,512]{2,1,0:T(8,128)(2,1)S(1)}, u32[]{:S(2)}, u32[]{:S(2)}) collective-permute-start(bf16[4,128,512]{2,1,0:T(8,128)(2,1)S(1)} %collective-permute-done.7.refs_0_), channel_id=1, source_target_pairs={{8,0},{16,8},{24,16},{32,24},{40,32},{48,40},{56,48},{0,56},{72,64... | collective-permute-start | bytes 1572872 | tf_op jit(solution)/shard_map/ppermute | solution.py:31
  39.0 0.1 pad_maximum_fusion.r_ref
  39.1 0.2 row_sums.1
  39.3 3.4 %chunk.4 = (f32[2,512,512]{2,1,0:T(8,128)S(1)}, bf16[4,128,256]{2,1,0:T(8,128)(2,1)S(1)}, bf16[4,128,256]{2,1,0:T(8,128)(2,1)S(1)}) custom-call(f32[8,32]{1,0:T(8,128)S(1)} %get-tuple-element.78.w_ref, bf16[2,512,512]{2,1,0:T(8,128)(2,1)S(1)} %pad_maximum_fusion.r_ref, f32[2,8,512]{2,1,0:T(8,128)S(1)} %row_sums.1, ...), custom_call_target="tpu_custom_call" | custom-call | flops 1610612736 | bytes 8388608 | tf_op jit(solution)/shard_map/chunk/pallas_call | solution.py:203
  42.8 6.1 %chunk.5 = (f32[2,512,512]{2,1,0:T(8,128)S(1)}, bf16[4,128,256]{2,1,0:T(8,128)(2,1)S(1)}, bf16[4,128,256]{2,1,0:T(8,128)(2,1)S(1)}, bf16[4,128,256]{2,1,0:T(8,128)(2,1)S(1)}, bf16[4,128,256]{2,1,0:T(8,128)(2,1)S(1)}) custom-call(f32[8,32]{1,0:T(8,128)S(1)} %get-tuple-element.78.w_ref, ...), custom_call_target="tpu_custom_call", output_to_operand_aliasing={{0}: (6, {})} | custom-call | flops 3221225472 | bytes 10485760 | tf_op jit(solution)/shard_map/chunk/pallas_call | solution.py:203
  48.9 2.2 %collective-permute-start.11 = (bf16[4,128,512]{2,1,0:T(8,128)(2,1)S(1)}, bf16[4,128,512]{2,1,0:T(8,128)(2,1)S(1)}, u32[]{:S(2)}, u32[]{:S(2)}) collective-permute-start(bf16[4,128,512]{2,1,0:T(8,128)(2,1)S(1)} %collective-permute-done.9.refs_0_), channel_id=1, source_target_pairs={{8,0},{16,8},{24,16},{32,24},{40,32},{48,40},{56,48},{0,56},{72,64... | collective-permute-start | bytes 1572872 | tf_op jit(solution)/shard_map/ppermute | solution.py:31
  51.1 6.1 %chunk.6 = (f32[2,512,512]{2,1,0:T(8,128)S(1)}, bf16[4,128,256]{2,1,0:T(8,128)(2,1)S(1)}, bf16[4,128,256]{2,1,0:T(8,128)(2,1)S(1)}, bf16[4,128,256]{2,1,0:T(8,128)(2,1)S(1)}, bf16[4,128,256]{2,1,0:T(8,128)(2,1)S(1)}) custom-call(f32[8,32]{1,0:T(8,128)S(1)} %get-tuple-element.78.w_ref, ...), custom_call_target="tpu_custom_call", output_to_operand_aliasing={{0}: (6, {})} | custom-call | flops 3221225472 | bytes 10485760 | tf_op jit(solution)/shard_map/chunk/pallas_call | solution.py:203
  57.2 2.4 %collective-permute-done.11.refs_0_ = bf16[4,128,512]{2,1,0:T(8,128)(2,1)S(1)} collective-permute-done((bf16[4,128,512]{2,1,0:T(8,128)(2,1)S(1)}, bf16[4,128,512]{2,1,0:T(8,128)(2,1)S(1)}, u32[]{:S(2)}, u32[]{:S(2)}) %collective-permute-start.11) | collective-permute-done | bytes 524320 | tf_op jit(solution)/shard_map/ppermute | solution.py:31
  59.6 3.0 %collective-permute-done.12.refs_1_ = bf16[4,128,512]{2,1,0:T(8,128)(2,1)S(1)} collective-permute-done((bf16[4,128,512]{2,1,0:T(8,128)(2,1)S(1)}, bf16[4,128,512]{2,1,0:T(8,128)(2,1)S(1)}, u32[]{:S(2)}, u32[]{:S(2)}) %collective-permute-start.12) | collective-permute-done | bytes 524320 | tf_op jit(solution)/shard_map/ppermute | solution.py:31
  62.6 0.6 collective-permute-start.13
  63.2 1.6 %collective-permute-start.14 = (bf16[2,128,512]{2,1,0:T(8,128)(2,1)S(1)}, bf16[2,128,512]{2,1,0:T(8,128)(2,1)S(1)}, u32[]{:S(2)}, u32[]{:S(2)}) collective-permute-start(bf16[2,128,512]{2,1,0:T(8,128)(2,1)S(1)} %slice.7), channel_id=1, source_target_pairs={{56,0},{0,8},{8,16},{16,24},{24,32},{32,40},{40,48},{48,56},{120,6... | collective-permute-start | bytes 786440 | tf_op jit(solution)/shard_map/ppermute | solution.py:31
  64.8 6.1 %chunk.7 = (f32[2,512,512]{2,1,0:T(8,128)S(1)}, bf16[4,128,256]{2,1,0:T(8,128)(2,1)S(1)}, bf16[4,128,256]{2,1,0:T(8,128)(2,1)S(1)}, bf16[4,128,256]{2,1,0:T(8,128)(2,1)S(1)}, bf16[4,128,256]{2,1,0:T(8,128)(2,1)S(1)}) custom-call(f32[8,32]{1,0:T(8,128)S(1)} %get-tuple-element.78.w_ref, ...), custom_call_target="tpu_custom_call", output_to_operand_aliasing={{0}: (6, {})} | custom-call | flops 3221225472 | bytes 10485760 | tf_op jit(solution)/shard_map/chunk/pallas_call | solution.py:203
  71.0 2.6 %far_cols.1 = (bf16[2,128,512]{2,1,0:T(8,128)(2,1)S(1)}, bf16[2,128,512]{2,1,0:T(8,128)(2,1)S(1)}, bf16[2,512,512]{2,1,0:T(8,128)(2,1)S(1)}) custom-call(f32[8,32]{1,0:T(8,128)S(1)} %get-tuple-element.78.w_ref, bf16[2,512,512]{2,1,0:T(8,128)(2,1)S(1)} %pad_maximum_fusion.r_ref, f32[2,8,512]{2,1,0:T(8,128)S(1)} %row_sums.1, ...), custom_call_target="tpu_custom_call" | custom-call | flops 1073741824 | bytes 4194304 | tf_op jit(solution)/shard_map/far_cols/pallas_call | solution.py:240
  73.6 1.0 collective-permute-start.19
  74.6 2.3 %collective-permute-start.20 = (bf16[2,128,512]{2,1,0:T(8,128)(2,1)S(1)}, bf16[2,128,512]{2,1,0:T(8,128)(2,1)S(1)}, u32[]{:S(2)}, u32[]{:S(2)}) collective-permute-start(bf16[2,128,512]{2,1,0:T(8,128)(2,1)S(1)} %get-tuple-element.101), channel_id=1, source_target_pairs={{8,0},{16,8},{24,16},{32,24},{40,32},{48,40},{56,48},{0,56},{72,64... | collective-permute-start | bytes 786440 | tf_op jit(solution)/shard_map/ppermute | solution.py:31
  76.9 1.3 %far_rows.1 = (f32[4,128,512]{2,1,0:T(8,128)S(1)}, bf16[4,128,512]{2,1,0:T(8,128)(2,1)S(1)}) custom-call(f32[8,32]{1,0:T(8,128)S(1)} %get-tuple-element.78.w_ref, bf16[2,512,512]{2,1,0:T(8,128)(2,1)S(1)} %get-tuple-element.88.coef_ref, bf16[4,128,512]{2,1,0:T(8,128)(2,1)S(1)} %constant_dynamic-update-slice_fusion.k_ref, ...), custom_call_target="tpu_custom_call" | custom-call | flops 536870912 | bytes 8388608 | tf_op jit(solution)/shard_map/far_rows/pallas_call | solution.py:268
  78.4 2.9 %collective-permute-done.19.up_in = bf16[2,128,512]{2,1,0:T(8,128)(2,1)S(1)} collective-permute-done((bf16[2,128,512]{2,1,0:T(8,128)(2,1)S(1)}, bf16[2,128,512]{2,1,0:T(8,128)(2,1)S(1)}, u32[]{:S(2)}, u32[]{:S(2)}) %collective-permute-start.19) | collective-permute-done | bytes 262176 | tf_op jit(solution)/shard_map/ppermute | solution.py:31
  81.3 0.1 first_hop.1
  81.5 3.3 %collective-permute-start.22 = (bf16[4,128,256]{2,1,0:T(8,128)(2,1)S(1)}, bf16[4,128,256]{2,1,0:T(8,128)(2,1)S(1)}, u32[]{:S(2)}, u32[]{:S(2)}) collective-permute-start(bf16[4,128,256]{2,1,0:T(8,128)(2,1)S(1)} %get-tuple-element.107), channel_id=1, source_target_pairs={{8,0},{16,8},{24,16},{32,24},{40,32},{48,40},{56,48},{0,56},{72,64... | collective-permute-start | bytes 786440 | tf_op jit(solution)/shard_map/ppermute | solution.py:31
  84.8 3.2 %collective-permute-start.31 = (bf16[4,128,256]{2,1,0:T(8,128)(2,1)S(1)}, bf16[4,128,256]{2,1,0:T(8,128)(2,1)S(1)}, u32[]{:S(2)}, u32[]{:S(2)}) collective-permute-start(bf16[4,128,256]{2,1,0:T(8,128)(2,1)S(1)} %get-tuple-element.122), channel_id=1, source_target_pairs={{8,0},{16,8},{24,16},{32,24},{40,32},{48,40},{56,48},{0,56},{72,64... | collective-permute-start | bytes 786440 | tf_op jit(solution)/shard_map/ppermute | solution.py:31
  88.1 3.9 %collective-permute-done.21.up_in = bf16[4,128,256]{2,1,0:T(8,128)(2,1)S(1)} collective-permute-done((bf16[4,128,256]{2,1,0:T(8,128)(2,1)S(1)}, bf16[4,128,256]{2,1,0:T(8,128)(2,1)S(1)}, u32[]{:S(2)}, u32[]{:S(2)}) %collective-permute-start.21) | collective-permute-done | bytes 262176 | tf_op jit(solution)/shard_map/ppermute | solution.py:31
  92.0 0.1 hop.4
  92.2 3.6 %collective-permute-start.24 = (bf16[4,128,256]{2,1,0:T(8,128)(2,1)S(1)}, bf16[4,128,256]{2,1,0:T(8,128)(2,1)S(1)}, u32[]{:S(2)}, u32[]{:S(2)}) collective-permute-start(bf16[4,128,256]{2,1,0:T(8,128)(2,1)S(1)} %get-tuple-element.109), channel_id=1, source_target_pairs={{8,0},{16,8},{24,16},{32,24},{40,32},{48,40},{56,48},{0,56},{72,64... | collective-permute-start | bytes 786440 | tf_op jit(solution)/shard_map/ppermute | solution.py:31
  95.9 1.7 %collective-permute-done.30.up_in = bf16[4,128,256]{2,1,0:T(8,128)(2,1)S(1)} collective-permute-done((bf16[4,128,256]{2,1,0:T(8,128)(2,1)S(1)}, bf16[4,128,256]{2,1,0:T(8,128)(2,1)S(1)}, u32[]{:S(2)}, u32[]{:S(2)}) %collective-permute-start.30) | collective-permute-done | bytes 262176 | tf_op jit(solution)/shard_map/ppermute | solution.py:31
  97.6 0.1 hop.6
  97.8 3.4 %collective-permute-start.33 = (bf16[4,128,256]{2,1,0:T(8,128)(2,1)S(1)}, bf16[4,128,256]{2,1,0:T(8,128)(2,1)S(1)}, u32[]{:S(2)}, u32[]{:S(2)}) collective-permute-start(bf16[4,128,256]{2,1,0:T(8,128)(2,1)S(1)} %get-tuple-element.126), channel_id=1, source_target_pairs={{8,0},{16,8},{24,16},{32,24},{40,32},{48,40},{56,48},{0,56},{72,64... | collective-permute-start | bytes 786440 | tf_op jit(solution)/shard_map/ppermute | solution.py:31
  101.2 1.4 %collective-permute-done.23.up_in = bf16[4,128,256]{2,1,0:T(8,128)(2,1)S(1)} collective-permute-done((bf16[4,128,256]{2,1,0:T(8,128)(2,1)S(1)}, bf16[4,128,256]{2,1,0:T(8,128)(2,1)S(1)}, u32[]{:S(2)}, u32[]{:S(2)}) %collective-permute-start.23) | collective-permute-done | bytes 262176 | tf_op jit(solution)/shard_map/ppermute | solution.py:31
  102.6 3.0 %collective-permute-start.17 = (bf16[128,512]{1,0:T(8,128)(2,1)S(1)}, bf16[128,512]{1,0:T(8,128)(2,1)S(1)}, u32[]{:S(2)}, u32[]{:S(2)}) collective-permute-start(bf16[128,512]{1,0:T(8,128)(2,1)S(1)} %get-tuple-element.93), channel_id=1, source_target_pairs={{4,0},{5,1},{6,2},{7,3},{0,4},{1,5},{2,6},{3,7},{12,8},{13,9},{14,... | collective-permute-start | bytes 393224 | tf_op jit(solution)/shard_map/ppermute | solution.py:36
  105.6 1.3 collective-permute-start.18
  106.9 0.1 hop.5
  107.0 0.4 collective-permute-done.16.refs_1_
  107.4 2.5 %collective-permute-done.17.refs_2_ = bf16[128,512]{1,0:T(8,128)(2,1)S(1)} collective-permute-done((bf16[128,512]{1,0:T(8,128)(2,1)S(1)}, bf16[128,512]{1,0:T(8,128)(2,1)S(1)}, u32[]{:S(2)}, u32[]{:S(2)}) %collective-permute-start.17) | collective-permute-done | bytes 131104 | tf_op jit(solution)/shard_map/ppermute | solution.py:36
  109.9 1.4 %collective-permute-start.26 = (bf16[4,128,256]{2,1,0:T(8,128)(2,1)S(1)}, bf16[4,128,256]{2,1,0:T(8,128)(2,1)S(1)}, u32[]{:S(2)}, u32[]{:S(2)}) collective-permute-start(bf16[4,128,256]{2,1,0:T(8,128)(2,1)S(1)} %get-tuple-element.111), channel_id=1, source_target_pairs={{8,0},{16,8},{24,16},{32,24},{40,32},{48,40},{56,48},{0,56},{72,64... | collective-permute-start | bytes 786440 | tf_op jit(solution)/shard_map/ppermute | solution.py:31
  111.3 0.1 hop.7
  111.5 0.7 collective-permute-start.34
  112.1 2.7 %collective-permute-start.35 = (bf16[4,128,256]{2,1,0:T(8,128)(2,1)S(1)}, bf16[4,128,256]{2,1,0:T(8,128)(2,1)S(1)}, u32[]{:S(2)}, u32[]{:S(2)}) collective-permute-start(bf16[4,128,256]{2,1,0:T(8,128)(2,1)S(1)} %get-tuple-element.130), channel_id=1, source_target_pairs={{8,0},{16,8},{24,16},{32,24},{40,32},{48,40},{56,48},{0,56},{72,64... | collective-permute-start | bytes 786440 | tf_op jit(solution)/shard_map/ppermute | solution.py:31
  114.8 0.2 collective-permute-done.25.up_in
  115.0 1.3 collective-permute-done.26.down_in
  116.4 2.2 %collective-permute-start.28 = (bf16[128,256]{1,0:T(8,128)(2,1)S(1)}, bf16[128,256]{1,0:T(8,128)(2,1)S(1)}, u32[]{:S(2)}, u32[]{:S(2)}) collective-permute-start(bf16[128,256]{1,0:T(8,128)(2,1)S(1)} %get-tuple-element.114), channel_id=1, source_target_pairs={{192,0},{200,8},{208,16},{216,24},{224,32},{232,40},{240,48},{248,... | collective-permute-start | bytes 196616 | tf_op jit(solution)/shard_map/ppermute | solution.py:26
  118.7 0.5 collective-permute-done.34.up_in
  119.2 3.0 %collective-permute-start.36 = (bf16[128,256]{1,0:T(8,128)(2,1)S(1)}, bf16[128,256]{1,0:T(8,128)(2,1)S(1)}, u32[]{:S(2)}, u32[]{:S(2)}) collective-permute-start(bf16[128,256]{1,0:T(8,128)(2,1)S(1)} %get-tuple-element.132), channel_id=1, source_target_pairs={{128,0},{136,8},{144,16},{152,24},{160,32},{168,40},{176,48},{184,... | collective-permute-start | bytes 196616 | tf_op jit(solution)/shard_map/ppermute | solution.py:26
  122.2 1.0 collective-permute-start.37
  123.2 1.0 collective-permute-start.38
  124.2 0.9 collective-permute-done.36.refs_9_
  125.1 1.4 %collective-permute-done.37.refs_10_ = bf16[128,256]{1,0:T(8,128)(2,1)S(1)} collective-permute-done((bf16[128,256]{1,0:T(8,128)(2,1)S(1)}, bf16[128,256]{1,0:T(8,128)(2,1)S(1)}, u32[]{:S(2)}, u32[]{:S(2)}) %collective-permute-start.37) | collective-permute-done | bytes 65568 | tf_op jit(solution)/shard_map/ppermute | solution.py:26
  126.5 2.2 %collective-permute-done.38.refs_11_ = bf16[128,256]{1,0:T(8,128)(2,1)S(1)} collective-permute-done((bf16[128,256]{1,0:T(8,128)(2,1)S(1)}, bf16[128,256]{1,0:T(8,128)(2,1)S(1)}, u32[]{:S(2)}, u32[]{:S(2)}) %collective-permute-start.38) | collective-permute-done | bytes 65568 | tf_op jit(solution)/shard_map/ppermute | solution.py:26
  128.7 0.8 final.1
  (42 shorter events, 1.0 us)
Async XLA Ops:
  0.0 22.5 %copy-start = (f32[1,32]{1,0:T(1,128)S(1)}, f32[1,32]{1,0:T(1,128)}, u32[]{:S(2)}) copy-start(f32[1,32]{1,0:T(1,128)} %nw.1) | copy-start | bytes 388
  1.0 9.2 %collective-permute-start = (bf16[128,512]{1,0:T(8,128)(2,1)S(1)}, bf16[128,512]{1,0:T(8,128)(2,1)S(1)}, u32[]{:S(2)}, u32[]{:S(2)}) collective-permute-start(bf16[128,512]{1,0:T(8,128)(2,1)S(1)} %convert_element_type.3), channel_id=1, source_target_pairs={{64,0},{72,8},{80,16},{88,24},{96,32},{104,40},{112,48},{120,56},{... | collective-permute-start | bytes 393224 | tf_op jit(solution)/shard_map/ppermute | solution.py:26
  1.8 9.4 %collective-permute-start.2 = (bf16[128,512]{1,0:T(8,128)(2,1)S(1)}, bf16[128,512]{1,0:T(8,128)(2,1)S(1)}, u32[]{:S(2)}, u32[]{:S(2)}) collective-permute-start(bf16[128,512]{1,0:T(8,128)(2,1)S(1)} %convert_element_type.3), channel_id=1, source_target_pairs={{192,0},{200,8},{208,16},{216,24},{224,32},{232,40},{240,48},{248,... | collective-permute-start | bytes 393224 | tf_op jit(solution)/shard_map/ppermute | solution.py:26
  4.3 7.8 %collective-permute-start.3 = (bf16[128,512]{1,0:T(8,128)(2,1)S(1)}, bf16[128,512]{1,0:T(8,128)(2,1)S(1)}, u32[]{:S(2)}, u32[]{:S(2)}) collective-permute-start(bf16[128,512]{1,0:T(8,128)(2,1)S(1)} %convert_element_type.3), channel_id=1, source_target_pairs={{2,0},{3,1},{4,2},{5,3},{6,4},{7,5},{0,6},{1,7},{10,8},{11,9},{12,... | collective-permute-start | bytes 393224 | tf_op jit(solution)/shard_map/ppermute | solution.py:36
  7.1 7.4 %collective-permute-start.4 = (bf16[128,512]{1,0:T(8,128)(2,1)S(1)}, bf16[128,512]{1,0:T(8,128)(2,1)S(1)}, u32[]{:S(2)}, u32[]{:S(2)}) collective-permute-start(bf16[128,512]{1,0:T(8,128)(2,1)S(1)} %convert_element_type.3), channel_id=1, source_target_pairs={{4,0},{5,1},{6,2},{7,3},{0,4},{1,5},{2,6},{3,7},{12,8},{13,9},{14,... | collective-permute-start | bytes 393224 | tf_op jit(solution)/shard_map/ppermute | solution.py:36
  7.9 7.9 %collective-permute-start.5 = (bf16[128,512]{1,0:T(8,128)(2,1)S(1)}, bf16[128,512]{1,0:T(8,128)(2,1)S(1)}, u32[]{:S(2)}, u32[]{:S(2)}) collective-permute-start(bf16[128,512]{1,0:T(8,128)(2,1)S(1)} %convert_element_type.3), channel_id=1, source_target_pairs={{6,0},{7,1},{0,2},{1,3},{2,4},{3,5},{4,6},{5,7},{14,8},{15,9},{8,1... | collective-permute-start | bytes 393224 | tf_op jit(solution)/shard_map/ppermute | solution.py:36
  10.2 6.2 %collective-permute-start.1 = (bf16[128,512]{1,0:T(8,128)(2,1)S(1)}, bf16[128,512]{1,0:T(8,128)(2,1)S(1)}, u32[]{:S(2)}, u32[]{:S(2)}) collective-permute-start(bf16[128,512]{1,0:T(8,128)(2,1)S(1)} %collective-permute-done), channel_id=1, source_target_pairs={{64,0},{72,8},{80,16},{88,24},{96,32},{104,40},{112,48},{120,56},{... | collective-permute-start | bytes 393224 | tf_op jit(solution)/shard_map/ppermute | solution.py:26
  16.6 15.8 %collective-permute-start.7 = (bf16[4,128,512]{2,1,0:T(8,128)(2,1)S(1)}, bf16[4,128,512]{2,1,0:T(8,128)(2,1)S(1)}, u32[]{:S(2)}, u32[]{:S(2)}) collective-permute-start(bf16[4,128,512]{2,1,0:T(8,128)(2,1)S(1)} %get-tuple-element.75.refs_0_), channel_id=1, source_target_pairs={{8,0},{16,8},{24,16},{32,24},{40,32},{48,40},{56,48},{0,56},{72,64... | collective-permute-start | bytes 1572872 | tf_op jit(solution)/shard_map/ppermute | solution.py:31
  22.5 13.3 %collective-permute-start.8 = (bf16[4,128,512]{2,1,0:T(8,128)(2,1)S(1)}, bf16[4,128,512]{2,1,0:T(8,128)(2,1)S(1)}, u32[]{:S(2)}, u32[]{:S(2)}) collective-permute-start(bf16[4,128,512]{2,1,0:T(8,128)(2,1)S(1)} %get-tuple-element.75.refs_0_), channel_id=1, source_target_pairs={{56,0},{0,8},{8,16},{16,24},{24,32},{32,40},{40,48},{48,56},{120,6... | collective-permute-start | bytes 1572872 | tf_op jit(solution)/shard_map/ppermute | solution.py:31
  28.7 10.3 %collective-permute-start.6 = (bf16[4,128,512]{2,1,0:T(8,128)(2,1)S(1)}, bf16[4,128,512]{2,1,0:T(8,128)(2,1)S(1)}, u32[]{:S(2)}, u32[]{:S(2)}) collective-permute-start(bf16[4,128,512]{2,1,0:T(8,128)(2,1)S(1)} %get-tuple-element.73), channel_id=1, source_target_pairs={{1,0},{0,1},{3,2},{2,3},{5,4},{4,5},{7,6},{6,7},{9,8},{8,9},{11,10... | collective-permute-start | bytes 1572872 | tf_op jit(solution)/shard_map/ppermute | solution.py:41
  35.8 13.1 %collective-permute-start.10 = (bf16[4,128,512]{2,1,0:T(8,128)(2,1)S(1)}, bf16[4,128,512]{2,1,0:T(8,128)(2,1)S(1)}, u32[]{:S(2)}, u32[]{:S(2)}) collective-permute-start(bf16[4,128,512]{2,1,0:T(8,128)(2,1)S(1)} %collective-permute-done.8.refs_1_), channel_id=1, source_target_pairs={{56,0},{0,8},{8,16},{16,24},{24,32},{32,40},{40,48},{48,56},{120,6... | collective-permute-start | bytes 1572872 | tf_op jit(solution)/shard_map/ppermute | solution.py:31
  35.8 13.1 %collective-permute-start.9 = (bf16[4,128,512]{2,1,0:T(8,128)(2,1)S(1)}, bf16[4,128,512]{2,1,0:T(8,128)(2,1)S(1)}, u32[]{:S(2)}, u32[]{:S(2)}) collective-permute-start(bf16[4,128,512]{2,1,0:T(8,128)(2,1)S(1)} %collective-permute-done.7.refs_0_), channel_id=1, source_target_pairs={{8,0},{16,8},{24,16},{32,24},{40,32},{48,40},{56,48},{0,56},{72,64... | collective-permute-start | bytes 1572872 | tf_op jit(solution)/shard_map/ppermute | solution.py:31
  48.9 10.7 %collective-permute-start.11 = (bf16[4,128,512]{2,1,0:T(8,128)(2,1)S(1)}, bf16[4,128,512]{2,1,0:T(8,128)(2,1)S(1)}, u32[]{:S(2)}, u32[]{:S(2)}) collective-permute-start(bf16[4,128,512]{2,1,0:T(8,128)(2,1)S(1)} %collective-permute-done.9.refs_0_), channel_id=1, source_target_pairs={{8,0},{16,8},{24,16},{32,24},{40,32},{48,40},{56,48},{0,56},{72,64... | collective-permute-start | bytes 1572872 | tf_op jit(solution)/shard_map/ppermute | solution.py:31
  51.1 11.5 %collective-permute-start.12 = (bf16[4,128,512]{2,1,0:T(8,128)(2,1)S(1)}, bf16[4,128,512]{2,1,0:T(8,128)(2,1)S(1)}, u32[]{:S(2)}, u32[]{:S(2)}) collective-permute-start(bf16[4,128,512]{2,1,0:T(8,128)(2,1)S(1)} %collective-permute-done.10.refs_1_), channel_id=1, source_target_pairs={{56,0},{0,8},{8,16},{16,24},{24,32},{32,40},{40,48},{48,56},{120,6... | collective-permute-start | bytes 1572872 | tf_op jit(solution)/shard_map/ppermute | solution.py:31
  62.6 8.3 %collective-permute-start.13 = (bf16[2,128,512]{2,1,0:T(8,128)(2,1)S(1)}, bf16[2,128,512]{2,1,0:T(8,128)(2,1)S(1)}, u32[]{:S(2)}, u32[]{:S(2)}) collective-permute-start(bf16[2,128,512]{2,1,0:T(8,128)(2,1)S(1)} %slice.6), channel_id=1, source_target_pairs={{8,0},{16,8},{24,16},{32,24},{40,32},{48,40},{56,48},{0,56},{72,64... | collective-permute-start | bytes 786440 | tf_op jit(solution)/shard_map/ppermute | solution.py:31
  63.2 7.8 %collective-permute-start.14 = (bf16[2,128,512]{2,1,0:T(8,128)(2,1)S(1)}, bf16[2,128,512]{2,1,0:T(8,128)(2,1)S(1)}, u32[]{:S(2)}, u32[]{:S(2)}) collective-permute-start(bf16[2,128,512]{2,1,0:T(8,128)(2,1)S(1)} %slice.7), channel_id=1, source_target_pairs={{56,0},{0,8},{8,16},{16,24},{24,32},{32,40},{40,48},{48,56},{120,6... | collective-permute-start | bytes 786440 | tf_op jit(solution)/shard_map/ppermute | solution.py:31
  73.6 7.7 %collective-permute-start.19 = (bf16[2,128,512]{2,1,0:T(8,128)(2,1)S(1)}, bf16[2,128,512]{2,1,0:T(8,128)(2,1)S(1)}, u32[]{:S(2)}, u32[]{:S(2)}) collective-permute-start(bf16[2,128,512]{2,1,0:T(8,128)(2,1)S(1)} %get-tuple-element.100), channel_id=1, source_target_pairs={{56,0},{0,8},{8,16},{16,24},{24,32},{32,40},{40,48},{48,56},{120,6... | collective-permute-start | bytes 786440 | tf_op jit(solution)/shard_map/ppermute | solution.py:31
  74.6 6.7 %collective-permute-start.20 = (bf16[2,128,512]{2,1,0:T(8,128)(2,1)S(1)}, bf16[2,128,512]{2,1,0:T(8,128)(2,1)S(1)}, u32[]{:S(2)}, u32[]{:S(2)}) collective-permute-start(bf16[2,128,512]{2,1,0:T(8,128)(2,1)S(1)} %get-tuple-element.101), channel_id=1, source_target_pairs={{8,0},{16,8},{24,16},{32,24},{40,32},{48,40},{56,48},{0,56},{72,64... | collective-permute-start | bytes 786440 | tf_op jit(solution)/shard_map/ppermute | solution.py:31
  78.3 17.5 %collective-permute-start.15 = (bf16[4,128,512]{2,1,0:T(8,128)(2,1)S(1)}, bf16[4,128,512]{2,1,0:T(8,128)(2,1)S(1)}, u32[]{:S(2)}, u32[]{:S(2)}) collective-permute-start(bf16[4,128,512]{2,1,0:T(8,128)(2,1)S(1)} %get-tuple-element.90), channel_id=1, source_target_pairs={{1,0},{0,1},{3,2},{2,3},{5,4},{4,5},{7,6},{6,7},{9,8},{8,9},{11,10... | collective-permute-start | bytes 1572872 | tf_op jit(solution)/shard_map/ppermute | solution.py:41
  81.4 10.5 %collective-permute-start.21 = (bf16[4,128,256]{2,1,0:T(8,128)(2,1)S(1)}, bf16[4,128,256]{2,1,0:T(8,128)(2,1)S(1)}, u32[]{:S(2)}, u32[]{:S(2)}) collective-permute-start(bf16[4,128,256]{2,1,0:T(8,128)(2,1)S(1)} %get-tuple-element.106), channel_id=1, source_target_pairs={{56,0},{0,8},{8,16},{16,24},{24,32},{32,40},{40,48},{48,56},{120,6... | collective-permute-start | bytes 786440 | tf_op jit(solution)/shard_map/ppermute | solution.py:31
  81.5 10.4 %collective-permute-start.22 = (bf16[4,128,256]{2,1,0:T(8,128)(2,1)S(1)}, bf16[4,128,256]{2,1,0:T(8,128)(2,1)S(1)}, u32[]{:S(2)}, u32[]{:S(2)}) collective-permute-start(bf16[4,128,256]{2,1,0:T(8,128)(2,1)S(1)} %get-tuple-element.107), channel_id=1, source_target_pairs={{8,0},{16,8},{24,16},{32,24},{40,32},{48,40},{56,48},{0,56},{72,64... | collective-permute-start | bytes 786440 | tf_op jit(solution)/shard_map/ppermute | solution.py:31
  84.8 12.8 %collective-permute-start.30 = (bf16[4,128,256]{2,1,0:T(8,128)(2,1)S(1)}, bf16[4,128,256]{2,1,0:T(8,128)(2,1)S(1)}, u32[]{:S(2)}, u32[]{:S(2)}) collective-permute-start(bf16[4,128,256]{2,1,0:T(8,128)(2,1)S(1)} %get-tuple-element.121), channel_id=1, source_target_pairs={{56,0},{0,8},{8,16},{16,24},{24,32},{32,40},{40,48},{48,56},{120,6... | collective-permute-start | bytes 786440 | tf_op jit(solution)/shard_map/ppermute | solution.py:31
  84.8 12.8 %collective-permute-start.31 = (bf16[4,128,256]{2,1,0:T(8,128)(2,1)S(1)}, bf16[4,128,256]{2,1,0:T(8,128)(2,1)S(1)}, u32[]{:S(2)}, u32[]{:S(2)}) collective-permute-start(bf16[4,128,256]{2,1,0:T(8,128)(2,1)S(1)} %get-tuple-element.122), channel_id=1, source_target_pairs={{8,0},{16,8},{24,16},{32,24},{40,32},{48,40},{56,48},{0,56},{72,64... | collective-permute-start | bytes 786440 | tf_op jit(solution)/shard_map/ppermute | solution.py:31
  92.1 10.5 %collective-permute-start.23 = (bf16[4,128,256]{2,1,0:T(8,128)(2,1)S(1)}, bf16[4,128,256]{2,1,0:T(8,128)(2,1)S(1)}, u32[]{:S(2)}, u32[]{:S(2)}) collective-permute-start(bf16[4,128,256]{2,1,0:T(8,128)(2,1)S(1)} %get-tuple-element.108), channel_id=1, source_target_pairs={{56,0},{0,8},{8,16},{16,24},{24,32},{32,40},{40,48},{48,56},{120,6... | collective-permute-start | bytes 786440 | tf_op jit(solution)/shard_map/ppermute | solution.py:31
  92.2 13.4 %collective-permute-start.24 = (bf16[4,128,256]{2,1,0:T(8,128)(2,1)S(1)}, bf16[4,128,256]{2,1,0:T(8,128)(2,1)S(1)}, u32[]{:S(2)}, u32[]{:S(2)}) collective-permute-start(bf16[4,128,256]{2,1,0:T(8,128)(2,1)S(1)} %get-tuple-element.109), channel_id=1, source_target_pairs={{8,0},{16,8},{24,16},{32,24},{40,32},{48,40},{56,48},{0,56},{72,64... | collective-permute-start | bytes 786440 | tf_op jit(solution)/shard_map/ppermute | solution.py:31
  97.7 13.6 %collective-permute-start.32 = (bf16[4,128,256]{2,1,0:T(8,128)(2,1)S(1)}, bf16[4,128,256]{2,1,0:T(8,128)(2,1)S(1)}, u32[]{:S(2)}, u32[]{:S(2)}) collective-permute-start(bf16[4,128,256]{2,1,0:T(8,128)(2,1)S(1)} %get-tuple-element.125), channel_id=1, source_target_pairs={{56,0},{0,8},{8,16},{16,24},{24,32},{32,40},{40,48},{48,56},{120,6... | collective-permute-start | bytes 786440 | tf_op jit(solution)/shard_map/ppermute | solution.py:31
  97.8 13.5 %collective-permute-start.33 = (bf16[4,128,256]{2,1,0:T(8,128)(2,1)S(1)}, bf16[4,128,256]{2,1,0:T(8,128)(2,1)S(1)}, u32[]{:S(2)}, u32[]{:S(2)}) collective-permute-start(bf16[4,128,256]{2,1,0:T(8,128)(2,1)S(1)} %get-tuple-element.126), channel_id=1, source_target_pairs={{8,0},{16,8},{24,16},{32,24},{40,32},{48,40},{56,48},{0,56},{72,64... | collective-permute-start | bytes 786440 | tf_op jit(solution)/shard_map/ppermute | solution.py:31
  101.2 6.2 %collective-permute-start.16 = (bf16[128,512]{1,0:T(8,128)(2,1)S(1)}, bf16[128,512]{1,0:T(8,128)(2,1)S(1)}, u32[]{:S(2)}, u32[]{:S(2)}) collective-permute-start(bf16[128,512]{1,0:T(8,128)(2,1)S(1)} %get-tuple-element.92), channel_id=1, source_target_pairs={{6,0},{7,1},{0,2},{1,3},{2,4},{3,5},{4,6},{5,7},{14,8},{15,9},{8,1... | collective-permute-start | bytes 393224 | tf_op jit(solution)/shard_map/ppermute | solution.py:36
  102.6 7.3 %collective-permute-start.17 = (bf16[128,512]{1,0:T(8,128)(2,1)S(1)}, bf16[128,512]{1,0:T(8,128)(2,1)S(1)}, u32[]{:S(2)}, u32[]{:S(2)}) collective-permute-start(bf16[128,512]{1,0:T(8,128)(2,1)S(1)} %get-tuple-element.93), channel_id=1, source_target_pairs={{4,0},{5,1},{6,2},{7,3},{0,4},{1,5},{2,6},{3,7},{12,8},{13,9},{14,... | collective-permute-start | bytes 393224 | tf_op jit(solution)/shard_map/ppermute | solution.py:36
  105.6 5.7 %collective-permute-start.18 = (bf16[128,512]{1,0:T(8,128)(2,1)S(1)}, bf16[128,512]{1,0:T(8,128)(2,1)S(1)}, u32[]{:S(2)}, u32[]{:S(2)}) collective-permute-start(bf16[128,512]{1,0:T(8,128)(2,1)S(1)} %get-tuple-element.94), channel_id=1, source_target_pairs={{2,0},{3,1},{4,2},{5,3},{6,4},{7,5},{0,6},{1,7},{10,8},{11,9},{12,... | collective-permute-start | bytes 393224 | tf_op jit(solution)/shard_map/ppermute | solution.py:36
  107.4 7.6 %collective-permute-start.25 = (bf16[4,128,256]{2,1,0:T(8,128)(2,1)S(1)}, bf16[4,128,256]{2,1,0:T(8,128)(2,1)S(1)}, u32[]{:S(2)}, u32[]{:S(2)}) collective-permute-start(bf16[4,128,256]{2,1,0:T(8,128)(2,1)S(1)} %get-tuple-element.110), channel_id=1, source_target_pairs={{56,0},{0,8},{8,16},{16,24},{24,32},{32,40},{40,48},{48,56},{120,6... | collective-permute-start | bytes 786440 | tf_op jit(solution)/shard_map/ppermute | solution.py:31
  109.9 6.4 %collective-permute-start.26 = (bf16[4,128,256]{2,1,0:T(8,128)(2,1)S(1)}, bf16[4,128,256]{2,1,0:T(8,128)(2,1)S(1)}, u32[]{:S(2)}, u32[]{:S(2)}) collective-permute-start(bf16[4,128,256]{2,1,0:T(8,128)(2,1)S(1)} %get-tuple-element.111), channel_id=1, source_target_pairs={{8,0},{16,8},{24,16},{32,24},{40,32},{48,40},{56,48},{0,56},{72,64... | collective-permute-start | bytes 786440 | tf_op jit(solution)/shard_map/ppermute | solution.py:31
  111.5 7.7 %collective-permute-start.34 = (bf16[4,128,256]{2,1,0:T(8,128)(2,1)S(1)}, bf16[4,128,256]{2,1,0:T(8,128)(2,1)S(1)}, u32[]{:S(2)}, u32[]{:S(2)}) collective-permute-start(bf16[4,128,256]{2,1,0:T(8,128)(2,1)S(1)} %get-tuple-element.129), channel_id=1, source_target_pairs={{56,0},{0,8},{8,16},{16,24},{24,32},{32,40},{40,48},{48,56},{120,6... | collective-permute-start | bytes 786440 | tf_op jit(solution)/shard_map/ppermute | solution.py:31
  112.1 7.0 %collective-permute-start.35 = (bf16[4,128,256]{2,1,0:T(8,128)(2,1)S(1)}, bf16[4,128,256]{2,1,0:T(8,128)(2,1)S(1)}, u32[]{:S(2)}, u32[]{:S(2)}) collective-permute-start(bf16[4,128,256]{2,1,0:T(8,128)(2,1)S(1)} %get-tuple-element.130), channel_id=1, source_target_pairs={{8,0},{16,8},{24,16},{32,24},{40,32},{48,40},{56,48},{0,56},{72,64... | collective-permute-start | bytes 786440 | tf_op jit(solution)/shard_map/ppermute | solution.py:31
  116.3 6.8 %collective-permute-start.27 = (bf16[128,256]{1,0:T(8,128)(2,1)S(1)}, bf16[128,256]{1,0:T(8,128)(2,1)S(1)}, u32[]{:S(2)}, u32[]{:S(2)}) collective-permute-start(bf16[128,256]{1,0:T(8,128)(2,1)S(1)} %get-tuple-element.113), channel_id=1, source_target_pairs={{128,0},{136,8},{144,16},{152,24},{160,32},{168,40},{176,48},{184,... | collective-permute-start | bytes 196616 | tf_op jit(solution)/shard_map/ppermute | solution.py:26
  116.4 7.8 %collective-permute-start.28 = (bf16[128,256]{1,0:T(8,128)(2,1)S(1)}, bf16[128,256]{1,0:T(8,128)(2,1)S(1)}, u32[]{:S(2)}, u32[]{:S(2)}) collective-permute-start(bf16[128,256]{1,0:T(8,128)(2,1)S(1)} %get-tuple-element.114), channel_id=1, source_target_pairs={{192,0},{200,8},{208,16},{216,24},{224,32},{232,40},{240,48},{248,... | collective-permute-start | bytes 196616 | tf_op jit(solution)/shard_map/ppermute | solution.py:26
  118.7 5.6 %collective-permute-start.29 = (bf16[128,256]{1,0:T(8,128)(2,1)S(1)}, bf16[128,256]{1,0:T(8,128)(2,1)S(1)}, u32[]{:S(2)}, u32[]{:S(2)}) collective-permute-start(bf16[128,256]{1,0:T(8,128)(2,1)S(1)} %get-tuple-element.115), channel_id=1, source_target_pairs={{64,0},{72,8},{80,16},{88,24},{96,32},{104,40},{112,48},{120,56},{... | collective-permute-start | bytes 196616 | tf_op jit(solution)/shard_map/ppermute | solution.py:26
  119.2 5.9 %collective-permute-start.36 = (bf16[128,256]{1,0:T(8,128)(2,1)S(1)}, bf16[128,256]{1,0:T(8,128)(2,1)S(1)}, u32[]{:S(2)}, u32[]{:S(2)}) collective-permute-start(bf16[128,256]{1,0:T(8,128)(2,1)S(1)} %get-tuple-element.132), channel_id=1, source_target_pairs={{128,0},{136,8},{144,16},{152,24},{160,32},{168,40},{176,48},{184,... | collective-permute-start | bytes 196616 | tf_op jit(solution)/shard_map/ppermute | solution.py:26
  122.2 4.3 %collective-permute-start.37 = (bf16[128,256]{1,0:T(8,128)(2,1)S(1)}, bf16[128,256]{1,0:T(8,128)(2,1)S(1)}, u32[]{:S(2)}, u32[]{:S(2)}) collective-permute-start(bf16[128,256]{1,0:T(8,128)(2,1)S(1)} %get-tuple-element.133), channel_id=1, source_target_pairs={{192,0},{200,8},{208,16},{216,24},{224,32},{232,40},{240,48},{248,... | collective-permute-start | bytes 196616 | tf_op jit(solution)/shard_map/ppermute | solution.py:26
  123.2 5.5 %collective-permute-start.38 = (bf16[128,256]{1,0:T(8,128)(2,1)S(1)}, bf16[128,256]{1,0:T(8,128)(2,1)S(1)}, u32[]{:S(2)}, u32[]{:S(2)}) collective-permute-start(bf16[128,256]{1,0:T(8,128)(2,1)S(1)} %get-tuple-element.134), channel_id=1, source_target_pairs={{64,0},{72,8},{80,16},{88,24},{96,32},{104,40},{112,48},{120,56},{... | collective-permute-start | bytes 196616 | tf_op jit(solution)/shard_map/ppermute | solution.py:26
